TPU v7x, 32 devices: a whole 2x2x4 slice. The times are simulated.
32 devices in a mesh: dp: 4 (over y, core), tensor: 8 (over z, x).
Axes of the slice: x: 2, y: 2, z: 4, core: 2. Of those that a mesh axis runs over, the one named last changes fastest.
Arguments:
- tokens: bfloat16 [12288, 2048], P(('dp', 'tensor')), may hold values from -6 to 6
- cotangent: bfloat16 [12288, 2048], P(('dp', 'tensor')), may hold values from -6 to 6
- w_qkv: bfloat16 [2048, 3, 2048], P(None, None, 'tensor'), may hold values from -0.1875 to 0.1875
- b_qkv: float32 [3, 2048], P(None, 'tensor'), may hold values from -3 to 3
- w_out: bfloat16 [2048, 2048], P('tensor'), may hold values from -3 to 3
- b_out: float32 [2048], replicated, may hold values from -4 to 4
- gain_one: float32 [2048], replicated, may hold values from 0.25 to 1.75
- shift_one: float32 [2048], replicated, may hold values from -3 to 3
- w_gu: bfloat16 [2048, 2, 5472], P(None, None, 'tensor'), may hold values from -0.125 to 0.125
- b_gu: float32 [2, 5472], P(None, 'tensor'), may hold values from -3 to 3
- w_down: bfloat16 [5472, 2048], P('tensor'), may hold values from -0.625 to 0.625
- b_down: float32 [2048], replicated, may hold values from -4 to 4
- gain_two: float32 [2048], replicated, may hold values from 0.25 to 1.75
- shift_two: float32 [2048], replicated, may hold values from -3 to 3
- prefix: int32 [12], P('dp'), may hold values from 256 to 768
- span_offset: int32 [12], P('dp'), may hold values from 0 to 255
- cluster: int32 [8], replicated, may hold values from 0 to 3, as said below
Outputs:
- layer_out: float32 [12288, 2048], P(('dp', 'tensor'))
- input_grad: float32 [12288, 2048], P(('dp', 'tensor'))
- grad_w_qkv: float32 [2048, 3, 2048], P(None, None, 'tensor')
- grad_b_qkv: float32 [3, 2048], P(None, 'tensor')
- grad_w_out: float32 [2048, 2048], P('tensor')
- grad_b_out: float32 [2048], replicated
- grad_gain_one: float32 [2048], replicated
- grad_shift_one: float32 [2048], replicated
- grad_w_gu: float32 [2048, 2, 5472], P(None, None, 'tensor')
- grad_b_gu: float32 [2, 5472], P(None, 'tensor')
- grad_w_down: float32 [5472, 2048], P('tensor')
- grad_b_down: float32 [2048], replicated
- grad_gain_two: float32 [2048], replicated
- grad_shift_two: float32 [2048], replicated
Inputs may be any that keep to these rules, and one draw needn't show every extreme that they name: Item i stands on index cluster[i] of dp, in slots filled from the lowest; no index holds more than 3 items, and some index holds exactly 3.
All inputs are finite; a program needn't handle non-finite values.
Results may differ from a plain program's by a relative error of at most 0.025.
The roundings to bfloat16 on the way count: a program that leaves them out, or rounds other values in their place, can miss the bound.
Values may be sent and summed in bfloat16 or wider, within the bound.
A program may use at most 256 MiB of HBM per device.

v0:
```python
import math

import jax
import jax.numpy as jnp
from jax import lax
from jax.sharding import PartitionSpec as P

HD = 128
FF = 5461
LEN = 1024


deep_alpha = math.sqrt(48.0)
epsilon = 1e-05
negative = -1e30
theta_base = 10000.0


def rotary_tables(prefix_len, span_start):
    position = jnp.arange(LEN)
    placed = jnp.where(position < prefix_len, position, span_start + position - prefix_len).astype(
        jnp.float32
    )
    frequency = theta_base ** (-(jnp.arange(HD // 2).astype(jnp.float32) * 2.0 / HD))
    angles = placed[:, None] * frequency[None, :]
    return (jnp.cos(angles), jnp.sin(angles))


def rotate(vectors, cos_table, sin_table):
    halfway = vectors.shape[-1] // 2
    leading = vectors[..., :halfway]
    trailing = vectors[..., halfway:]
    cos_table = cos_table[:, None, :]
    sin_table = sin_table[:, None, :]
    return jnp.concatenate(
        [leading * cos_table - trailing * sin_table, trailing * cos_table + leading * sin_table], -1
    )


def unrotate(gradient, cos_table, sin_table):
    halfway = gradient.shape[-1] // 2
    leading = gradient[..., :halfway]
    trailing = gradient[..., halfway:]
    cos_table = cos_table[:, None, :]
    sin_table = sin_table[:, None, :]
    return jnp.concatenate(
        [leading * cos_table + trailing * sin_table, trailing * cos_table - leading * sin_table], -1
    )


def norm_forward(values, gain, shift):
    centre = values - jnp.mean(values, -1, keepdims=True)
    scale_inv = lax.rsqrt(jnp.mean(centre * centre, -1, keepdims=True) + epsilon)
    normed = centre * scale_inv
    return (normed * gain + shift, normed, scale_inv)


def norm_input_grad(grad_out, normed, scale_inv, gain):
    grad_normed = grad_out * gain
    centred = grad_normed - jnp.mean(grad_normed, -1, keepdims=True)
    return scale_inv * (centred - normed * jnp.mean(grad_normed * normed, -1, keepdims=True))


def norm_backward(grad_out, normed, scale_inv, gain):
    grad_gain = jnp.sum(grad_out * normed, 0)
    grad_shift = jnp.sum(grad_out, 0)
    return (norm_input_grad(grad_out, normed, scale_inv, gain), grad_gain, grad_shift)


def score_block(query_block, keys_rot, first_row, prefix_len):
    block_rows = query_block.shape[0]
    scores = jnp.einsum(
        "qhe,khe->hqk", query_block, keys_rot, preferred_element_type=jnp.float32
    ) * HD ** (-0.5)
    query_index = first_row + jnp.arange(block_rows)
    key_index = jnp.arange(keys_rot.shape[0])
    allowed = (key_index[None, :] < prefix_len) | (key_index[None, :] <= query_index[:, None])
    return jnp.where(allowed[None], scores, negative)


def attend_slot(packed):
    queries, keys_rot, values_in, prefix_len = packed
    block_rows = min(512, LEN)

    def one_block(first_row):
        query_block = lax.dynamic_slice_in_dim(queries, first_row, block_rows, 0)
        scores = score_block(query_block, keys_rot, first_row, prefix_len)
        row_top = jnp.max(scores, -1, keepdims=True)
        weights_raw = jnp.exp(scores - row_top)
        row_total = jnp.sum(weights_raw, -1, keepdims=True)
        weights = (weights_raw / row_total).astype(jnp.bfloat16)
        context = jnp.einsum("hqk,khe->qhe", weights, values_in, preferred_element_type=jnp.float32)
        return (context.astype(jnp.bfloat16), (row_top + jnp.log(row_total))[..., 0])

    context, log_total = lax.map(one_block, jnp.arange(LEN // block_rows) * block_rows)
    return (context.reshape(LEN, context.shape[2], context.shape[3]), log_total)


def attend_back(packed):
    queries, keys_rot, values_in, log_total, grad_context, prefix_len = packed
    block_rows = min(512, LEN)
    score_scale = HD ** (-0.5)

    def one_block(totals, sliced):
        grad_keys, grad_values = totals
        first_row, log_block = sliced
        query_block = lax.dynamic_slice_in_dim(queries, first_row, block_rows, 0)
        grad_block = lax.dynamic_slice_in_dim(grad_context, first_row, block_rows, 0)
        scores = score_block(query_block, keys_rot, first_row, prefix_len)
        weights = jnp.exp(scores - log_block[..., None])
        grad_weights = jnp.einsum(
            "qhe,khe->hqk", grad_block, values_in, preferred_element_type=jnp.float32
        )
        row_inner = jnp.sum(weights * grad_weights, -1, keepdims=True)
        grad_scores = (weights * (grad_weights - row_inner)).astype(jnp.bfloat16)
        grad_query = (
            jnp.einsum("hqk,khe->qhe", grad_scores, keys_rot, preferred_element_type=jnp.float32)
            * score_scale
        )
        grad_keys = (
            grad_keys
            + jnp.einsum(
                "hqk,qhe->khe", grad_scores, query_block, preferred_element_type=jnp.float32
            )
            * score_scale
        )
        grad_values = grad_values + jnp.einsum(
            "hqk,qhe->khe",
            weights.astype(jnp.bfloat16),
            grad_block,
            preferred_element_type=jnp.float32,
        )
        return ((grad_keys, grad_values), grad_query)

    starting = jnp.zeros(keys_rot.shape, jnp.float32)
    block_starts = jnp.arange(LEN // block_rows) * block_rows
    (grad_keys, grad_values), grad_query = lax.scan(
        one_block, (starting, starting), (block_starts, log_total)
    )
    return (grad_query.reshape(keys_rot.shape), grad_keys, grad_values)


def on_device(
    tokens,
    cotangent,
    w_qkv,
    b_qkv,
    w_out,
    b_out,
    gain_one,
    shift_one,
    w_gu,
    b_gu,
    w_down,
    b_down,
    gain_two,
    shift_two,
    prefix,
    span_offset,
    cluster,
):
    rows_local = tokens.shape[0]
    slots_local = prefix.shape[0]
    rows_group = slots_local * LEN
    width_qkv = w_qkv.shape[2]
    heads_local = width_qkv // HD
    width_ffn = w_gu.shape[2]
    data_index = lax.axis_index("dp")
    tensor_index = lax.axis_index("tensor")
    own_start = tensor_index * rows_local
    occupied = jnp.sum((cluster == data_index).astype(jnp.int32))
    row_global = own_start + jnp.arange(rows_local)
    live_rows = jnp.where(row_global // LEN < occupied, 1.0, 0.0).astype(jnp.float32)[:, None]
    live_columns = tensor_index * width_ffn + jnp.arange(width_ffn) < FF
    cos_tables, sin_tables = jax.vmap(rotary_tables)(prefix, span_offset)

    def project_inputs(gathered):
        linear = (
            jnp.einsum("td,dcn->tcn", gathered, w_qkv, preferred_element_type=jnp.float32) + b_qkv
        )
        linear = linear.reshape(slots_local, LEN, 3, heads_local, HD)
        queries = jax.vmap(rotate)(linear[:, :, 0], cos_tables, sin_tables).astype(jnp.bfloat16)
        keys_rot = jax.vmap(rotate)(linear[:, :, 1], cos_tables, sin_tables).astype(jnp.bfloat16)
        return (queries, keys_rot, linear[:, :, 2].astype(jnp.bfloat16))

    def activate(gate_up):
        return jnp.where(
            live_columns, jax.nn.gelu(gate_up[:, 0], approximate=True) * gate_up[:, 1], 0.0
        )

    def feed_inputs(gathered):
        gate_up = (
            jnp.einsum("td,dcn->tcn", gathered, w_gu, preferred_element_type=jnp.float32) + b_gu
        )
        activated, pull_act = jax.vjp(activate, gate_up)
        return (activated.astype(jnp.bfloat16), pull_act)

    tokens_all = lax.all_gather(tokens, "tensor", axis=0, tiled=True)
    queries, keys_rot, values_in = project_inputs(tokens_all)
    context, log_total = lax.map(attend_slot, (queries, keys_rot, values_in, prefix))
    context_rows = context.reshape(rows_group, width_qkv)
    attended = (
        lax.psum_scatter(
            jnp.dot(context_rows, w_out, preferred_element_type=jnp.float32).astype(jnp.bfloat16),
            "tensor",
            scatter_dimension=0,
            tiled=True,
        ).astype(jnp.float32)
        + b_out
    )
    first_sum = deep_alpha * tokens.astype(jnp.float32) + attended
    hidden_one, normed_one, inv_one = norm_forward(first_sum, gain_one, shift_one)
    hidden_low = hidden_one.astype(jnp.bfloat16)
    hidden_all = lax.all_gather(hidden_low, "tensor", axis=0, tiled=True)
    inner_low, pull_act = feed_inputs(hidden_all)
    fed = (
        lax.psum_scatter(
            jnp.dot(inner_low, w_down, preferred_element_type=jnp.float32).astype(jnp.bfloat16),
            "tensor",
            scatter_dimension=0,
            tiled=True,
        ).astype(jnp.float32)
        + b_down
    )
    second_sum = deep_alpha * hidden_one + fed
    layer_rows, normed_two, inv_two = norm_forward(second_sum, gain_two, shift_two)
    layer_out = layer_rows * live_rows
    grad_layer = cotangent.astype(jnp.float32) * live_rows
    grad_second, grad_gain_two, grad_shift_two = norm_backward(
        grad_layer, normed_two, inv_two, gain_two
    )
    grad_second_all = lax.all_gather(
        grad_second.astype(jnp.bfloat16), "tensor", axis=0, tiled=True
    ).astype(grad_second.dtype)
    grad_fed_all = grad_second_all.astype(jnp.bfloat16)
    hidden_all = lax.all_gather(hidden_low, "tensor", axis=0, tiled=True)
    inner_low, pull_act = feed_inputs(hidden_all)
    grad_w_down = jnp.einsum(
        "tn,td->nd", inner_low, grad_fed_all, preferred_element_type=jnp.float32
    )
    grad_inner = jnp.einsum("td,nd->tn", grad_fed_all, w_down, preferred_element_type=jnp.float32)
    grad_gate_up = pull_act(grad_inner)[0].astype(jnp.bfloat16)
    grad_b_gu = jnp.sum(grad_gate_up.astype(jnp.float32), 0)
    grad_w_gu = jnp.einsum(
        "td,tcn->dcn", hidden_all, grad_gate_up, preferred_element_type=jnp.float32
    )
    grad_hidden = (
        lax.psum_scatter(
            jnp.einsum(
                "tcn,dcn->td", grad_gate_up, w_gu, preferred_element_type=jnp.float32
            ).astype(jnp.bfloat16),
            "tensor",
            scatter_dimension=0,
            tiled=True,
        ).astype(jnp.float32)
        + deep_alpha * grad_second
    )
    grad_first, grad_gain_one, grad_shift_one = norm_backward(
        grad_hidden, normed_one, inv_one, gain_one
    )
    grad_att_all = lax.all_gather(grad_first.astype(jnp.bfloat16), "tensor", axis=0, tiled=True)
    grad_w_out = jnp.einsum(
        "tn,td->nd", context_rows, grad_att_all, preferred_element_type=jnp.float32
    )
    grad_context = jnp.einsum("td,nd->tn", grad_att_all, w_out, preferred_element_type=jnp.float32)
    grad_context = grad_context.astype(jnp.bfloat16).reshape(slots_local, LEN, heads_local, HD)
    tokens_all = lax.all_gather(tokens, "tensor", axis=0, tiled=True)
    queries, keys_rot, values_in = project_inputs(tokens_all)
    grad_query, grad_keys, grad_values = lax.map(
        attend_back, (queries, keys_rot, values_in, log_total, grad_context, prefix)
    )
    grad_linear = jnp.stack(
        [
            jax.vmap(unrotate)(grad_query, cos_tables, sin_tables),
            jax.vmap(unrotate)(grad_keys, cos_tables, sin_tables),
            grad_values,
        ],
        2,
    )
    grad_linear = grad_linear.reshape(rows_group, 3, width_qkv).astype(jnp.bfloat16)
    grad_b_qkv = jnp.sum(grad_linear.astype(jnp.float32), 0)
    grad_w_qkv = jnp.einsum(
        "td,tcn->dcn", tokens_all, grad_linear, preferred_element_type=jnp.float32
    )
    input_grad = (
        lax.psum_scatter(
            jnp.einsum(
                "tcn,dcn->td", grad_linear, w_qkv, preferred_element_type=jnp.float32
            ).astype(jnp.bfloat16),
            "tensor",
            scatter_dimension=0,
            tiled=True,
        ).astype(jnp.float32)
        + deep_alpha * grad_first
    )
    norm_grads = lax.psum(
        (
            grad_gain_one,
            grad_shift_one,
            jnp.sum(grad_first, 0),
            grad_gain_two,
            grad_shift_two,
            jnp.sum(grad_second, 0),
        ),
        ("dp", "tensor"),
    )
    grad_w_qkv, grad_b_qkv, grad_w_out, grad_w_gu, grad_b_gu, grad_w_down = (
        lax.psum(grad_w_qkv.astype(jnp.bfloat16), "dp").astype(jnp.float32),
        lax.psum(grad_b_qkv.astype(jnp.bfloat16), "dp").astype(jnp.float32),
        lax.psum(grad_w_out.astype(jnp.bfloat16), "dp").astype(jnp.float32),
        lax.psum(grad_w_gu.astype(jnp.bfloat16), "dp").astype(jnp.float32),
        lax.psum(grad_b_gu.astype(jnp.bfloat16), "dp").astype(jnp.float32),
        lax.psum(grad_w_down.astype(jnp.bfloat16), "dp").astype(jnp.float32),
    )
    return (
        layer_out,
        input_grad,
        grad_w_qkv,
        grad_b_qkv,
        grad_w_out,
        norm_grads[2],
        norm_grads[0],
        norm_grads[1],
        grad_w_gu,
        grad_b_gu,
        grad_w_down,
        norm_grads[5],
        norm_grads[3],
        norm_grads[4],
    )


def solution(mesh):
    placed = (
        P(("dp", "tensor"), None),
        P(("dp", "tensor"), None),
        P(None, None, "tensor"),
        P(None, "tensor"),
        P("tensor", None),
        P(),
        P(),
        P(),
        P(None, None, "tensor"),
        P(None, "tensor"),
        P("tensor", None),
        P(),
        P(),
        P(),
        P("dp"),
        P("dp"),
        P(),
    )
    return jax.shard_map(
        on_device,
        mesh=mesh,
        in_specs=placed,
        out_specs=(
            P(("dp", "tensor"), None),
            P(("dp", "tensor"), None),
            P(None, None, "tensor"),
            P(None, "tensor"),
            P("tensor", None),
            P(),
            P(),
            P(),
            P(None, None, "tensor"),
            P(None, "tensor"),
            P("tensor", None),
            P(),
            P(),
            P(),
        ),
        check_vma=False,
    )
```

profile of v0, /device:TPU:10, one launch (start us, length us, event | category | flops | bytes accessed | tf_op | source)
XLA Modules:
  0.0 2318.8 jit_solution(13830182877447541743)
XLA Ops:
  12.7 172.2 %all-gather.5.cloned.1.call-done = bf16[3072,2048]{1,0:T(8,128)(2,1)} async-done(((bf16[384,2048]{1,0:T(8,128)(2,1)}), bf16[3072,2048]{1,0:T(8,128)(2,1)}) %all-gather.5.cloned.1.call-update) | async-done | bytes 12582928 | tf_op jit(solution)/shard_map/all_gather | solution.py:198
  185.0 15.1 fusion.57
  200.1 12.8 reshape.305
  248.9 85.4 %while.54 = (s32[]{:T(128)}, bf16[3,1024,2,128]{3,2,1,0:T(2,128)(2,1)}, f32[3,2,2,512]{3,2,1,0:T(2,128)}, bf16[3,1024,2,128]{3,1,2,0:T(8,128)(2,1)}, bf16[3,1024...) while((s32[]{:T(128)}, ...), condition=%wide.region_5.6_spmd, body=%wide.region_0.5_spmd.sunk | while | flops 550633984 | bytes 23125944 | solution.py:200
  254.1 20.8 while.57
  282.4 20.8 while.57
  310.7 20.8 while.57
  334.3 9.7 convolution_convert_fusion.1
  344.1 206.8 %reduce-scatter.5.cloned.1.call-done = bf16[384,2048]{1,0:T(8,128)(2,1)} async-done(((bf16[3072,2048]{1,0:T(8,128)(2,1)}), bf16[384,2048]{1,0:T(8,128)(2,1)}) %reduce-scatter.5.cloned.1.call-update) | async-done | bytes 1572880 | tf_op jit(solution)/shard_map/reduce_scatter | solution.py:203
  557.0 174.5 %all-gather.7.cloned.1.call-done = bf16[3072,2048]{1,0:T(8,128)(2,1)} async-done(((bf16[384,2048]{1,0:T(8,128)(2,1)}), bf16[3072,2048]{1,0:T(8,128)(2,1)}) %all-gather.7.cloned.1.call-update) | async-done | bytes 12582928 | tf_op jit(solution)/shard_map/all_gather | solution.py:214
  731.5 27.2 %broadcast_add_fusion = f32[3072,2,684]{0,2,1:T(8,128)S(1)} fusion(f32[2,684]{1,0:T(2,128)S(1)} %copy-done.37, bf16[3072,2048]{1,0:T(8,128)(2,1)} %all-gather.7.cloned.1.call-done, bf16[2048,2,684]{0,1,2:T(2,128)(2,1)} %param.33), kind=kOutput, calls=%fused_computation.95 | convolution fusion | flops 17217626112 | bytes 35001696 | tf_op jit(solution)/shard_map/td,dcn->tcn/dot_general | solution.py:193
  769.6 14.9 convolution_convert_fusion
  786.4 204.9 %reduce-scatter.7.cloned.1.call-done = bf16[384,2048]{1,0:T(8,128)(2,1)} async-done(((bf16[3072,2048]{1,0:T(8,128)(2,1)}), bf16[384,2048]{1,0:T(8,128)(2,1)}) %reduce-scatter.7.cloned.1.call-update) | async-done | bytes 1572880 | tf_op jit(solution)/shard_map/reduce_scatter | solution.py:217
  1002.9 174.5 %all-gather.9.cloned.1.call-done = bf16[3072,2048]{1,0:T(8,128)(2,1)} async-done(((bf16[384,2048]{1,0:T(8,128)(2,1)}), bf16[3072,2048]{1,0:T(8,128)(2,1)}) %all-gather.9.cloned.1.call-update) | async-done | bytes 12582928 | tf_op jit(solution)/shard_map/all_gather | solution.py:232
  1177.4 25.2 %multiply_bitcast_fusion = (f32[3072,1,684]{0,2,1:T(8,128)}, f32[3072,1,684]{0,2,1:T(8,128)}) fusion(pred[684]{0:T(1024)(128)(4,1)S(1)} %add_compare_fusion, f32[3072,2,684]{0,2,1:T(8,128)} %copy-done.14, bf16[3072,2048]{1,0:T(8,128)(2,1)} %all-gather.9.cloned.1.call-done, bf16[684,2048]{1,0:T(8,128)(2,1)} %param.35), kind=kOutput, calls=%fused_computation.93 | convolution fusion | flops 8655040512 | bytes 49005228 | tf_op jit(solution)/shard_map/td,nd->tn/dot_general | solution.py:241
  1202.6 29.6 %bitcast_convert_fusion.1 = bf16[3072,2048]{1,0:T(8,128)(2,1)} fusion(bf16[2048,2,684]{0,1,2:T(2,128)(2,1)} %param.33, f32[3072,1,684]{0,2,1:T(8,128)} %get-tuple-element.388, f32[3072,1,684]{0,2,1:T(8,128)} %get-tuple-element.387), kind=kOutput, calls=%fused_computation.70 | convolution fusion | flops 17228120064 | bytes 34996224 | tf_op jit(solution)/shard_map/tcn,dcn->td/dot_general | solution.py:249
  1232.2 206.8 %reduce-scatter.9.cloned.1.call-done = bf16[384,2048]{1,0:T(8,128)(2,1)} async-done(((bf16[3072,2048]{1,0:T(8,128)(2,1)}), bf16[384,2048]{1,0:T(8,128)(2,1)}) %reduce-scatter.9.cloned.1.call-update) | async-done | bytes 1572880 | tf_op jit(solution)/shard_map/reduce_scatter | solution.py:248
  1450.5 14.5 convolution_convert_fusion.3
  1465.0 23.7 %fusion.62 = bf16[2048,2,684]{0,2,1:T(8,128)(2,1)} fusion(bf16[3072,2048]{1,0:T(8,128)(2,1)} %all-gather.7.cloned.1.call-done, f32[3072,1,684]{0,2,1:T(8,128)} %get-tuple-element.388, f32[3072,1,684]{0,2,1:T(8,128)S(1)} %bitcast.201), kind=kOutput, calls=%fused_computation.100 | convolution fusion | flops 17224630272 | bytes 34996224 | tf_op jit(solution)/shard_map/td,tcn->dcn/dot_general | solution.py:244
  1488.7 136.2 %all-gather.11.cloned.1.call-done = bf16[3072,2048]{1,0:T(8,128)(2,1)} async-done(((bf16[384,2048]{1,0:T(8,128)(2,1)}), bf16[3072,2048]{1,0:T(8,128)(2,1)}) %all-gather.11.cloned.1.call-update) | async-done | bytes 12582928 | tf_op jit(solution)/shard_map/all_gather | solution.py:261
  1624.9 9.4 convolution_convert_fusion.2
  1637.9 169.4 %while.56 = (s32[]{:T(128)}, f32[3,1024,2,128]{1,3,2,0:T(8,128)}, f32[3,1024,2,128]{1,3,2,0:T(8,128)}, bf16[3,1024,2,128]{1,3,2,0:T(8,128)(2,1)}, f32[3,2,2,512]...) while((s32[]{:T(128)}, f32[3,1024,2,128]{1,3,2,0:T(8,128)}, ...), condition=%wide.region_22.23_spmd, body=%wide.region_18.22_spmd.sunk | while | flops 1360396800 | bytes 105959632 | solution.py:269
  1647.2 39.7 %while.58 = (s32[]{:T(128)}, f32[1024,2,128]{0,2,1:T(8,128)}, f32[1024,2,128]{0,2,1:T(8,128)}, f32[2,512,2,128]{3,2,1,0:T(2,128)}, s32[2]{0:T(128)S(1)}, /*index...) while((s32[]{:T(128)}, f32[1024,2,128]{0,2,1:T(8,128)}, ...), condition=%wide.region_21.21_spmd.clone, body=%wide.region_19.20_spmd.clone.sunk | while | flops 1360396800 | bytes 92310432 | solution.py:137
  1703.6 39.7 %while.58 = (s32[]{:T(128)}, f32[1024,2,128]{0,2,1:T(8,128)}, f32[1024,2,128]{0,2,1:T(8,128)}, f32[2,512,2,128]{3,2,1,0:T(2,128)}, s32[2]{0:T(128)S(1)}, /*index...) while((s32[]{:T(128)}, f32[1024,2,128]{0,2,1:T(8,128)}, ...), condition=%wide.region_21.21_spmd.clone, body=%wide.region_19.20_spmd.clone.sunk | while | flops 1360396800 | bytes 92310432 | solution.py:137
  1760.0 39.7 %while.58 = (s32[]{:T(128)}, f32[1024,2,128]{0,2,1:T(8,128)}, f32[1024,2,128]{0,2,1:T(8,128)}, f32[2,512,2,128]{3,2,1,0:T(2,128)}, s32[2]{0:T(128)S(1)}, /*index...) while((s32[]{:T(128)}, f32[1024,2,128]{0,2,1:T(8,128)}, ...), condition=%wide.region_21.21_spmd.clone, body=%wide.region_19.20_spmd.clone.sunk | while | flops 1360396800 | bytes 92310432 | solution.py:137
  1849.7 7.9 convolution_convert_fusion.4
  1857.5 14.6 fusion.71
  1872.1 14.7 bitcast_convert_fusion
  1893.8 44.6 %all-reduce.2 = (f32[2048]{0:T(1024)}, f32[2048]{0:T(1024)}, f32[2048]{0:T(1024)}, f32[2048]{0:T(1024)}, f32[2048]{0:T(1024)}, /*index=5*/f32[2048]{0:T(1024)}) all-reduce(f32[2048]{0:T(1024)S(1)} %copy-done.31, f32[2048]{0:T(1024)S(1)} %copy-done.28, f32[2048]{0:T(1024)S(1)} %copy-done.29, ...), channel_id=1, replica_groups=mesh['dp'=4,'tensor'=8] {'dp','tensor'}, use_global_device_ids=true, to_apply=%region_29.30 | all-reduce | flops 12288 | bytes 98304 | tf_op jit(solution)/shard_map/psum | solution.py:296
  1949.4 148.3 %all-reduce.7.cloned.1.call-done = (bf16[2048,3,256]{0,2,1:T(8,128)(2,1)}, bf16[2048,2,684]{0,2,1:T(8,128)(2,1)}, bf16[256,2048]{1,0:T(8,128)(2,1)}, bf16[684,2048]{1,0:T(8,128)(2,1)}) async-done(((bf16[2048,3,256]{0,2,1:T(8,128)(2,1)}, bf16[2048,2,684]{0,2,1:T(8,128)(2,1)}, bf16[256,2048]{1,0:T(8,128)(2,1)}, bf16[684,2048]{1,0:T(8,128)(2,1)}), (bf16[2048,3,256]{0,2,1:T(8,128)(2,1)}, ...) | async-done | bytes 12599312 | tf_op jit(solution)/shard_map/psum | solution.py:308
  2097.8 26.4 %copy.54 = f32[2048,2,684]{0,1,2:T(2,128)} copy(bf16[2048,2,684]{0,2,1:T(8,128)(2,1)} %get-tuple-element.370) | data formatting | bytes 16809984
  2136.3 170.8 %reduce-scatter.11.cloned.1.call-done = bf16[384,2048]{1,0:T(8,128)(2,1)} async-done(((bf16[3072,2048]{1,0:T(8,128)(2,1)}), bf16[384,2048]{1,0:T(8,128)(2,1)}) %reduce-scatter.11.cloned.1.call-update) | async-done | bytes 1572880 | tf_op jit(solution)/shard_map/reduce_scatter | solution.py:286
  (438 shorter events, 393.6 us)
Async XLA Ops:
  7.2 177.8 %copy-start = (bf16[2048,3,256]{2,0,1:T(8,128)(2,1)S(1)}, bf16[2048,3,256]{2,0,1:T(8,128)(2,1)}, u32[]{:S(2)}) copy-start(bf16[2048,3,256]{2,0,1:T(8,128)(2,1)} %param.27) | copy-start | bytes 9437188
  7.2 177.8 %copy-start.38 = (f32[3,256]{1,0:T(4,128)S(1)}, f32[3,256]{1,0:T(4,128)}, u32[]{:S(2)}) copy-start(f32[3,256]{1,0:T(4,128)} %param.28) | copy-start | bytes 9220
  7.2 177.8 %all-gather.5.cloned.1.call-start = ((), (), s32[]{:S(2)}) async-start(), calls=%async_computation.4 | async-start | bytes 14155776 | tf_op jit(solution)/shard_map/all_gather | solution.py:198
  7.9 542.9 %reduce-scatter.5.cloned.1.call-start = ((), (), s32[]{:S(2)}) async-start(), calls=%async_computation.5 | async-start | bytes 14155776 | tf_op jit(solution)/shard_map/reduce_scatter | solution.py:203
  243.5 5.4 copy-start.34
  344.0 206.8 %copy-start.22 = (f32[2048]{0:T(1024)S(1)}, f32[2048]{0:T(1024)}, u32[]{:S(2)}) copy-start(f32[2048]{0:T(1024)} %param.30) | copy-start | bytes 24580
  344.0 210.6 %copy-start.27 = (f32[2048]{0:T(1024)S(1)}, f32[2048]{0:T(1024)}, u32[]{:S(2)}) copy-start(f32[2048]{0:T(1024)} %param.32) | copy-start | bytes 24580
  344.0 210.6 %copy-start.23 = (f32[2048]{0:T(1024)S(1)}, f32[2048]{0:T(1024)}, u32[]{:S(2)}) copy-start(f32[2048]{0:T(1024)} %param.31) | copy-start | bytes 24580
  344.0 387.4 %all-gather.7.cloned.1.call-start = ((), (), s32[]{:S(2)}) async-start(), calls=%async_computation.6 | async-start | bytes 14155776 | tf_op jit(solution)/shard_map/all_gather | solution.py:214
  554.6 176.8 %copy-start.37 = (f32[2,684]{1,0:T(2,128)S(1)}, f32[2,684]{1,0:T(2,128)}, u32[]{:S(2)}) copy-start(f32[2,684]{1,0:T(2,128)} %param.34) | copy-start | bytes 16420
  556.9 434.5 %reduce-scatter.7.cloned.1.call-start = ((), (), s32[]{:S(2)}) async-start(), calls=%async_computation.7 | async-start | bytes 14155776 | tf_op jit(solution)/shard_map/reduce_scatter | solution.py:217
  758.6 5.9 copy-start.14
  784.5 206.9 %copy-start.33 = (f32[2048]{0:T(1024)S(1)}, f32[2048]{0:T(1024)}, u32[]{:S(2)}) copy-start(f32[2048]{0:T(1024)} %param.36) | copy-start | bytes 24580
  784.5 392.9 %all-gather.9.cloned.1.call-start = ((), (), s32[]{:S(2)}) async-start(), calls=%async_computation.8 | async-start | bytes 14155776 | tf_op jit(solution)/shard_map/all_gather | solution.py:232
  1002.9 436.2 %reduce-scatter.9.cloned.1.call-start = ((), (), s32[]{:S(2)}) async-start(), calls=%async_computation.9 | async-start | bytes 14155776 | tf_op jit(solution)/shard_map/reduce_scatter | solution.py:248
  1232.2 392.7 %all-gather.11.cloned.1.call-start = ((), (), s32[]{:S(2)}) async-start(), calls=%async_computation.10 | async-start | bytes 14155776 | tf_op jit(solution)/shard_map/all_gather | solution.py:261
  1439.1 5.2 copy-start.9
  1439.1 5.2 copy-start.11
  1439.1 5.2 copy-start.13
  1439.1 5.6 copy-start.20
  1449.0 16.0 slice-start
  1450.4 647.4 %all-reduce.7.cloned.1.call-start = ((), (), s32[]{:S(2)}) async-start(), calls=%async_computation.12 | async-start | bytes 25296896 | tf_op jit(solution)/shard_map/psum | solution.py:308
  1450.5 14.6 slice-start.1
  1450.5 14.6 slice-start.2
  1849.7 7.9 copy-start.17
  1872.1 435.0 %reduce-scatter.11.cloned.1.call-start = ((), (), s32[]{:S(2)}) async-start(), calls=%async_computation.11 | async-start | bytes 14155776 | tf_op jit(solution)/shard_map/reduce_scatter | solution.py:286
  1886.9 6.9 copy-start.25
  1886.9 6.9 copy-start.26
  1886.9 6.9 copy-start.28
  1886.9 6.8 copy-start.29
  1886.9 6.8 copy-start.30
  1886.9 6.8 copy-start.31
  (60 other events, 163.0 us)
Sparse Core Ops, SparseCore 0:
  10.2 174.7 all-gather.4
  344.2 206.6 reduce-scatter.4
  557.0 174.3 all-gather.6
  784.6 206.7 reduce-scatter.6
  1003.0 174.3 all-gather.8
  1232.3 206.7 reduce-scatter.8
  1450.5 174.3 all-gather.10
  1872.2 225.4 all-reduce.6
  2101.3 205.7 reduce-scatter.10
where the time goes:
time: 2330 us; the launch traced here: 2320 us
  waiting for transfers between devices  1600 us (69%)
  matrix products  300 us (13%)
  local copies, waits for them, and re-layouts  220 us (9%)
  other arithmetic  111 us (5%)
  blocking collectives  51.3 us (2%)
  loops' own time  25.2 us (1%)
    reduce_scatter x1, waiting for transfers between devices, on_device(): lax.psum_scatter(jnp.einsum('tcn,dcn->td', grad_gate_up, w_gu, preferred_...  207 us
    reduce_scatter x1, waiting for transfers between devices, on_device(): lax.psum_scatter(jnp.dot(context_rows, w_out, preferred_element_type=jnp....  207 us
    reduce_scatter x1, waiting for transfers between devices, on_device(): lax.psum_scatter(jnp.dot(inner_low, w_down, preferred_element_type=jnp.fl...  205 us
    all_gather x1, waiting for transfers between devices, on_device(): lax.all_gather(grad_second.astype(jnp.bfloat16), 'tensor', axis=0, tiled=...  174 us
    all_gather x1, waiting for transfers between devices, on_device(): hidden_all = lax.all_gather(hidden_low, 'tensor', axis=0, tiled=True)  174 us
    all_gather x1, waiting for transfers between devices, on_device(): tokens_all = lax.all_gather(tokens, 'tensor', axis=0, tiled=True)  172 us
    reduce_scatter x1, waiting for transfers between devices, on_device(): lax.psum_scatter(jnp.einsum('tcn,dcn->td', grad_linear, w_qkv, preferred_...  171 us
    psum x1, waiting for transfers between devices, on_device(): lax.psum(grad_w_qkv.astype(jnp.bfloat16), 'dp').astype(jnp.float32)  148 us
  transfers between devices with their start and end apart: 9, of which 9 were waited for; matrix products, arithmetic and copies ran while one was open for 5% of the time, Pallas kernels for 0%

commit v1 on v0

v1 whole, which is shorter than its diff:
```python
import math

import jax
import jax.numpy as jnp
from jax import lax
from jax.sharding import PartitionSpec as P

HD = 128
FF = 5461
LEN = 1024
CAP = 3

deep_alpha = math.sqrt(48.0)
epsilon = 1e-05
negative = -1e30
theta_base = 10000.0
f32 = jnp.float32
bf16 = jnp.bfloat16


def bits_of(count):
    return [1 << b for b in range(count.bit_length() - 1)]


def permute(value, axis, size, bit):
    return lax.ppermute(value, axis, [(i, i ^ bit) for i in range(size)])


def rotate(vectors, cos_table, sin_table):
    halfway = vectors.shape[-1] // 2
    leading = vectors[..., :halfway]
    trailing = vectors[..., halfway:]
    return jnp.concatenate(
        [leading * cos_table - trailing * sin_table, trailing * cos_table + leading * sin_table], -1
    )


def norm_forward(values, gain, shift):
    centre = values - jnp.mean(values, -1, keepdims=True)
    scale_inv = lax.rsqrt(jnp.mean(centre * centre, -1, keepdims=True) + epsilon)
    normed = centre * scale_inv
    return (normed * gain + shift, normed, scale_inv)


def norm_backward(grad_out, normed, scale_inv, gain):
    grad_gain = jnp.sum(grad_out * normed, 0)
    grad_shift = jnp.sum(grad_out, 0)
    grad_normed = grad_out * gain
    centred = grad_normed - jnp.mean(grad_normed, -1, keepdims=True)
    grad_in = scale_inv * (
        centred - normed * jnp.mean(grad_normed * normed, -1, keepdims=True)
    )
    return (grad_in, grad_gain, grad_shift)


def top_bit(number):
    return 1 << (number.bit_length() - 1)


def low_bit(number):
    return number & -number


class Group:
    def __init__(self, size):
        self.size = size
        self.width = size // 2

    def gather(self, own):
        rows = own.shape[0] // 2
        got = {0: own}
        for offset in range(1, self.width):
            high, low = top_bit(offset), low_bit(offset)
            if high == low:
                got[offset] = permute(own, "tensor", self.size, high)
            else:
                got[offset] = jnp.concatenate(
                    [
                        permute(got[offset ^ high][:rows], "tensor", self.size, high),
                        permute(got[offset ^ low][rows:], "tensor", self.size, low),
                    ],
                    0,
                )
        return [got[offset] for offset in range(self.width)]

    def scatter(self, parts):
        rows = parts[0].shape[0] // 2
        low_half = {o: part[:rows] for o, part in enumerate(parts)}
        high_half = {o: part[rows:] for o, part in enumerate(parts)}
        total = parts[0].astype(f32)

        def add(mine, theirs):
            return (mine.astype(f32) + theirs.astype(f32)).astype(bf16)

        count = lambda o: bin(o).count("1")
        for offset in sorted(range(1, self.width), key=lambda o: -count(o)):
            high, low = top_bit(offset), low_bit(offset)
            if high == low:
                whole = jnp.concatenate([low_half[offset], high_half[offset]], 0)
                total = total + permute(whole, "tensor", self.size, high).astype(f32)
            else:
                a, b = offset ^ high, offset ^ low
                low_half[a] = add(low_half[a], permute(low_half[offset], "tensor", self.size, high))
                high_half[b] = add(high_half[b], permute(high_half[offset], "tensor", self.size, low))
        return total


def block_moves(size):
    width = size // 2
    edges = {0: [], 1: []}
    for b in range(CAP * size):
        slot, j = divmod(b, size)
        target = (width if slot else 0) + j // 2
        edges[1 if slot == 2 else 0].append((b // CAP, b % CAP, target, j % 2))
    plans = {}
    for kind, listed in edges.items():
        local = [e for e in listed if e[0] == e[2]]
        rounds = []
        for e in (e for e in listed if e[0] != e[2]):
            for r in rounds:
                if all(e[0] != o[0] and e[2] != o[2] for o in r):
                    r.append(e)
                    break
            else:
                rounds.append([e])
        plans[kind] = (local, rounds)
    return plans


def pick(index, values):
    out = values[0]
    for k, value in enumerate(values[1:], 1):
        out = jnp.where(index == k, value, out)
    return out


def lookup(table, index):
    return jnp.asarray(table, jnp.int32)[index]


def move_in(blocks, t, size, kind):
    local, rounds = block_moves(size)[kind]
    got = []
    for r in rounds:
        which = [0] * size
        for src, i, dst, place in r:
            which[src] = i
        send = pick(lookup(which, t), blocks)
        got.append(lax.ppermute(send, "tensor", [(e[0], e[2]) for e in r]))
    places = []
    for place in range(2):
        choice = [0] * size
        for src, i, dst, at in local:
            if at == place:
                choice[dst] = i
        for k, r in enumerate(rounds):
            for src, i, dst, at in r:
                if at == place:
                    choice[dst] = CAP + k
        places.append(pick(lookup(choice, t), blocks + got))
    return jnp.concatenate(places, 0)


def move_out(item, other, t, size):
    plans = block_moves(size)
    half = item.shape[0] // 2
    pieces = {0: [item[:half], item[half:]], 1: [other[:half], other[half:]]}
    sources = []
    choice = [[0] * size for _ in range(CAP)]
    for kind in (0, 1):
        local, rounds = plans[kind]
        for src, i, dst, at in local:
            choice[i][src] = len(sources) + at
        sources += pieces[kind]
        for r in rounds:
            which = [0] * size
            for src, i, dst, at in r:
                which[dst] = at
                choice[i][src] = len(sources)
            send = pick(lookup(which, t), pieces[kind])
            sources.append(lax.ppermute(send, "tensor", [(e[2], e[0]) for e in r]))
    return jnp.concatenate([pick(lookup(choice[i], t), sources) for i in range(CAP)], 0)


def across(value, n_dp):
    got = {0: value}
    for bit in reversed(bits_of(n_dp)):
        for offset in list(got):
            got[offset | bit] = permute(got[offset], "dp", n_dp, bit)
    return [got[offset] for offset in range(n_dp)]


def attend(queries, keys_rot, values_in, allowed):
    scores = jnp.einsum("qhe,khe->hqk", queries, keys_rot, preferred_element_type=f32)
    scores = jnp.where(allowed[None], scores * HD ** (-0.5), negative)
    row_top = jnp.max(scores, -1, keepdims=True)
    weights_raw = jnp.exp(scores - row_top)
    row_total = jnp.sum(weights_raw, -1, keepdims=True)
    weights = (weights_raw / row_total).astype(bf16)
    context = jnp.einsum("hqk,khe->qhe", weights, values_in, preferred_element_type=f32)
    return context.astype(bf16), (row_top + jnp.log(row_total))[..., 0]


def attend_back(queries, keys_rot, values_in, log_total, grad_context, allowed):
    scale = HD ** (-0.5)
    scores = jnp.einsum("qhe,khe->hqk", queries, keys_rot, preferred_element_type=f32)
    scores = jnp.where(allowed[None], scores * scale, negative)
    weights = jnp.exp(scores - log_total[..., None])
    grad_weights = jnp.einsum("qhe,khe->hqk", grad_context, values_in, preferred_element_type=f32)
    row_inner = jnp.sum(weights * grad_weights, -1, keepdims=True)
    grad_scores = (weights * (grad_weights - row_inner)).astype(bf16)
    grad_query = jnp.einsum("hqk,khe->qhe", grad_scores, keys_rot, preferred_element_type=f32) * scale
    grad_keys = jnp.einsum("hqk,qhe->khe", grad_scores, queries, preferred_element_type=f32) * scale
    grad_values = jnp.einsum(
        "hqk,qhe->khe", weights.astype(bf16), grad_context, preferred_element_type=f32
    )
    return grad_query, grad_keys, grad_values


def on_device(
    n_dp,
    n_tensor,
    tokens,
    cotangent,
    w_qkv,
    b_qkv,
    w_out,
    b_out,
    gain_one,
    shift_one,
    w_gu,
    b_gu,
    w_down,
    b_down,
    gain_two,
    shift_two,
    prefix,
    span_offset,
    cluster,
):
    d = lax.axis_index("dp")
    t = lax.axis_index("tensor")
    group = Group(n_tensor)
    width = group.width
    h = t // width
    q = t % width
    rows = LEN // width
    model = tokens.shape[1]
    block = LEN // n_tensor

    counts = jnp.sum((cluster[None, :] == jnp.arange(n_dp)[:, None]).astype(jnp.int32), 1)
    spare = jnp.maximum(2 - counts, 0)
    extra = (counts == CAP).astype(jnp.int32)
    spare_before = jnp.cumsum(spare) - spare
    extra_rank = jnp.cumsum(extra) - extra

    def overflow_source(index, place):
        rank = spare_before[index] + place - counts[index]
        hit = (extra == 1) & (extra_rank == rank)
        return jnp.sum(jnp.where(hit, jnp.arange(n_dp), 0))

    source_here = overflow_source(d, h)
    source_other = overflow_source(d, 0)
    foreign = counts[d] <= h
    any_empty = jnp.any(counts == 0)
    rank_out = extra_rank[d]
    ends = spare_before + spare
    out_index = jnp.sum((ends <= rank_out).astype(jnp.int32))
    out_place = jnp.minimum(counts[out_index], 2) + rank_out - spare_before[out_index]

    def spread(array):
        blocks = [array[i * block : (i + 1) * block] for i in range(CAP)]
        third = across(move_in(blocks, t, n_tensor, 1), n_dp)
        first = move_in(blocks, t, n_tensor, 0)

        def with_empty(first):
            sent = permute(pick(d ^ source_other, third), "tensor", n_tensor, width)
            return jnp.where((h == 0) & foreign, sent, first)

        first = lax.cond(any_empty, with_empty, lambda v: v, first)
        return jnp.where((h == 1) & foreign, pick(d ^ source_here, third), first)

    def collect(array):
        third = pick(d ^ out_index, across(array, n_dp))

        def with_empty(third):
            other = across(permute(array, "tensor", n_tensor, width), n_dp)
            return jnp.where(out_place == 0, pick(d ^ out_index, other), third)

        third = lax.cond(any_empty, with_empty, lambda v: v, third)
        third = jnp.where(counts[d] == CAP, third, 0)
        return move_out(jnp.where(foreign, 0, array), third, t, n_tensor)

    facts = jnp.stack([prefix, span_offset])
    facts_all = lax.all_gather(facts, "dp", axis=0, tiled=False)
    fact = jnp.where(foreign, facts_all[source_here][:, 2], jnp.where(h == 0, facts[:, 0], facts[:, 1]))
    prefix_len, span_start = fact[0], fact[1]

    position = ((q ^ jnp.arange(width))[:, None] * rows + jnp.arange(rows)[None, :]).reshape(LEN)
    placed = jnp.where(position < prefix_len, position, span_start + position - prefix_len).astype(f32)
    frequency = theta_base ** (-(jnp.arange(HD // 2).astype(f32) * 2.0 / HD))
    angles = placed[:, None] * frequency[None, :]
    cos_table, sin_table = jnp.cos(angles)[:, None, :], jnp.sin(angles)[:, None, :]
    allowed = (position[None, :] < prefix_len) | (position[None, :] <= position[:, None])

    def fetch(weight, axis):
        part = weight.shape[axis] // n_dp
        share = lax.dynamic_slice_in_dim(weight, d * part, part, axis)
        share = permute(share, "tensor", n_tensor, width)
        for bit in reversed(bits_of(n_dp)):
            got = permute(share, "dp", n_dp, bit)
            mine_first = (d & bit) == 0
            share = jnp.concatenate(
                [jnp.where(mine_first, share, got), jnp.where(mine_first, got, share)], axis
            )
        count = len(bits_of(n_dp))
        shaped = share.reshape(share.shape[:axis] + (2,) * count + (part,) + share.shape[axis + 1 :])
        order = (
            list(range(axis))
            + list(reversed(range(axis, axis + count)))
            + list(range(axis + count, shaped.ndim))
        )
        return shaped.transpose(order).reshape(weight.shape)

    def pair(weight, axis, cut):
        return jnp.stack([weight, fetch(weight, cut)], axis)

    width_qkv = w_qkv.shape[2]
    heads = width_qkv // HD
    width_ffn = w_gu.shape[2]

    wq = pair(w_qkv, 2, 0)
    wo = pair(w_out, 0, 1)
    wg = pair(w_gu, 2, 0)
    wd = pair(w_down, 0, 1)
    bq = jnp.stack([b_qkv, permute(b_qkv, "tensor", n_tensor, width)], 1)
    bg = jnp.stack([b_gu, permute(b_gu, "tensor", n_tensor, width)], 1)
    slices = jnp.stack([t, t ^ width])
    live_columns = slices[:, None] * width_ffn + jnp.arange(width_ffn)[None, :] < FF

    def parts_of(array):
        return [array[o * rows : (o + 1) * rows] for o in range(width)]

    own_tokens = spread(tokens)
    own_cotangent = spread(cotangent)
    tokens_all = jnp.concatenate(group.gather(own_tokens), 0)

    linear = jnp.einsum("td,dcpn->tcpn", tokens_all, wq, preferred_element_type=f32) + bq
    linear = linear.reshape(LEN, 3, 2 * heads, HD)
    queries = rotate(linear[:, 0], cos_table, sin_table).astype(bf16)
    keys_rot = rotate(linear[:, 1], cos_table, sin_table).astype(bf16)
    values_in = linear[:, 2].astype(bf16)
    context, log_total = attend(queries, keys_rot, values_in, allowed)
    context_rows = context.reshape(LEN, 2, width_qkv)
    partial_out = jnp.einsum("tpn,pnd->td", context_rows, wo, preferred_element_type=f32).astype(bf16)
    attended = group.scatter(parts_of(partial_out)) + b_out
    first_sum = deep_alpha * own_tokens.astype(f32) + attended
    hidden_one, normed_one, inv_one = norm_forward(first_sum, gain_one, shift_one)
    hidden_all = jnp.concatenate(group.gather(hidden_one.astype(bf16)), 0)

    def activate(gate_up):
        return jnp.where(
            live_columns, jax.nn.gelu(gate_up[:, 0], approximate=True) * gate_up[:, 1], 0.0
        )

    gate_up = jnp.einsum("td,dcpn->tcpn", hidden_all, wg, preferred_element_type=f32) + bg
    activated, pull_act = jax.vjp(activate, gate_up)
    inner_low = activated.astype(bf16)
    partial_fed = jnp.einsum("tpn,pnd->td", inner_low, wd, preferred_element_type=f32).astype(bf16)
    fed = group.scatter(parts_of(partial_fed)) + b_down
    second_sum = deep_alpha * hidden_one + fed
    layer_rows, normed_two, inv_two = norm_forward(second_sum, gain_two, shift_two)
    layer_out = collect(layer_rows.astype(bf16)).astype(f32)

    grad_layer = own_cotangent.astype(f32)
    grad_second, grad_gain_two, grad_shift_two = norm_backward(
        grad_layer, normed_two, inv_two, gain_two
    )
    grad_fed_all = jnp.concatenate(group.gather(grad_second.astype(bf16)), 0)
    grad_inner = jnp.einsum("td,pnd->tpn", grad_fed_all, wd, preferred_element_type=f32)
    grad_gate_up = pull_act(grad_inner)[0].astype(bf16)
    partial_hidden = jnp.einsum(
        "tcpn,dcpn->td", grad_gate_up, wg, preferred_element_type=f32
    ).astype(bf16)
    grad_w_down = jnp.einsum("tpn,td->pnd", inner_low, grad_fed_all, preferred_element_type=f32)
    grad_b_gu = jnp.sum(grad_gate_up.astype(f32), 0)
    grad_w_gu = jnp.einsum("td,tcpn->pdcn", hidden_all, grad_gate_up, preferred_element_type=f32)
    grad_hidden = group.scatter(parts_of(partial_hidden)) + deep_alpha * grad_second
    grad_first, grad_gain_one, grad_shift_one = norm_backward(
        grad_hidden, normed_one, inv_one, gain_one
    )
    grad_att_all = jnp.concatenate(group.gather(grad_first.astype(bf16)), 0)
    grad_context = jnp.einsum("td,pnd->tpn", grad_att_all, wo, preferred_element_type=f32)
    grad_context = grad_context.astype(bf16).reshape(LEN, 2 * heads, HD)
    grad_w_out = jnp.einsum("tpn,td->pnd", context_rows, grad_att_all, preferred_element_type=f32)
    grad_query, grad_keys, grad_values = attend_back(
        queries, keys_rot, values_in, log_total, grad_context, allowed
    )
    grad_linear = jnp.stack(
        [
            rotate(grad_query, cos_table, -sin_table),
            rotate(grad_keys, cos_table, -sin_table),
            grad_values,
        ],
        1,
    )
    grad_linear = grad_linear.reshape(LEN, 3, 2, width_qkv).astype(bf16)
    partial_in = jnp.einsum("tcpn,dcpn->td", grad_linear, wq, preferred_element_type=f32).astype(bf16)
    grad_b_qkv = jnp.sum(grad_linear.astype(f32), 0)
    grad_w_qkv = jnp.einsum("td,tcpn->pdcn", tokens_all, grad_linear, preferred_element_type=f32)
    input_rows = group.scatter(parts_of(partial_in)) + deep_alpha * grad_first
    input_grad = collect(input_rows.astype(bf16)).astype(f32)

    def reduce_weight(grads, axis):
        value = grads.astype(bf16)
        for bit in bits_of(n_dp):
            part = value.shape[axis + 1] // 2
            upper = ((d & bit) != 0).astype(jnp.int32)
            send = lax.dynamic_slice_in_dim(value, (1 - upper) * part, part, axis + 1)
            keep = lax.dynamic_slice_in_dim(value, upper * part, part, axis + 1)
            value = (keep.astype(f32) + permute(send, "dp", n_dp, bit).astype(f32)).astype(bf16)
        value = (
            value[0].astype(f32) + permute(value[1], "tensor", n_tensor, width).astype(f32)
        ).astype(bf16)
        for bit in reversed(bits_of(n_dp)):
            got = permute(value, "dp", n_dp, bit)
            mine_first = (d & bit) == 0
            value = jnp.concatenate(
                [jnp.where(mine_first, value, got), jnp.where(mine_first, got, value)], axis
            )
        return value.astype(f32)

    def reduce_small(everywhere, own, other):
        for bit in bits_of(n_dp):
            everywhere, own, other = jax.tree.map(
                lambda v: v + permute(v, "dp", n_dp, bit), (everywhere, own, other)
            )
        own = own + permute(other, "tensor", n_tensor, width)
        for bit in bits_of(n_tensor):
            everywhere = everywhere + permute(everywhere, "tensor", n_tensor, bit)
        return everywhere, own

    norm_grads = jnp.stack(
        [
            grad_gain_one,
            grad_shift_one,
            jnp.sum(grad_first, 0),
            grad_gain_two,
            grad_shift_two,
            jnp.sum(grad_second, 0),
        ]
    )
    bias = [
        jnp.concatenate([grad_b_qkv[:, p].reshape(-1), grad_b_gu[:, p].reshape(-1)]) for p in range(2)
    ]
    norm_grads, bias = reduce_small(norm_grads, bias[0], bias[1])
    grad_b_qkv = bias[: 3 * width_qkv].reshape(3, width_qkv)
    grad_b_gu = bias[3 * width_qkv :].reshape(2, width_ffn)
    return (
        layer_out,
        input_grad,
        reduce_weight(grad_w_qkv, 0),
        grad_b_qkv,
        reduce_weight(grad_w_out, 1),
        norm_grads[2],
        norm_grads[0],
        norm_grads[1],
        reduce_weight(grad_w_gu, 0),
        grad_b_gu,
        reduce_weight(grad_w_down, 1),
        norm_grads[5],
        norm_grads[3],
        norm_grads[4],
    )


def solution(mesh):
    rows = P(("dp", "tensor"), None)
    weights = (P(None, None, "tensor"), P(None, "tensor"), P("tensor", None), P(), P(), P())
    placed_ffn = (P(None, None, "tensor"), P(None, "tensor"), P("tensor", None), P(), P(), P())
    placed = (rows, rows) + weights + placed_ffn + (P("dp"), P("dp"), P())
    n_dp, n_tensor = mesh.shape["dp"], mesh.shape["tensor"]

    def body(*arguments):
        return on_device(n_dp, n_tensor, *arguments)

    return jax.shard_map(
        body,
        mesh=mesh,
        in_specs=placed,
        out_specs=(rows, rows) + weights + placed_ffn,
        check_vma=False,
    )
```

time: 2330 us -> 1280 us (0.55)
  waiting for transfers between devices: 1600 us -> 464 us
  starting transfers between devices: 0.58 us -> 146 us
  matrix products: 300 us -> 165 us
  other arithmetic: 111 us -> 175 us
  blocking collectives: 51.3 us -> 5.07 us
  local copies, waits for them, and re-layouts: 220 us -> 262 us
  between operations: 14.7 us -> 51.5 us
  loops' own time: 25.2 us -> 0.38 us
    reduce_scatter x4 -> x0, waiting for transfers between devices: 789 us -> none  [the longest x1 207 us: on_device(): lax.psum_scatter(jnp.einsum('tcn,dcn->td', grad_gate_up, w_gu, preferred_...]
    all_gather x4 -> x0, waiting for transfers between devices: 657 us -> none  [the longest x1 174 us: on_device(): lax.all_gather(grad_second.astype(jnp.bfloat16), 'tensor', axis=0, tiled=...]
    ppermute x0 -> x108, waiting for transfers between devices: none -> 464 us  [the longest x88 460 us: permute(): return lax.ppermute(value, axis, [(i, i ^ bit) for i in range(size)])]
    psum x1 -> x0, waiting for transfers between devices: 148 us -> none  [on_device(): lax.psum(grad_w_qkv.astype(jnp.bfloat16), 'dp').astype(jnp.float32)]
    ppermute x0 -> x108, starting transfers between devices: none -> 146 us  [the longest x88 102 us: permute(): return lax.ppermute(value, axis, [(i, i ^ bit) for i in range(size)])]
    dot_general x54 -> x18, matrix products: 300 us -> 165 us  [the longest x1 18.8 us: on_device(): jnp.einsum('td,tcpn->pdcn', hidden_all, grad_gate_up, preferred_element_t...]
    dynamic_slice x24 -> x37, local copies, waits for them, and re-layouts: 17.2 us -> 72 us  [the longest x12 51 us: reduce_weight(): send = lax.dynamic_slice_in_dim(value, (1 - upper) * part, part, axis + 1)]
    psum x2 -> x0, blocking collectives: 51.3 us -> none  [the longest x1 44.6 us: on_device(): lax.psum((grad_gain_one, grad_shift_one, jnp.sum(grad_first, 0), grad_gai...]
  transfers between devices with their start and end apart: 9 -> 108, of which waited for: 9 -> 36; matrix products, arithmetic and copies ran while one was open for 5% -> 43% of each run, Pallas kernels for 0% -> 0%
where the time goes in v1:
time: 1280 us; the launch traced here: 1270 us
  waiting for transfers between devices  464 us (36%)
  local copies, waits for them, and re-layouts  262 us (20%)
  other arithmetic  175 us (14%)
  matrix products  165 us (13%)
  starting transfers between devices  146 us (11%)
  between operations  51.5 us (4%)
    ppermute x88, waiting for transfers between devices, permute(): return lax.ppermute(value, axis, [(i, i ^ bit) for i in range(size)])  460 us
    ppermute x88, starting transfers between devices, permute(): return lax.ppermute(value, axis, [(i, i ^ bit) for i in range(size)])  102 us
    unnamed x301, local copies, waits for them, and re-layouts  77.4 us
    dynamic_slice x12, local copies, waits for them, and re-layouts, reduce_weight(): send = lax.dynamic_slice_in_dim(value, (1 - upper) * part, part, axis + 1)  51 us
    reshape x7, local copies, waits for them, and re-layouts, fetch(): share.reshape(share.shape[:axis] + (2,) * count + (part,) + share.shape[a...  39.4 us
  transfers between devices with their start and end apart: 108, of which 36 were waited for; matrix products, arithmetic and copies ran while one was open for 43% of the time, Pallas kernels for 0%

profile of v1, /device:TPU:10, one launch (start us, length us, event | category | flops | bytes accessed | tf_op | source)
XLA Modules:
  0.0 1268.5 jit_solution(2310679853595267801)
XLA Ops:
  83.6 10.4 collective-permute-done.27
  179.9 16.7 %collective-permute-done.19 = bf16[256,2048]{1,0:T(8,128)(2,1)} collective-permute-done((bf16[256,2048]{1,0:T(8,128)(2,1)}, bf16[256,2048]{1,0:T(8,128)(2,1)}, u32[]{:S(2)}, u32[]{:S(2)}) %collective-permute-start.19) | collective-permute-done | bytes 1048608 | tf_op jit(solution)/shard_map/ppermute | solution.py:26
  203.1 18.6 %collective-permute-done.20 = bf16[128,2048]{1,0:T(8,128)(2,1)S(1)} collective-permute-done((bf16[128,2048]{1,0:T(8,128)(2,1)S(1)}, bf16[128,2048]{1,0:T(8,128)(2,1)S(1)}, u32[]{:S(2)}, u32[]{:S(2)}) %collective-permute-start.20) | collective-permute-done | bytes 524320 | tf_op jit(solution)/shard_map/ppermute | solution.py:26
  226.5 9.0 broadcast_add_fusion.1
  250.6 8.7 fusion.91
  259.3 8.0 fusion
  267.3 9.6 fusion.46
  284.6 7.9 collective-permute-done.29
  296.7 18.2 %collective-permute-done.38 = bf16[512,2,684]{0,1,2:T(2,128)(2,1)S(1)} collective-permute-done((bf16[512,2,684]{0,1,2:T(2,128)(2,1)}, bf16[512,2,684]{0,1,2:T(2,128)(2,1)S(1)}, u32[]{:S(2)}, u32[]{:S(2)}) %collective-permute-start.38) | collective-permute-done | bytes 1400864 | tf_op jit(solution)/shard_map/ppermute | solution.py:26
  375.1 11.0 copy.203
  408.6 15.8 %broadcast_add_fusion = f32[1024,2,2,684]{0,3,2,1:T(8,128)S(1)} fusion(f32[2,2,684]{2,1,0:T(2,128)S(1)} %copy.205, bf16[2048,2,1,684]{0,3,2,1:T(8,128)(2,1)S(1)} %bitcast.281, bf16[2048,2,1,684]{0,3,2,1:T(8,128)(2,1)} %bitcast.276, bf16[1024,2048]{1,0:T(8,128)(2,1)} %constant_dynamic-update-slice_fusion.5), kind=kOutput, calls=%fused_computation.53 | convolution fusion | flops 11500830720 | bytes 26618560 | tf_op jit(solution)/shard_map/td,dcpn->tcpn/dot_general | solution.py:366
  453.2 21.3 %collective-permute-done.46 = bf16[128,2048]{1,0:T(8,128)(2,1)S(1)} collective-permute-done((bf16[128,2048]{1,0:T(8,128)(2,1)S(1)}, bf16[128,2048]{1,0:T(8,128)(2,1)S(1)}, u32[]{:S(2)}, u32[]{:S(2)}) %collective-permute-start.46) | collective-permute-done | bytes 524320 | tf_op jit(solution)/shard_map/ppermute | solution.py:26
  480.6 22.3 %collective-permute-done.47 = bf16[256,2048]{1,0:T(8,128)(2,1)} collective-permute-done((bf16[256,2048]{1,0:T(8,128)(2,1)}, bf16[256,2048]{1,0:T(8,128)(2,1)}, u32[]{:S(2)}, u32[]{:S(2)}) %collective-permute-start.47) | collective-permute-done | bytes 1048608 | tf_op jit(solution)/shard_map/ppermute | solution.py:26
  555.3 16.0 %collective-permute-done.65 = bf16[256,2048]{1,0:T(8,128)(2,1)S(1)} collective-permute-done((bf16[256,2048]{1,0:T(8,128)(2,1)}, bf16[256,2048]{1,0:T(8,128)(2,1)S(1)}, u32[]{:S(2)}, u32[]{:S(2)}) %collective-permute-start.65) | collective-permute-done | bytes 1048608 | tf_op jit(solution)/shard_map/ppermute | solution.py:26
  591.1 16.8 %multiply_bitcast_fusion = (f32[1024,1,2,684]{0,3,2,1:T(8,128)}, f32[1024,1,2,684]{0,3,2,1:T(8,128)}) fusion(pred[2,684]{1,0:T(4,128)(4,1)S(1)} %copy-done.92, f32[1024,2,2,684]{0,3,2,1:T(8,128)} %copy-done, bf16[1,684,2048]{2,1,0:T(8,128)(2,1)S(1)} %copy-done.56, bf16[1,684,2048]{2,1,0:T(8,128)(2,1)} %bitcast.304, ...), kind=kOutput, calls=%fused_computation.51 | convolution fusion | flops 5781233664 | bytes 32212312 | tf_op jit(solution)/shard_map/td,pnd->tpn/dot_general | solution.py:380
  607.9 18.3 %bitcast_convert_fusion.1 = bf16[1024,2048]{1,0:T(8,128)(2,1)} fusion(bf16[2048,2,1,684]{0,3,2,1:T(8,128)(2,1)} %bitcast.280, bf16[2048,2,1,684]{0,3,2,1:T(8,128)(2,1)S(1)} %bitcast.279, f32[1024,1,2,684]{0,3,2,1:T(8,128)} %get-tuple-element.207, f32[1024,1,2,684]{0,3,2,1:T(8,128)} %get-tuple-element.206), kind=kOutput, calls=%fused_computation.21 | convolution fusion | flops 11488919552 | bytes 26607616 | tf_op jit(solution)/shard_map/tcpn,dcpn->td/dot_general | solution.py:382
  626.2 18.8 %convolution_convert_fusion = bf16[2,2,684,2048]{3,2,1,0:T(8,128)(2,1)} fusion(bf16[1024,2048]{1,0:T(8,128)(2,1)S(1)} %copy-done.25, f32[1024,1,2,684]{0,3,2,1:T(8,128)} %get-tuple-element.207, f32[1024,1,2,684]{0,3,2,1:T(8,128)} %get-tuple-element.206), kind=kOutput, calls=%fused_computation.30 | convolution fusion | flops 11486822400 | bytes 26607616 | tf_op jit(solution)/shard_map/td,tcpn->pdcn/dot_general | solution.py:387
  647.5 9.9 convolution_convert_fusion.2
  679.9 24.5 %copy.224 = bf16[2,1024,2,684]{1,2,3,0:T(2,128)(2,1)} copy(bf16[2,1024,2,684]{1,3,0,2:T(8,128)(2,1)} %dynamic-slice_bitcast_fusion) | data formatting | bytes 11206656 | tf_op jit(solution)/shard_map/dynamic_slice | solution.py:419
  722.1 7.8 collective-permute-done.103
  740.8 21.2 %collective-permute-done.106 = f32[6,2048]{1,0:T(8,128)S(1)} collective-permute-done((f32[6,2048]{1,0:T(8,128)S(1)}, f32[6,2048]{1,0:T(8,128)S(1)}, u32[]{:S(2)}, u32[]{:S(2)}) %collective-permute-start.106) | collective-permute-done | bytes 49184 | tf_op jit(solution)/shard_map/ppermute | solution.py:26
  762.0 17.1 %collective-permute-start.107 = (f32[6,2048]{1,0:T(8,128)S(1)}, f32[6,2048]{1,0:T(8,128)S(1)}, u32[]{:S(2)}, u32[]{:S(2)}) collective-permute-start(f32[6,2048]{1,0:T(8,128)S(1)} %add.441), channel_id=1, source_target_pairs={{0,4},{1,5},{2,6},{3,7},{4,0},{5,1},{6,2},{7,3},{8,12},{9,13},{10,... | collective-permute-start | bytes 147464 | tf_op jit(solution)/shard_map/ppermute | solution.py:26
  803.1 13.1 %multiply_reduce_fusion = (f32[4,1024]{1,0:T(4,128)S(1)}, f32[4,1024,1024]{1,2,0:T(8,128)}) fusion(f32[4,1024,1024]{1,2,0:T(8,128)} %get-tuple-element.323, f32[4,1024]{1,0:T(4,128)} %log_add_fusion, bf16[1024,4,128]{0,2,1:T(8,128)(2,1)S(1)} %bitcast.303, f32[1024,3,4,128]{0,3,2,1:T(8,128)} %bitcast.289), kind=kOutput, calls=%fused_computation.7 | convolution fusion | flops 1086320640 | bytes 35684352 | tf_op jit(solution)/shard_map/qhe,khe->hqk/dot_general | solution.py:209
  816.3 12.3 multiply_convert_fusion
  852.0 9.5 bitcast_convert_fusion
  883.6 9.0 convolution_convert_fusion.1
  924.4 18.8 %collective-permute-done.115 = bf16[684,512]{1,0:T(8,128)(2,1)} collective-permute-done((bf16[684,512]{1,0:T(8,128)(2,1)}, bf16[684,512]{1,0:T(8,128)(2,1)}, u32[]{:S(2)}, u32[]{:S(2)}) %collective-permute-start.115) | collective-permute-done | bytes 700448 | tf_op jit(solution)/shard_map/ppermute | solution.py:26
  975.0 90.2 %collective-permute-done.101 = bf16[256,512]{1,0:T(8,128)(2,1)S(1)} collective-permute-done((bf16[256,512]{1,0:T(8,128)(2,1)S(1)}, bf16[256,512]{1,0:T(8,128)(2,1)S(1)}, u32[]{:S(2)}, u32[]{:S(2)}) %collective-permute-start.101) | collective-permute-done | bytes 262176 | tf_op jit(solution)/shard_map/ppermute | solution.py:26
  1082.2 89.2 %collective-permute-done.90 = bf16[512,3,256]{0,2,1:T(8,128)(2,1)S(1)} collective-permute-done((bf16[512,3,256]{0,2,1:T(8,128)(2,1)S(1)}, bf16[512,3,256]{0,2,1:T(8,128)(2,1)S(1)}, u32[]{:S(2)}, u32[]{:S(2)}) %collective-permute-start.90) | collective-permute-done | bytes 786464 | tf_op jit(solution)/shard_map/ppermute | solution.py:26
  1182.8 9.4 collective-permute-done.91
  1193.0 27.7 %collective-permute-done.111 = bf16[512,2,684]{0,1,2:T(2,128)(2,1)S(1)} collective-permute-done((bf16[512,2,684]{0,1,2:T(2,128)(2,1)S(1)}, bf16[512,2,684]{0,1,2:T(2,128)(2,1)S(1)}, u32[]{:S(2)}, u32[]{:S(2)}) %collective-permute-start.111) | collective-permute-done | bytes 1400864 | tf_op jit(solution)/shard_map/ppermute | solution.py:26
  1253.6 14.7 %copy.241 = f32[2048,2,684]{0,1,2:T(2,128)} copy(f32[2048,2,684]{0,2,1:T(8,128)S(1)} %maximum_convert_fusion) | data formatting | bytes 22413312
  (758 shorter events, 595.0 us)
Async XLA Ops:
  7.6 92.5 %collective-permute-start.22 = (bf16[512,3,256]{0,2,1:T(8,128)(2,1)}, bf16[512,3,256]{0,2,1:T(8,128)(2,1)}, u32[]{:S(2)}, u32[]{:S(2)}) collective-permute-start(bf16[512,3,256]{0,2,1:T(8,128)(2,1)} %constant_dynamic-slice_fusion.10), channel_id=1, source_target_pairs={{0,4},{1,5},{2,6},{3,7},{4,0},{5,1},{6,2},{7,3},{8,12},{9,13},{10,... | collective-permute-start | bytes 2359304 | tf_op jit(solution)/shard_map/ppermute | solution.py:26
  17.2 87.0 %collective-permute-start.15 = (bf16[128,2048]{1,0:T(8,128)(2,1)}, bf16[128,2048]{1,0:T(8,128)(2,1)}, u32[]{:S(2)}, u32[]{:S(2)}) collective-permute-start(bf16[128,2048]{1,0:T(8,128)(2,1)} %get-tuple-element.274), channel_id=1, source_target_pairs={{2,4},{3,5},{4,7},{10,12},{11,13},{12,15},{18,20},{19,21},{20,23},... | collective-permute-start | bytes 1572872 | tf_op jit(solution)/shard_map/ppermute | solution.py:149
  19.3 85.0 %collective-permute-start.16 = (bf16[128,2048]{1,0:T(8,128)(2,1)}, bf16[128,2048]{1,0:T(8,128)(2,1)}, u32[]{:S(2)}, u32[]{:S(2)}) collective-permute-start(bf16[128,2048]{1,0:T(8,128)(2,1)} %get-tuple-element.275), channel_id=1, source_target_pairs={{1,2},{2,3},{3,5},{4,6},{9,10},{10,11},{11,13},{12,14},{17,18},{18... | collective-permute-start | bytes 1572872 | tf_op jit(solution)/shard_map/ppermute | solution.py:149
  104.2 175.5 %collective-permute-start.40 = (f32[2,684]{1,0:T(2,128)S(1)}, f32[2,684]{1,0:T(2,128)S(1)}, u32[]{:S(2)}, u32[]{:S(2)}) collective-permute-start(f32[2,684]{1,0:T(2,128)S(1)} %copy-done.96), channel_id=1, source_target_pairs={{0,4},{1,5},{2,6},{3,7},{4,0},{5,1},{6,2},{7,3},{8,12},{9,13},{10,... | collective-permute-start | bytes 16424 | tf_op jit(solution)/shard_map/ppermute | solution.py:26
  139.5 141.5 %collective-permute-start.37 = (bf16[512,2,684]{0,1,2:T(2,128)(2,1)}, bf16[512,2,684]{0,1,2:T(2,128)(2,1)}, u32[]{:S(2)}, u32[]{:S(2)}) collective-permute-start(bf16[512,2,684]{0,1,2:T(2,128)(2,1)} %constant_dynamic-slice_fusion.7), channel_id=1, source_target_pairs={{0,4},{1,5},{2,6},{3,7},{4,0},{5,1},{6,2},{7,3},{8,12},{9,13},{10,... | collective-permute-start | bytes 4202504 | tf_op jit(solution)/shard_map/ppermute | solution.py:26
  139.8 56.7 %collective-permute-start.19 = (bf16[256,2048]{1,0:T(8,128)(2,1)}, bf16[256,2048]{1,0:T(8,128)(2,1)}, u32[]{:S(2)}, u32[]{:S(2)}) collective-permute-start(bf16[256,2048]{1,0:T(8,128)(2,1)} %get-tuple-element.205), channel_id=1, source_target_pairs={{0,2},{1,3},{2,0},{3,1},{4,6},{5,7},{6,4},{7,5},{8,10},{9,11},{10,... | collective-permute-start | bytes 3145736 | tf_op jit(solution)/shard_map/ppermute | solution.py:26
  153.3 130.7 %collective-permute-start.41 = (bf16[684,512]{1,0:T(8,128)(2,1)}, bf16[684,512]{1,0:T(8,128)(2,1)}, u32[]{:S(2)}, u32[]{:S(2)}) collective-permute-start(bf16[684,512]{1,0:T(8,128)(2,1)} %constant_dynamic-slice_fusion.6), channel_id=1, source_target_pairs={{0,4},{1,5},{2,6},{3,7},{4,0},{5,1},{6,2},{7,3},{8,12},{9,13},{10,... | collective-permute-start | bytes 2101256 | tf_op jit(solution)/shard_map/ppermute | solution.py:26
  157.9 63.7 %collective-permute-start.20 = (bf16[128,2048]{1,0:T(8,128)(2,1)S(1)}, bf16[128,2048]{1,0:T(8,128)(2,1)S(1)}, u32[]{:S(2)}, u32[]{:S(2)}) collective-permute-start(bf16[128,2048]{1,0:T(8,128)(2,1)S(1)} %slice.391), channel_id=1, source_target_pairs={{0,2},{1,3},{2,0},{3,1},{4,6},{5,7},{6,4},{7,5},{8,10},{9,11},{10,... | collective-permute-start | bytes 1572872 | tf_op jit(solution)/shard_map/ppermute | solution.py:26
  221.6 58.2 %collective-permute-start.56 = (bf16[128,2048]{1,0:T(8,128)(2,1)}, bf16[128,2048]{1,0:T(8,128)(2,1)}, u32[]{:S(2)}, u32[]{:S(2)}) collective-permute-start(bf16[128,2048]{1,0:T(8,128)(2,1)} %get-tuple-element.271), channel_id=1, source_target_pairs={{5,4},{6,5},{13,12},{14,13},{21,20},{22,21},{29,28},{30,29}} | collective-permute-start | bytes 1572872 | tf_op jit(solution)/shard_map/ppermute | solution.py:149
  224.2 58.5 %collective-permute-start.57 = (bf16[128,2048]{1,0:T(8,128)(2,1)}, bf16[128,2048]{1,0:T(8,128)(2,1)}, u32[]{:S(2)}, u32[]{:S(2)}) collective-permute-start(bf16[128,2048]{1,0:T(8,128)(2,1)} %get-tuple-element.268), channel_id=1, source_target_pairs={{5,4},{6,5},{7,6},{13,12},{14,13},{15,14},{21,20},{22,21},{23,22},... | collective-permute-start | bytes 1572872 | tf_op jit(solution)/shard_map/ppermute | solution.py:149
  323.8 125.8 %collective-permute-start.58 = (bf16[256,2048]{1,0:T(8,128)(2,1)}, bf16[256,2048]{1,0:T(8,128)(2,1)}, u32[]{:S(2)}, u32[]{:S(2)}) collective-permute-start(bf16[256,2048]{1,0:T(8,128)(2,1)} %pad_maximum_fusion.37), channel_id=1, source_target_pairs={{0,16},{8,24},{16,0},{24,8},{1,17},{9,25},{17,1},{25,9},{2,18},{10... | collective-permute-start | bytes 3145736 | tf_op jit(solution)/shard_map/ppermute | solution.py:26
  335.8 57.1 %collective-permute-start.34 = (bf16[256,2048]{1,0:T(8,128)(2,1)}, bf16[256,2048]{1,0:T(8,128)(2,1)}, u32[]{:S(2)}, u32[]{:S(2)}) collective-permute-start(bf16[256,2048]{1,0:T(8,128)(2,1)} %get-tuple-element.201), channel_id=1, source_target_pairs={{0,2},{1,3},{2,0},{3,1},{4,6},{5,7},{6,4},{7,5},{8,10},{9,11},{10,... | collective-permute-start | bytes 3145736 | tf_op jit(solution)/shard_map/ppermute | solution.py:26
  551.2 106.2 %collective-permute-start.50 = (bf16[256,2048]{1,0:T(8,128)(2,1)S(1)}, bf16[256,2048]{1,0:T(8,128)(2,1)}, u32[]{:S(2)}, u32[]{:S(2)}) collective-permute-start(bf16[256,2048]{1,0:T(8,128)(2,1)S(1)} %get-tuple-element.197), channel_id=1, source_target_pairs={{0,8},{8,0},{16,24},{24,16},{1,9},{9,1},{17,25},{25,17},{2,10},{10... | collective-permute-start | bytes 3145736 | tf_op jit(solution)/shard_map/ppermute | solution.py:26
  554.0 165.8 %collective-permute-start.53 = (bf16[128,2048]{1,0:T(8,128)(2,1)}, bf16[128,2048]{1,0:T(8,128)(2,1)}, u32[]{:S(2)}, u32[]{:S(2)}) collective-permute-start(bf16[128,2048]{1,0:T(8,128)(2,1)} %get-tuple-element.294), channel_id=1, source_target_pairs={{4,2},{5,3},{7,4},{12,10},{13,11},{15,12},{20,18},{21,19},{23,20},... | collective-permute-start | bytes 1572872 | tf_op jit(solution)/shard_map/ppermute | solution.py:181
  582.5 137.4 %collective-permute-start.54 = (bf16[128,2048]{1,0:T(8,128)(2,1)}, bf16[128,2048]{1,0:T(8,128)(2,1)}, u32[]{:S(2)}, u32[]{:S(2)}) collective-permute-start(bf16[128,2048]{1,0:T(8,128)(2,1)} %get-tuple-element.295), channel_id=1, source_target_pairs={{2,1},{3,2},{5,3},{6,4},{10,9},{11,10},{13,11},{14,12},{18,17},{19... | collective-permute-start | bytes 1572872 | tf_op jit(solution)/shard_map/ppermute | solution.py:181
  585.3 135.1 %collective-permute-start.55 = (bf16[128,2048]{1,0:T(8,128)(2,1)}, bf16[128,2048]{1,0:T(8,128)(2,1)}, u32[]{:S(2)}, u32[]{:S(2)}) collective-permute-start(bf16[128,2048]{1,0:T(8,128)(2,1)} %get-tuple-element.293), channel_id=1, source_target_pairs={{1,0},{2,1},{3,2},{4,3},{6,4},{7,5},{9,8},{10,9},{11,10},{12,11},{... | collective-permute-start | bytes 1572872 | tf_op jit(solution)/shard_map/ppermute | solution.py:181
  590.1 67.3 %collective-permute-start.49 = (bf16[256,2048]{1,0:T(8,128)(2,1)}, bf16[256,2048]{1,0:T(8,128)(2,1)}, u32[]{:S(2)}, u32[]{:S(2)}) collective-permute-start(bf16[256,2048]{1,0:T(8,128)(2,1)} %collective-permute-done.48), channel_id=1, source_target_pairs={{0,8},{8,0},{16,24},{24,16},{1,9},{9,1},{17,25},{25,17},{2,10},{10... | collective-permute-start | bytes 3145736 | tf_op jit(solution)/shard_map/ppermute | solution.py:26
  719.8 228.0 %collective-permute-start.108 = (bf16[2,1024,2,684]{1,2,3,0:T(2,128)(2,1)}, bf16[2,1024,2,684]{1,2,3,0:T(2,128)(2,1)}, u32[]{:S(2)}, u32[]{:S(2)}) collective-permute-start(bf16[2,1024,2,684]{1,2,3,0:T(2,128)(2,1)} %copy.224), channel_id=1, source_target_pairs={{0,8},{8,0},{16,24},{24,16},{1,9},{9,1},{17,25},{25,17},{2,10},{10... | collective-permute-start | bytes 16809992 | tf_op jit(solution)/shard_map/ppermute | solution.py:26
  719.9 66.0 %collective-permute-start.113 = (bf16[2,684,1024]{2,0,1:T(2,128)(2,1)}, bf16[2,684,1024]{2,0,1:T(2,128)(2,1)S(1)}, u32[]{:S(2)}, u32[]{:S(2)}) collective-permute-start(bf16[2,684,1024]{2,0,1:T(2,128)(2,1)} %copy.236), channel_id=1, source_target_pairs={{0,8},{8,0},{16,24},{24,16},{1,9},{9,1},{17,25},{25,17},{2,10},{10... | collective-permute-start | bytes 8405000 | tf_op jit(solution)/shard_map/ppermute | solution.py:26
  790.0 107.6 %collective-permute-start.114 = (bf16[2,684,512]{2,0,1:T(2,128)(2,1)}, bf16[2,684,512]{2,0,1:T(2,128)(2,1)}, u32[]{:S(2)}, u32[]{:S(2)}) collective-permute-start(bf16[2,684,512]{2,0,1:T(2,128)(2,1)} %copy.238), channel_id=1, source_target_pairs={{0,16},{8,24},{16,0},{24,8},{1,17},{9,25},{17,1},{25,9},{2,18},{10... | collective-permute-start | bytes 4202504 | tf_op jit(solution)/shard_map/ppermute | solution.py:26
  896.3 67.3 %collective-permute-start.88 = (bf16[2,1024,3,256]{1,3,0,2:T(8,128)(2,1)}, bf16[2,1024,3,256]{1,3,0,2:T(8,128)(2,1)}, u32[]{:S(2)}, u32[]{:S(2)}) collective-permute-start(bf16[2,1024,3,256]{1,3,0,2:T(8,128)(2,1)} %dynamic-slice_bitcast_fusion.1), channel_id=1, source_target_pairs={{0,8},{8,0},{16,24},{24,16},{1,9},{9,1},{17,25},{25,17},{2,10},{10... | collective-permute-start | bytes 9437192 | tf_op jit(solution)/shard_map/ppermute | solution.py:26
  923.1 47.3 %collective-permute-start.82 = (bf16[256,2048]{1,0:T(8,128)(2,1)}, bf16[256,2048]{1,0:T(8,128)(2,1)S(1)}, u32[]{:S(2)}, u32[]{:S(2)}) collective-permute-start(bf16[256,2048]{1,0:T(8,128)(2,1)} %get-tuple-element.189), channel_id=1, source_target_pairs={{0,8},{8,0},{16,24},{24,16},{1,9},{9,1},{17,25},{25,17},{2,10},{10... | collective-permute-start | bytes 3145736 | tf_op jit(solution)/shard_map/ppermute | solution.py:26
  947.8 120.6 %collective-permute-start.116 = (bf16[684,512]{1,0:T(8,128)(2,1)S(1)}, bf16[684,512]{1,0:T(8,128)(2,1)}, u32[]{:S(2)}, u32[]{:S(2)}) collective-permute-start(bf16[684,512]{1,0:T(8,128)(2,1)S(1)} %fusion.53), channel_id=1, source_target_pairs={{0,16},{8,24},{16,0},{24,8},{1,17},{9,25},{17,1},{25,9},{2,18},{10... | collective-permute-start | bytes 2101256 | tf_op jit(solution)/shard_map/ppermute | solution.py:26
  962.5 110.1 %collective-permute-start.109 = (bf16[2,512,2,684]{1,2,3,0:T(2,128)(2,1)}, bf16[2,512,2,684]{1,2,3,0:T(2,128)(2,1)}, u32[]{:S(2)}, u32[]{:S(2)}) collective-permute-start(bf16[2,512,2,684]{1,2,3,0:T(2,128)(2,1)} %copy.226), channel_id=1, source_target_pairs={{0,16},{8,24},{16,0},{24,8},{1,17},{9,25},{17,1},{25,9},{2,18},{10... | collective-permute-start | bytes 8405000 | tf_op jit(solution)/shard_map/ppermute | solution.py:26
  969.4 100.6 %collective-permute-start.89 = (bf16[2,512,3,256]{1,3,0,2:T(8,128)(2,1)}, bf16[2,512,3,256]{1,3,0,2:T(8,128)(2,1)}, u32[]{:S(2)}, u32[]{:S(2)}) collective-permute-start(bf16[2,512,3,256]{1,3,0,2:T(8,128)(2,1)} %constant_dynamic-slice_fusion.5), channel_id=1, source_target_pairs={{0,16},{8,24},{16,0},{24,8},{1,17},{9,25},{17,1},{25,9},{2,18},{10... | collective-permute-start | bytes 4718600 | tf_op jit(solution)/shard_map/ppermute | solution.py:26
  972.2 92.9 %collective-permute-start.101 = (bf16[256,512]{1,0:T(8,128)(2,1)S(1)}, bf16[256,512]{1,0:T(8,128)(2,1)S(1)}, u32[]{:S(2)}, u32[]{:S(2)}) collective-permute-start(bf16[256,512]{1,0:T(8,128)(2,1)S(1)} %fusion.55), channel_id=1, source_target_pairs={{0,16},{8,24},{16,0},{24,8},{1,17},{9,25},{17,1},{25,9},{2,18},{10... | collective-permute-start | bytes 786440 | tf_op jit(solution)/shard_map/ppermute | solution.py:26
  973.4 254.5 %collective-permute-start.85 = (bf16[128,2048]{1,0:T(8,128)(2,1)S(1)}, bf16[128,2048]{1,0:T(8,128)(2,1)S(1)}, u32[]{:S(2)}, u32[]{:S(2)}) collective-permute-start(bf16[128,2048]{1,0:T(8,128)(2,1)S(1)} %get-tuple-element.287), channel_id=1, source_target_pairs={{4,2},{5,3},{7,4},{12,10},{13,11},{15,12},{20,18},{21,19},{23,20},... | collective-permute-start | bytes 1572872 | tf_op jit(solution)/shard_map/ppermute | solution.py:181
  1065.2 163.0 %collective-permute-start.86 = (bf16[128,2048]{1,0:T(8,128)(2,1)S(1)}, bf16[128,2048]{1,0:T(8,128)(2,1)S(1)}, u32[]{:S(2)}, u32[]{:S(2)}) collective-permute-start(bf16[128,2048]{1,0:T(8,128)(2,1)S(1)} %get-tuple-element.288), channel_id=1, source_target_pairs={{2,1},{3,2},{5,3},{6,4},{10,9},{11,10},{13,11},{14,12},{18,17},{19... | collective-permute-start | bytes 1572872 | tf_op jit(solution)/shard_map/ppermute | solution.py:181
  1070.0 105.7 %collective-permute-start.117 = (bf16[684,1024]{1,0:T(8,128)(2,1)S(1)}, bf16[684,1024]{1,0:T(8,128)(2,1)S(1)}, u32[]{:S(2)}, u32[]{:S(2)}) collective-permute-start(bf16[684,1024]{1,0:T(8,128)(2,1)S(1)} %pad_maximum_fusion.25), channel_id=1, source_target_pairs={{0,8},{8,0},{16,24},{24,16},{1,9},{9,1},{17,25},{25,17},{2,10},{10... | collective-permute-start | bytes 4202504 | tf_op jit(solution)/shard_map/ppermute | solution.py:26
  1077.2 95.4 %collective-permute-start.110 = (bf16[512,2,684]{0,1,2:T(2,128)(2,1)S(1)}, bf16[512,2,684]{0,1,2:T(2,128)(2,1)S(1)}, u32[]{:S(2)}, u32[]{:S(2)}) collective-permute-start(bf16[512,2,684]{0,1,2:T(2,128)(2,1)S(1)} %copy.228), channel_id=1, source_target_pairs={{0,4},{1,5},{2,6},{3,7},{4,0},{5,1},{6,2},{7,3},{8,12},{9,13},{10,... | collective-permute-start | bytes 4202504 | tf_op jit(solution)/shard_map/ppermute | solution.py:26
  1077.4 94.1 %collective-permute-start.90 = (bf16[512,3,256]{0,2,1:T(8,128)(2,1)S(1)}, bf16[512,3,256]{0,2,1:T(8,128)(2,1)S(1)}, u32[]{:S(2)}, u32[]{:S(2)}) collective-permute-start(bf16[512,3,256]{0,2,1:T(8,128)(2,1)S(1)} %slice_bitcast_fusion.4), channel_id=1, source_target_pairs={{0,4},{1,5},{2,6},{3,7},{4,0},{5,1},{6,2},{7,3},{8,12},{9,13},{10,... | collective-permute-start | bytes 2359304 | tf_op jit(solution)/shard_map/ppermute | solution.py:26
  1175.7 53.0 %collective-permute-start.87 = (bf16[128,2048]{1,0:T(8,128)(2,1)S(1)}, bf16[128,2048]{1,0:T(8,128)(2,1)S(1)}, u32[]{:S(2)}, u32[]{:S(2)}) collective-permute-start(bf16[128,2048]{1,0:T(8,128)(2,1)S(1)} %get-tuple-element.286), channel_id=1, source_target_pairs={{1,0},{2,1},{3,2},{4,3},{6,4},{7,5},{9,8},{10,9},{11,10},{12,11},{... | collective-permute-start | bytes 1572872 | tf_op jit(solution)/shard_map/ppermute | solution.py:181
  (216 other events, 3399.0 us)

commit v2 on v1

v2 whole, which is shorter than its diff:
```python
import functools
import math

import jax
import jax.numpy as jnp
from jax import lax
from jax.experimental import pallas as pl
from jax.experimental.pallas import tpu as pltpu
from jax.sharding import PartitionSpec as P

HD = 128
FF = 5461
LEN = 1024
CAP = 3

deep_alpha = math.sqrt(48.0)
epsilon = 1e-05
negative = -1e30
theta_base = 10000.0
f32 = jnp.float32
bf16 = jnp.bfloat16


def bits_of(count):
    return [1 << b for b in range(count.bit_length() - 1)]


def permute(value, axis, size, bit):
    return lax.ppermute(value, axis, [(i, i ^ bit) for i in range(size)])


def top_bit(number):
    return 1 << (number.bit_length() - 1)


def low_bit(number):
    return number & -number


def popcount(number):
    return bin(number).count("1")


def partner(t, bit):
    return t + bit - 2 * bit * ((t // bit) % 2)


def step(ref, start, count):
    return ref.at[pl.ds(start, count)]


ROW_TILE = 16


def row_tiles(count, body):
    def run(i, carry):
        body(pl.multiple_of(i * ROW_TILE, ROW_TILE))
        return carry

    lax.fori_loop(0, count // ROW_TILE, run, 0)


class Ship:
    def __init__(self, n_dp, n_tensor, send, recv, local):
        self.n_dp, self.n_tensor = n_dp, n_tensor
        self.width = n_tensor // 2
        self.send, self.recv, self.local_sems = send, recv, local
        self.used = 0
        self.d, self.t = lax.axis_index("dp"), lax.axis_index("tensor")
        self.h, self.q = self.t // self.width, self.t % self.width

    def slots(self, count):
        self.used += count
        return self.used - count

    def far(self, source, target, axis, place, k, k_recv=None):
        return pltpu.make_async_remote_copy(
            src_ref=source,
            dst_ref=target,
            send_sem=self.send.at[k],
            recv_sem=self.recv.at[k if k_recv is None else k_recv],
            device_id={axis: place},
            device_id_type=pl.DeviceIdType.MESH,
        )

    def near(self, source, target, k):
        return pltpu.make_async_copy(source, target, self.local_sems.at[k])


def along(ref, axis, start, count):
    return ref.at[(slice(None),) * axis + (pl.ds(start, count),)]


def mixed(index, offset):
    for bit in bits_of(offset * 2):
        if offset & bit:
            index = partner(index, bit)
    return index


def mirrored(index, count):
    bits = bits_of(count)
    return sum(((index // bit) % 2) * (count // (2 * bit)) for bit in bits)


def dp_copies(n_dp):
    return n_dp - 1


def dp_steps(ship, view, first=None, only=None):
    base = ship.slots(dp_copies(ship.n_dp))
    guard = (lambda f: f()) if only is None else pl.when(only)
    offsets, copies = [0], []
    for bit in reversed(bits_of(ship.n_dp)):
        new = []
        for o in offsets:
            at = view(mixed(ship.d, o))
            source = first if (first is not None and o == 0) else at
            new.append(ship.far(source, at, "dp", partner(ship.d, bit), base + len(copies) + len(new)))

        @guard
        def _():
            for c in new:
                c.start()

        yield

        @guard
        def _():
            for c in new:
                c.wait_recv()

        copies += new
        offsets += [o | bit for o in offsets]

    @guard
    def _():
        for c in copies:
            c.wait_send()


class Cargo:
    def __init__(self, inputs, outputs, count, run):
        self.inputs, self.outputs, self.count, self.run = inputs, outputs, count, run


def send_share(weight, axis, n_dp):
    part = weight.shape[axis] // n_dp
    shape = list(weight.shape)
    shape[axis] = part

    def run(ship, ins, outs):
        c = ship.far(
            along(ins[0], axis, ship.d * part, part),
            outs[0],
            "tensor",
            partner(ship.t, ship.width),
            ship.slots(1),
        )
        c.start()
        yield
        c.wait()

    return Cargo([weight], [(tuple(shape), weight.dtype)], 1, run)


def join_shares(share, axis, n_dp):
    part = share.shape[axis]
    shape = list(share.shape)
    shape[axis] = part * n_dp

    def run(ship, ins, outs):
        view = lambda i: along(outs[0], axis, i * part, part)
        put = ship.near(ins[0], view(ship.d), ship.slots(1))
        put.start()
        yield from dp_steps(ship, view, first=ins[0])
        put.wait()

    return Cargo([share], [(tuple(shape), share.dtype)], 1 + dp_copies(n_dp), run)


def fetch(weight, axis, n_dp):
    part = weight.shape[axis] // n_dp

    def run(ship, ins, outs):
        view = lambda i: along(outs[0], axis, i * part, part)
        c = ship.far(
            along(ins[0], axis, ship.d * part, part),
            view(ship.d),
            "tensor",
            partner(ship.t, ship.width),
            ship.slots(1),
        )
        c.start()
        yield
        c.wait()
        yield from dp_steps(ship, view)

    return Cargo([weight], [(weight.shape, weight.dtype)], 1 + dp_copies(n_dp), run)


def swap_cargo(array, axis, bit):
    def run(ship, ins, outs):
        index = ship.d if axis == "dp" else ship.t
        c = ship.far(ins[0], outs[0], axis, partner(index, bit), ship.slots(1))
        c.start()
        yield
        c.wait()

    return Cargo([array], [(array.shape, array.dtype)], 1, run)


def gather_dp(share, axis, n_dp):
    part = share.shape[axis]
    shape = list(share.shape)
    shape[axis] = part * n_dp

    def run(ship, ins, outs):
        view = lambda i: along(outs[0], axis, mirrored(i, n_dp) * part, part)
        put = ship.near(ins[0], view(ship.d), ship.slots(1))
        put.start()
        yield from dp_steps(ship, view, first=ins[0])
        put.wait()

    return Cargo([share], [(tuple(shape), share.dtype)], 1 + dp_copies(n_dp), run)


def rows_dp(array, n_dp, upper=True):
    def run(ship, ins, outs):
        view = lambda i: outs[0].at[i]
        only = ship.h >= int(upper)
        k = ship.slots(1)

        @pl.when(only)
        def _():
            ship.near(ins[0], view(ship.d), k).start()

        yield from dp_steps(ship, view, first=ins[0], only=only)

        @pl.when(only)
        def _():
            ship.near(ins[0], view(ship.d), k).wait()

    return Cargo([array], [((n_dp,) + array.shape, array.dtype)], 1 + dp_copies(n_dp), run)


def spread_cargo(array, n_dp, n_tensor):
    block = array.shape[0] // CAP
    model = array.shape[1]

    def run(ship, ins, outs):
        source = ins[0]
        item, third = outs
        t, d = ship.t, ship.d
        base = ship.slots(4)

        def block_copy(i, start):
            b = CAP * t + i
            j = b % n_tensor
            target = jnp.where(b >= n_tensor, ship.width, 0) + j // 2
            at = j % 2
            rows = step(source, i * block, block)
            for kind in range(2):
                here = b >= 2 * n_tensor if kind else b < 2 * n_tensor
                into = step(third.at[d] if kind else item, at * block, block)

                @pl.when(here & (target == t))
                def _():
                    c = ship.near(rows, into, base + i)
                    c.start() if start else c.wait()

                @pl.when(here & (target != t))
                def _():
                    c = ship.far(rows, into, "tensor", target, base + i, base + 2 * kind + at)
                    c.start() if start else c.wait_send()

        def wait_place(kind, at):
            b = (2 if kind else ship.h) * n_tensor + 2 * ship.q + at

            @pl.when(b // CAP != t)
            def _():
                into = step(third.at[d] if kind else item, at * block, block)
                ship.far(into, into, "tensor", t, base, base + 2 * kind + at).wait_recv()

        for i in reversed(range(CAP)):
            block_copy(i, True)
        yield
        for i in range(CAP):
            block_copy(i, False)
        only = ship.h == 1

        @pl.when(only)
        def _():
            for at in range(2):
                wait_place(1, at)

        yield from dp_steps(ship, lambda i: third.at[i], only=only)
        for at in range(2):
            wait_place(0, at)

    outputs = [((2 * block, model), array.dtype), ((n_dp, 2 * block, model), array.dtype)]
    return Cargo([array], outputs, 4 + dp_copies(n_dp), run)


def return_cargo(item, third, n_tensor):
    block = item.shape[0] // 2
    model = item.shape[1]

    def run(ship, ins, outs):
        t = ship.t
        base = ship.slots(4)

        def send(kind, at, start):
            b = (2 if kind else ship.h) * n_tensor + 2 * ship.q + at
            target, i = b // CAP, b % CAP
            rows = step(ins[kind], at * block, block)
            into = step(outs[0], i * block, block)

            @pl.when(target == t)
            def _():
                c = ship.near(rows, into, base + 2 * kind + at)
                c.start() if start else c.wait()

            @pl.when(target != t)
            def _():
                c = ship.far(rows, into, "tensor", target, base + 2 * kind + at, base + i)
                c.start() if start else c.wait_send()

        def all_sends(start):
            for at in range(2):
                send(0, at, start)

            @pl.when(ship.h == 1)
            def _():
                for at in range(2):
                    send(1, at, start)

        all_sends(True)
        yield
        for i in range(CAP):
            b = CAP * t + i
            holder = jnp.where(b >= n_tensor, ship.width, 0) + (b % n_tensor) // 2

            @pl.when(holder != t)
            def _():
                into = step(outs[0], i * block, block)
                ship.far(into, into, "tensor", t, base, base + i).wait_recv()

        all_sends(False)

    return Cargo([item, third], [((CAP * block, model), item.dtype)], 4, run)


def exchange(
    cid,
    n_dp,
    n_tensor,
    rows,
    model,
    inputs=(),
    outputs=(),
    middle=None,
    scatter=False,
    gather=False,
    cargo=(),
    vmem_mib=40,
):
    width = n_tensor // 2
    half = rows // 2
    pieces = [(o, hs) for o in range(1, width) for hs in range(2)]
    number = {piece: k for k, piece in enumerate(pieces)}
    bits = bits_of(width)

    def last_bit(piece):
        return top_bit(piece[0]) if piece[1] == 0 else low_bit(piece[0])

    def incoming(piece):
        return [p for p in pieces if p[1] == piece[1] and p[0] ^ last_bit(p) == piece[0]]

    scatter_order = sorted(pieces, key=lambda p: (-popcount(p[0]), len(incoming(p)), p[0]))
    gather_order = sorted(
        pieces, key=lambda p: (popcount(p[0]), p[1] if last_bit(p) != bits[-1] else 1 - p[1])
    )
    n_in, n_out = len(inputs), len(outputs)
    carried = [array for c in cargo for array in c.inputs]
    landed = [shape for c in cargo for shape in c.outputs]
    cargo_copies = max(sum(c.count for c in cargo), 1)

    def kernel(*refs):
        rest = list(refs)

        def take(count):
            taken = rest[:count]
            del rest[:count]
            return taken

        ins, cargo_ins, outs, cargo_outs = take(n_in), take(len(carried)), take(n_out), take(len(landed))
        gathered = rest.pop(0) if gather else None
        ship = Ship(n_dp, n_tensor, *take(3))
        own = rest.pop(0)
        local_sem = rest.pop(0)
        if scatter:
            arrived, s_send, s_recv = rest.pop(0), rest.pop(0), rest.pop(0)
        if gather:
            g_send, g_recv = rest.pop(0), rest.pop(0)
        t, d = ship.t, ship.d
        barrier = pltpu.get_barrier_semaphore()
        greeted = [("tensor", (t + k) % n_tensor) for k in range(1, n_tensor)]
        greeted += [("dp", partner(d, bit)) for bit in bits_of(n_dp)]
        for axis, place in greeted:
            pl.semaphore_signal(
                barrier, inc=1, device_id={axis: place}, device_id_type=pl.DeviceIdType.MESH
            )
        pl.semaphore_wait(barrier, len(greeted))

        stages = []
        for c in cargo:
            c_ins, cargo_ins = cargo_ins[: len(c.inputs)], cargo_ins[len(c.inputs) :]
            c_outs, cargo_outs = cargo_outs[: len(c.outputs)], cargo_outs[len(c.outputs) :]
            stages.append(c.run(ship, c_ins, c_outs))
        for stage in stages:
            next(stage)

        if scatter:
            part = ins[0]
            copies = {}
            for piece in scatter_order:
                o, hs = piece
                came = incoming(piece)
                base = o * rows + hs * half
                for p in came:
                    copies[p].wait_recv()
                source = step(part, base, half)
                if came:
                    source = arrived.at[number[came[0]]]

                    def add(r, base=base, came=came):
                        total = part[pl.ds(base + r, ROW_TILE)].astype(f32)
                        for p in came:
                            total = total + arrived[number[p], pl.ds(r, ROW_TILE)].astype(f32)
                        arrived[number[came[0]], pl.ds(r, ROW_TILE)] = total.astype(bf16)

                    row_tiles(half, add)
                k = number[piece]
                copies[piece] = pltpu.make_async_remote_copy(
                    src_ref=source,
                    dst_ref=arrived.at[k],
                    send_sem=s_send.at[k],
                    recv_sem=s_recv.at[k],
                    device_id={"tensor": partner(t, last_bit(piece))},
                    device_id_type=pl.DeviceIdType.MESH,
                )
                copies[piece].start()
            for piece in pieces:
                if popcount(piece[0]) == 1:
                    copies[piece].wait_recv()

        def summed(hs, r):
            total = ins[0][pl.ds(hs * half + r, ROW_TILE)].astype(f32)
            for bit in bits:
                total = total + arrived[number[(bit, hs)], pl.ds(r, ROW_TILE)].astype(f32)
            return total

        if middle is not None:
            middle(half, summed, ins, outs, own)

        if gather:
            keep = pltpu.make_async_copy(own, step(gathered, 0, rows), local_sem)
            keep.start()
            sent = {}
            for piece in gather_order:
                o, hs = piece
                bit = last_bit(piece)
                before = o ^ bit
                if before:
                    sent[(before, hs)].wait_recv()
                    source = step(gathered, before * rows + hs * half, half)
                else:
                    source = step(own, hs * half, half)
                k = number[piece]
                sent[piece] = pltpu.make_async_remote_copy(
                    src_ref=source,
                    dst_ref=step(gathered, o * rows + hs * half, half),
                    send_sem=g_send.at[k],
                    recv_sem=g_recv.at[k],
                    device_id={"tensor": partner(t, bit)},
                    device_id_type=pl.DeviceIdType.MESH,
                )
                sent[piece].start()
        while stages:
            stages = [stage for stage in stages if next(stage, stage) is not stage]
        if gather:
            used = {(p[0] ^ last_bit(p), p[1]) for p in pieces if p[0] ^ last_bit(p)}
            for piece in pieces:
                if piece not in used:
                    sent[piece].wait_recv()
            keep.wait()
            for piece in pieces:
                sent[piece].wait_send()
        if scatter:
            for piece in pieces:
                copies[piece].wait_send()

    vmem = pl.BlockSpec(memory_space=pltpu.VMEM)
    anywhere = pl.BlockSpec(memory_space=pl.ANY)
    shapes = [jax.ShapeDtypeStruct(*o) for o in list(outputs) + landed]
    specs = [vmem] * n_out + [anywhere] * len(landed)
    if gather:
        shapes.append(jax.ShapeDtypeStruct((width * rows, model), bf16))
        specs.append(anywhere)
    scratch = [pltpu.SemaphoreType.DMA((cargo_copies,)) for _ in range(3)]
    scratch += [pltpu.VMEM((rows, model), bf16), pltpu.SemaphoreType.DMA]
    count = len(pieces)
    if scatter:
        scratch += [
            pltpu.VMEM((count, half, model), bf16),
            pltpu.SemaphoreType.DMA((count,)),
            pltpu.SemaphoreType.DMA((count,)),
        ]
    if gather:
        scratch += [pltpu.SemaphoreType.DMA((count,)), pltpu.SemaphoreType.DMA((count,))]
    results = pl.pallas_call(
        kernel,
        out_shape=shapes,
        in_specs=[vmem] * n_in + [anywhere] * len(carried),
        out_specs=specs,
        scratch_shapes=scratch,
        compiler_params=pltpu.CompilerParams(
            collective_id=cid, has_side_effects=True, vmem_limit_bytes=vmem_mib << 20
        ),
        name=f"exchange_{cid}",
    )(*inputs, *carried)
    plain, rest = list(results[:n_out]), list(results[n_out:])
    if gather:
        plain.append(rest.pop())
    brought = []
    for c in cargo:
        brought.append(rest[: len(c.outputs)])
        rest = rest[len(c.outputs) :]
    return plain, brought


def norm_tile(values):
    centre = values - jnp.mean(values, -1, keepdims=True)
    scale_inv = lax.rsqrt(jnp.mean(centre * centre, -1, keepdims=True) + epsilon)
    return centre * scale_inv, scale_inv


def norm_back_tile(grad_out, normed, scale_inv, gain):
    grad_normed = grad_out * gain
    centred = grad_normed - jnp.mean(grad_normed, -1, keepdims=True)
    return scale_inv * (centred - normed * jnp.mean(grad_normed * normed, -1, keepdims=True))


def each_tile(half, body):
    for hs in range(2):
        row_tiles(half, lambda r, hs=hs: body(hs, r, pl.ds(hs * half + r, ROW_TILE)))


def fold(values):
    return jnp.sum(values.reshape(-1, 8, values.shape[-1]), 0)


def gather_middle(half, summed, ins, outs, own):
    def body(hs, r, at):
        own[at] = ins[0][at]

    each_tile(half, body)


def first_middle(half, summed, ins, outs, own):
    _, tokens, b_out, gain, shift = ins

    def body(hs, r, at):
        first = deep_alpha * tokens[at].astype(f32) + (summed(hs, r) + b_out[...])
        outs[0][at] = first
        normed, _ = norm_tile(first)
        own[at] = (normed * gain[...] + shift[...]).astype(bf16)

    each_tile(half, body)


def second_middle(half, summed, ins, outs, own):
    _, first_sum, cotangent, b_down, gain_one, shift_one, gain_two, shift_two = ins
    layer_rows, grad_second, sums = outs
    sums[...] = jnp.zeros_like(sums)

    def body(hs, r, at):
        normed, _ = norm_tile(first_sum[at])
        hidden = normed * gain_one[...] + shift_one[...]
        second = deep_alpha * hidden + (summed(hs, r) + b_down[...])
        normed, inv = norm_tile(second)
        layer_rows[at] = (normed * gain_two[...] + shift_two[...]).astype(bf16)
        grad = cotangent[at].astype(f32)
        back = norm_back_tile(grad, normed, inv, gain_two[...])
        grad_second[at] = back
        own[at] = back.astype(bf16)
        sums[0] += fold(grad * normed)
        sums[1] += fold(grad)
        sums[2] += fold(back)

    each_tile(half, body)


def third_middle(half, summed, ins, outs, own):
    _, first_sum, grad_second, gain_one = ins
    grad_first, sums = outs
    sums[...] = jnp.zeros_like(sums)

    def body(hs, r, at):
        normed, inv = norm_tile(first_sum[at])
        grad = summed(hs, r) + deep_alpha * grad_second[at]
        back = norm_back_tile(grad, normed, inv, gain_one[...])
        grad_first[at] = back
        own[at] = back.astype(bf16)
        sums[0] += fold(grad * normed)
        sums[1] += fold(grad)
        sums[2] += fold(back)

    each_tile(half, body)


def last_middle(half, summed, ins, outs, own):
    _, grad_first = ins

    def body(hs, r, at):
        outs[0][at] = (summed(hs, r) + deep_alpha * grad_first[at]).astype(bf16)

    each_tile(half, body)


def pick(index, values):
    out = values[0]
    for k, value in enumerate(values[1:], 1):
        out = jnp.where(index == k, value, out)
    return out


def across(value, n_dp):
    got = {0: value}
    for bit in reversed(bits_of(n_dp)):
        for offset in list(got):
            got[offset | bit] = permute(got[offset], "dp", n_dp, bit)
    return [got[offset] for offset in range(n_dp)]


def turn(vectors, cos_table, sin_table):
    return vectors * cos_table + pltpu.roll(vectors, HD // 2, 1) * sin_table


def score_tile(queries, keys, base, key_at, prefix_len):
    scores = lax.dot_general(
        queries, keys, (((1,), (1,)), ((), ())), preferred_element_type=f32
    ) * HD ** (-0.5)
    query_at = base + lax.broadcasted_iota(jnp.int32, (queries.shape[0], 1), 0)
    allowed = (key_at < prefix_len) | (key_at <= query_at)
    return jnp.where(allowed, scores, negative)


def attend_kernel(
    heads, rows, place, own, other, bias, cos_table, sin_table, key_at, turned, context
):
    prefix_len = place[0]
    size = heads * HD
    for head in range(heads):
        for c in range(3):
            at = pl.ds(c * size + head * HD, HD)
            p, local = divmod(head, heads // 2)
            came = pl.ds(local * HD, HD)
            value = (own, other)[p][c, :, came] + bias[p, c : c + 1, came]
            if c < 2:
                value = turn(value, cos_table[...], sin_table[...])
            turned[:, at] = value.astype(bf16)
    for head in range(heads):
        at = head * HD

        def one_block(i, carry, at=at):
            run = pl.ds(pl.multiple_of(i * rows, rows), rows)
            scores = score_tile(
                turned[run, at : at + HD],
                turned[:, size + at : size + at + HD],
                place[1 + i],
                key_at[...],
                prefix_len,
            )
            raw = jnp.exp(scores - jnp.max(scores, -1, keepdims=True))
            weights = (raw / jnp.sum(raw, -1, keepdims=True)).astype(bf16)
            context[run, at : at + HD] = jnp.dot(
                weights, turned[:, 2 * size + at : 2 * size + at + HD], preferred_element_type=f32
            ).astype(bf16)
            return carry

        lax.fori_loop(0, LEN // rows, one_block, 0)


def attend(linear, bias, place, cos_table, sin_table, key_at, rows):
    size = 2 * 3 * linear[0].shape[2]
    heads = size // (3 * HD)
    vmem = pl.BlockSpec(memory_space=pltpu.VMEM)
    return pl.pallas_call(
        functools.partial(attend_kernel, heads, rows),
        out_shape=[
            jax.ShapeDtypeStruct((LEN, size), bf16),
            jax.ShapeDtypeStruct((LEN, size // 3), bf16),
        ],
        in_specs=[pl.BlockSpec(memory_space=pltpu.SMEM)] + [vmem] * 6,
        out_specs=[vmem] * 2,
        compiler_params=pltpu.CompilerParams(vmem_limit_bytes=40 << 20),
        name="attend",
    )(place, *linear, bias, cos_table, sin_table, key_at)


def attend_back_kernel(
    heads, rows, place, turned, grad_context, cos_table, sin_table, key_at, own, other, dk, dv
):
    prefix_len = place[0]
    size = heads * HD
    scale = HD ** (-0.5)
    over_rows = (((0,), (0,)), ((), ()))
    over_last = (((1,), (1,)), ((), ()))
    for head in range(heads):
        at = head * HD
        p, local = divmod(head, heads // 2)
        came = pl.ds(local * HD, HD)
        grad_linear = (own, other)[p]
        dk[...] = jnp.zeros_like(dk)
        dv[...] = jnp.zeros_like(dv)

        def one_block(i, carry, at=at, grad_linear=grad_linear, came=came):
            run = pl.ds(pl.multiple_of(i * rows, rows), rows)
            queries = turned[run, at : at + HD]
            keys = turned[:, size + at : size + at + HD]
            scores = score_tile(queries, keys, place[1 + i], key_at[...], prefix_len)
            raw = jnp.exp(scores - jnp.max(scores, -1, keepdims=True))
            probs = raw / jnp.sum(raw, -1, keepdims=True)
            grad = grad_context[run, at : at + HD]
            grad_weights = lax.dot_general(
                grad,
                turned[:, 2 * size + at : 2 * size + at + HD],
                over_last,
                preferred_element_type=f32,
            )
            inner = jnp.sum(probs * grad_weights, -1, keepdims=True)
            grad_scores = (probs * (grad_weights - inner)).astype(bf16)
            dq = jnp.dot(grad_scores, keys, preferred_element_type=f32) * scale
            grad_linear[0, run, came] = turn(dq, cos_table[run], sin_table[run]).astype(bf16)
            dk[...] += lax.dot_general(grad_scores, queries, over_rows, preferred_element_type=f32)
            dv[...] += lax.dot_general(
                probs.astype(bf16), grad, over_rows, preferred_element_type=f32
            )
            return carry

        lax.fori_loop(0, LEN // rows, one_block, 0)
        grad_linear[1, :, came] = turn(dk[...] * scale, cos_table[...], sin_table[...]).astype(bf16)
        grad_linear[2, :, came] = dv[...].astype(bf16)


def attend_back(turned, grad_context, place, cos_table, sin_table, key_at, rows):
    size = turned.shape[1]
    heads = size // (3 * HD)
    vmem = pl.BlockSpec(memory_space=pltpu.VMEM)
    return pl.pallas_call(
        functools.partial(attend_back_kernel, heads, rows),
        out_shape=[jax.ShapeDtypeStruct((3, LEN, size // 6), bf16)] * 2,
        in_specs=[pl.BlockSpec(memory_space=pltpu.SMEM)] + [vmem] * 5,
        out_specs=[vmem] * 2,
        scratch_shapes=[pltpu.VMEM((LEN, HD), f32), pltpu.VMEM((LEN, HD), f32)],
        compiler_params=pltpu.CompilerParams(vmem_limit_bytes=40 << 20),
        name="attend_back",
    )(place, turned, grad_context, cos_table, sin_table, key_at)


def on_device(
    n_dp,
    n_tensor,
    tokens,
    cotangent,
    w_qkv,
    b_qkv,
    w_out,
    b_out,
    gain_one,
    shift_one,
    w_gu,
    b_gu,
    w_down,
    b_down,
    gain_two,
    shift_two,
    prefix,
    span_offset,
    cluster,
):
    d = lax.axis_index("dp")
    t = lax.axis_index("tensor")
    width = n_tensor // 2
    h = t // width
    q = t % width
    rows = LEN // width
    model = tokens.shape[1]
    block = LEN // n_tensor

    counts = jnp.sum((cluster[None, :] == jnp.arange(n_dp)[:, None]).astype(jnp.int32), 1)
    spare = jnp.maximum(2 - counts, 0)
    extra = (counts == CAP).astype(jnp.int32)
    spare_before = jnp.cumsum(spare) - spare
    extra_rank = jnp.cumsum(extra) - extra

    def overflow_source(index, place):
        rank = spare_before[index] + place - counts[index]
        hit = (extra == 1) & (extra_rank == rank)
        return jnp.sum(jnp.where(hit, jnp.arange(n_dp), 0))

    source_here = overflow_source(d, h)
    source_other = overflow_source(d, 0)
    foreign = counts[d] <= h
    any_empty = jnp.any(counts == 0)
    rank_out = extra_rank[d]
    ends = spare_before + spare
    out_index = jnp.sum((ends <= rank_out).astype(jnp.int32))
    out_place = jnp.minimum(counts[out_index], 2) + rank_out - spare_before[out_index]

    def chosen(item, third):
        def with_empty(item):
            sent = permute(third[source_other], "tensor", n_tensor, width)
            return jnp.where((h == 0) & foreign, sent, item)

        item = lax.cond(any_empty, with_empty, lambda v: v, item)
        return jnp.where((h == 1) & foreign, third[source_here], item)

    def sorted_out(item, everywhere, absolute):
        third = everywhere[out_index if absolute else d ^ out_index]

        def with_empty(third):
            other = across(permute(item, "tensor", n_tensor, width), n_dp)
            return jnp.where(out_place == 0, pick(d ^ out_index, other), third)

        third = lax.cond(any_empty, with_empty, lambda v: v, third)
        return jnp.where(foreign, 0, item), jnp.where(counts[d] == CAP, third, 0)

    def flipped(array):
        return permute(array, "tensor", n_tensor, width)

    width_qkv = w_qkv.shape[2]
    width_ffn = w_gu.shape[2]
    wq = w_qkv.transpose(1, 0, 2)
    wg = w_gu.transpose(2, 1, 0)
    cut_ffn = 0 if width_ffn % n_dp == 0 else 2
    columns = jnp.arange(width_ffn)
    live_columns = [s * width_ffn + columns < FF for s in (t, t ^ width)]
    pairs = (0, 1)

    def row(vector):
        return vector.reshape(1, -1)

    def tile_of(array):
        return jnp.pad(array, ((0, 8 - array.shape[0]), (0, -array.shape[1] % 128)))

    swap = functools.partial(exchange, n_dp=n_dp, n_tensor=n_tensor, rows=rows, model=model)
    facts = jnp.stack([prefix, span_offset])

    _, (spread_tokens, (wq_other,), (facts_all,), (bq_other,), (bg_other,)) = swap(
        0,
        cargo=[
            spread_cargo(tokens, n_dp, n_tensor),
            fetch(wq, 1, n_dp),
            rows_dp(tile_of(facts), n_dp, upper=False),
            swap_cargo(tile_of(b_qkv), "tensor", width),
            swap_cargo(tile_of(b_gu), "tensor", width),
        ],
    )
    wq = [wq, wq_other]
    bq = jnp.stack([b_qkv, bq_other[:3, :width_qkv]])
    bg = [b_gu, bg_other[:2, :width_ffn]]
    facts_all = facts_all[:, :2, :CAP]
    own_tokens = chosen(*spread_tokens)
    (tokens_all,), ((wo_other,), (wg_share,)) = swap(
        1,
        inputs=[own_tokens],
        middle=gather_middle,
        gather=True,
        cargo=[fetch(w_out, 0, n_dp), send_share(wg, cut_ffn, n_dp)],
    )
    fact = jnp.where(foreign, facts_all[source_here][:, 2], jnp.where(h == 0, facts[:, 0], facts[:, 1]))
    prefix_len, span_start = fact[0], fact[1]

    starts = (q ^ jnp.arange(width)) * rows
    position = (starts[:, None] + jnp.arange(rows)[None, :]).reshape(LEN)
    placed = jnp.where(position < prefix_len, position, span_start + position - prefix_len).astype(f32)
    frequency = theta_base ** (-(jnp.arange(HD // 2).astype(f32) * 2.0 / HD))
    angles = placed[:, None] * frequency[None, :]
    cos_half, sin_half = jnp.cos(angles), jnp.sin(angles)
    cos_table = jnp.concatenate([cos_half, cos_half], 1)
    sin_table = jnp.concatenate([-sin_half, sin_half], 1)
    key_at = position[None, :].astype(jnp.int32)
    place = jnp.concatenate([prefix_len[None], starts]).astype(jnp.int32)

    def dot(a, b):
        return jnp.dot(a, b, preferred_element_type=f32)

    def sum_of(spec, a, b):
        terms = [jnp.einsum(spec, a[p], b[p], preferred_element_type=f32) for p in pairs]
        return (terms[0] + terms[1]).astype(bf16)

    wo = jnp.concatenate([w_out, wo_other], 0)
    linear = [jnp.einsum("td,cdn->ctn", tokens_all, wq[p], preferred_element_type=f32) for p in pairs]
    turned, context = attend(linear, bq, place, cos_table, sin_table, key_at, rows)
    partial_out = dot(context, wo).astype(bf16)
    full = ((rows, model), f32)
    (first_sum, hidden_all), (spread_cotangent, (wg_other,), (wd_other,)) = swap(
        2,
        inputs=[partial_out, own_tokens, row(b_out), row(gain_one), row(shift_one)],
        outputs=[full],
        middle=first_middle,
        scatter=True,
        gather=True,
        cargo=[
            spread_cargo(cotangent, n_dp, n_tensor),
            join_shares(wg_share, cut_ffn, n_dp),
            fetch(w_down, 1, n_dp),
        ],
    )
    wg = [wg, wg_other]
    wd = [w_down, wd_other]
    own_cotangent = chosen(*spread_cotangent)

    def activate(live, gate_up):
        return jnp.where(live, jax.nn.gelu(gate_up[0], approximate=True) * gate_up[1], 0.0)

    inner, pull = [], []
    for p in pairs:
        gate_up = jnp.einsum("td,ncd->ctn", hidden_all, wg[p], preferred_element_type=f32)
        activated, pull_act = jax.vjp(
            functools.partial(activate, live_columns[p]), gate_up + bg[p][:, None]
        )
        inner.append(activated.astype(bf16))
        pull.append(pull_act)
    partial_fed = sum_of("tn,nd->td", inner, wd)
    sums_shape = ((3, 8, model), f32)
    (layer_rows, grad_second, sums_two, grad_fed_all), _ = swap(
        3,
        inputs=[
            partial_fed,
            first_sum,
            own_cotangent,
            row(b_down),
            row(gain_one),
            row(shift_one),
            row(gain_two),
            row(shift_two),
        ],
        outputs=[((rows, model), bf16), full, sums_shape],
        middle=second_middle,
        scatter=True,
        gather=True,
    )

    def halve(value, axis, bit):
        part = value.shape[axis] // 2
        upper = ((d & bit) != 0).astype(jnp.int32)
        return (
            lax.dynamic_slice_in_dim(value, upper * part, part, axis),
            lax.dynamic_slice_in_dim(value, (1 - upper) * part, part, axis),
        )

    def add(a, b):
        return (a.astype(f32) + b.astype(f32)).astype(bf16)

    dp_bits = bits_of(n_dp)

    def dot_rows(a, b):
        return lax.dot_general(a, b, (((0,), (0,)), ((), ())), preferred_element_type=f32)

    def halve_first(value, axis):
        for bit in dp_bits[:-1]:
            keep, send = halve(value, axis, bit)
            value = add(keep, permute(send, "dp", n_dp, bit))
        return halve(value, axis, dp_bits[-1])

    def across_dp(value):
        return swap_cargo(value, "dp", dp_bits[-1])

    def across_pair(value):
        return swap_cargo(value, "tensor", width)

    grad_gate_up = [
        pull[p](jnp.einsum("td,nd->tn", grad_fed_all, wd[p], preferred_element_type=f32))[0].astype(bf16)
        for p in pairs
    ]

    def halve_pair(values, axis):
        halves = [halve_first(v.astype(bf16), axis) for v in values]
        return [x[0] for x in halves], [x[1] for x in halves]

    grad_w_gu = [
        jnp.einsum("td,ctn->ncd", hidden_all, grad_gate_up[p], preferred_element_type=f32)
        for p in pairs
    ]
    gu_keep, gu_send = halve_pair(grad_w_gu, cut_ffn)
    grad_w_down = [
        jnp.einsum("tn,td->nd", inner[p], grad_fed_all, preferred_element_type=f32) for p in pairs
    ]
    down_keep, down_send = halve_pair(grad_w_down, 1)
    grad_b_gu = jnp.stack([jnp.sum(grad_gate_up[p].astype(f32), 1) for p in pairs])
    partial_hidden = sum_of("ctn,ncd->td", grad_gate_up, wg)
    (grad_first, sums_one, grad_att_all), ((gu_came0,), (gu_came1,)) = swap(
        4,
        inputs=[partial_hidden, first_sum, grad_second, row(gain_one)],
        outputs=[full, sums_shape],
        middle=third_middle,
        scatter=True,
        gather=True,
        cargo=[across_dp(gu_send[0]), across_dp(gu_send[1])],
    )
    gu = add(gu_keep[0], gu_came0)
    gu_other = add(gu_keep[1], gu_came1)
    gu = add(gu, flipped(gu_other))
    down = [add(down_keep[p], permute(down_send[p], "dp", n_dp, dp_bits[-1])) for p in pairs]
    layer_everywhere = jnp.stack(across(layer_rows, n_dp))
    grad_context = lax.dot_general(
        grad_att_all, wo, (((1,), (1,)), ((), ())), preferred_element_type=f32
    ).astype(bf16)
    grad_linear = attend_back(turned, grad_context, place, cos_table, -sin_table, key_at, rows)
    grad_w_out = dot_rows(context, grad_att_all).astype(bf16).reshape(2, width_qkv, model)
    grad_w_qkv = [
        jnp.einsum("td,ctn->cdn", tokens_all, grad_linear[p], preferred_element_type=f32)
        for p in pairs
    ]
    grad_b_qkv = jnp.stack([jnp.sum(grad_linear[p].astype(f32), 1) for p in pairs])
    out_keep, out_send = halve_first(grad_w_out, 1)
    qkv_keep, qkv_send = halve_pair(grad_w_qkv, 1)
    partial_in = sum_of("ctn,cdn->td", grad_linear, wq)
    (
        (input_rows,),
        ((out_came,), (qkv_came0,), (qkv_came1,), (down_came,), (layer_out,), (gu,)),
    ) = swap(
        5,
        inputs=[partial_in, grad_first],
        outputs=[((rows, model), bf16)],
        middle=last_middle,
        scatter=True,
        cargo=[
            across_dp(out_send),
            across_dp(qkv_send[0]),
            across_dp(qkv_send[1]),
            across_pair(down[1]),
            return_cargo(*sorted_out(layer_rows, layer_everywhere, False), n_tensor),
            gather_dp(gu, cut_ffn, n_dp),
        ],
    )
    down = add(down[0], down_came)
    out = add(out_keep, out_came)
    qkv = [add(qkv_keep[0], qkv_came0), add(qkv_keep[1], qkv_came1)]
    _, ((input_everywhere,), (out_came,), (qkv_came,), (down,)) = swap(
        6,
        cargo=[
            rows_dp(input_rows, n_dp),
            across_pair(out[1]),
            across_pair(qkv[1]),
            gather_dp(down, 1, n_dp),
        ],
    )
    out = add(out[0], out_came)
    qkv = add(qkv[0], qkv_came)
    _, ((input_grad,), (out,), (qkv,)) = swap(
        7,
        cargo=[
            return_cargo(*sorted_out(input_rows, input_everywhere, True), n_tensor),
            gather_dp(out, 0, n_dp),
            gather_dp(qkv, 1, n_dp),
        ],
    )

    def reduce_small(everywhere, pair):
        for bit in dp_bits:
            everywhere, pair = jax.tree.map(
                lambda v: v + permute(v, "dp", n_dp, bit), (everywhere, pair)
            )
        own = pair[0] + flipped(pair[1])
        for bit in bits_of(n_tensor):
            everywhere = everywhere + permute(everywhere, "tensor", n_tensor, bit)
        return everywhere, own

    norm_grads = jnp.concatenate([jnp.sum(sums_one, 1), jnp.sum(sums_two, 1)])
    bias = jnp.concatenate(
        [grad_b_qkv.reshape(2, 3 * width_qkv), grad_b_gu.reshape(2, 2 * width_ffn)], 1
    )
    norm_grads, bias = reduce_small(norm_grads, bias)
    grad_b_qkv = bias[: 3 * width_qkv].reshape(3, width_qkv)
    grad_b_gu = bias[3 * width_qkv :].reshape(2, width_ffn)
    return (
        layer_out.astype(f32),
        input_grad.astype(f32),
        qkv.astype(f32).transpose(1, 0, 2),
        grad_b_qkv,
        out.astype(f32),
        norm_grads[2],
        norm_grads[0],
        norm_grads[1],
        gu.astype(f32).transpose(2, 1, 0),
        grad_b_gu,
        down.astype(f32),
        norm_grads[5],
        norm_grads[3],
        norm_grads[4],
    )


def solution(mesh):
    rows = P(("dp", "tensor"), None)
    weights = (P(None, None, "tensor"), P(None, "tensor"), P("tensor", None), P(), P(), P())
    placed_ffn = (P(None, None, "tensor"), P(None, "tensor"), P("tensor", None), P(), P(), P())
    placed = (rows, rows) + weights + placed_ffn + (P("dp"), P("dp"), P())
    n_dp, n_tensor = mesh.shape["dp"], mesh.shape["tensor"]

    def body(*arguments):
        return on_device(n_dp, n_tensor, *arguments)

    return jax.shard_map(
        body,
        mesh=mesh,
        in_specs=placed,
        out_specs=(rows, rows) + weights + placed_ffn,
        check_vma=False,
    )
```

time: 1280 us -> 1110 us (0.87)
  Pallas kernels: 0 us -> 692 us
  waiting for transfers between devices: 464 us -> 54.5 us
  local copies, waits for them, and re-layouts: 262 us -> 94 us
  starting transfers between devices: 146 us -> 14.3 us
  other arithmetic: 175 us -> 79.9 us
  between operations: 51.5 us -> 13.7 us
  matrix products: 165 us -> 144 us
    pallas_call x0 -> x10, Pallas kernels: none -> 692 us  [the longest x8 655 us: exchange(): pl.pallas_call(kernel, out_shape=shapes, in_specs=[vmem] * n_in + [anywhe...]
    ppermute x88 -> x21, waiting for transfers between devices: 460 us -> 54.5 us  [permute(): return lax.ppermute(value, axis, [(i, i ^ bit) for i in range(size)])]
    ppermute x88 -> x21, starting transfers between devices: 102 us -> 14.3 us  [permute(): return lax.ppermute(value, axis, [(i, i ^ bit) for i in range(size)])]
    dynamic_slice x33 -> x15, local copies, waits for them, and re-layouts: 69.6 us -> 22.5 us  [the longest x14 21.9 us: halve(): lax.dynamic_slice_in_dim(value, (1 - upper) * part, part, axis)]
    unnamed x301 -> x201, local copies, waits for them, and re-layouts: 77.4 us -> 33.7 us
    ppermute x20 -> x0, starting transfers between devices: 43.7 us -> none  [the longest x10 22.9 us: move_in(): got.append(lax.ppermute(send, 'tensor', [(e[0], e[2]) for e in r]))]
    reshape x7 -> x0, local copies, waits for them, and re-layouts: 39.4 us -> none  [fetch(): share.reshape(share.shape[:axis] + (2,) * count + (part,) + share.shape[a...]
    select_n x40 -> x6, other arithmetic: 44.7 us -> 5.8 us  [the longest x2 3.1 us: chosen(): return jnp.where((h == 1) & foreign, third[source_here], item)]
  transfers between devices with their start and end apart: 108 -> 21, of which waited for: 36 -> 5; matrix products, arithmetic and copies ran while one was open for 43% -> 18% of each run, Pallas kernels for 0% -> 17%
where the time goes in v2:
time: 1110 us; the launch traced here: 1090 us
  Pallas kernels  692 us (62%)
  matrix products  144 us (13%)
  local copies, waits for them, and re-layouts  94 us (8%)
  other arithmetic  79.9 us (7%)
  waiting for transfers between devices  54.5 us (5%)
  starting transfers between devices  14.3 us (1%)
  between operations  13.7 us (1%)
    pallas_call x8, Pallas kernels, exchange(): pl.pallas_call(kernel, out_shape=shapes, in_specs=[vmem] * n_in + [anywhe...  655 us
    ppermute x21, waiting for transfers between devices, permute(): return lax.ppermute(value, axis, [(i, i ^ bit) for i in range(size)])  54.5 us
    dot_general x6, matrix products, sum_of(): jnp.einsum(spec, a[p], b[p], preferred_element_type=f32)  50.9 us
    unnamed x201, local copies, waits for them, and re-layouts  33.7 us
    convert_element_type x15, other arithmetic, add(): return (a.astype(f32) + b.astype(f32)).astype(bf16)  33.6 us
    dot_general x2, local copies, waits for them, and re-layouts, on_device(): jnp.einsum('td,ctn->ncd', hidden_all, grad_gate_up[p], preferred_element_...  30.3 us
  transfers between devices with their start and end apart: 21, of which 5 were waited for; matrix products, arithmetic and copies ran while one was open for 18% of the time, Pallas kernels for 17%

profile of v2, /device:TPU:10, one launch (start us, length us, event | category | flops | bytes accessed | tf_op | source)
XLA Modules:
  0.0 1093.0 jit_solution(10025139203904067652)
XLA Ops:
  17.1 92.3 %exchange_0.1 = (bf16[256,2048]{1,0:T(8,128)(2,1)}, bf16[4,256,2048]{2,1,0:T(8,128)(2,1)}, bf16[3,2048,256]{2,1,0:T(8,128)(2,1)S(1)}, s32[4,8,128]{2,1,0:T(8,128...) custom-call(bf16[384,2048]{1,0:T(8,128)(2,1)S(1)} %copy-done.21, bf16[3,2048,256]{2,1,0:T(8,128)(2,1)S(1)} %bitcast.242, ...), custom_call_target="tpu_custom_call" | custom-call | tf_op jit(solution)/shard_map/exchange_0/pallas_call | solution.py:522
  117.5 80.9 %exchange_1.1 = (bf16[256,2048]{1,0:T(8,128)(2,1)S(1)}, bf16[171,2,2048]{2,1,0:T(2,128)(2,1)S(1)}, bf16[1024,2048]{1,0:T(8,128)(2,1)S(1)}) custom-call(bf16[256,2048]{1,0:T(8,128)(2,1)S(1)} %bitcast_select_fusion.1.refs_0_.refs_1_, bf16[256,2048]{1,0:T(8,128)(2,1)S(1)} %copy-done.4, bf16[684,2,2048]{2,1,0:T(2,128)(2,1)S(1)} %bitcast.238), custom_call_target="tpu_custom_call" | custom-call | tf_op jit(solution)/shard_map/exchange_1/pallas_call | solution.py:522
  210.1 15.2 %attend.1 = (bf16[1024,1536]{1,0:T(8,128)(2,1)S(1)}, bf16[1024,512]{1,0:T(8,128)(2,1)S(1)}) custom-call(s32[5]{0:T(128)S(1)} %pad_add_fusion.1.place, f32[3,1024,256]{2,1,0:T(8,128)S(1)} %fusion.58.own, f32[3,1024,256]{2,1,0:T(8,128)S(1)} %fusion.61.other, f32[2,3,256]{2,1,0:T(4,128)S(1)} %pad_maximum_fusion.3.bias, ...), custom_call_target="tpu_custom_call" | custom-call | tf_op jit(solution)/shard_map/attend/pallas_call | solution.py:700
  230.2 117.7 %exchange_2.1 = (f32[256,2048]{1,0:T(8,128)S(1)}, bf16[256,2048]{1,0:T(8,128)(2,1)S(1)}, bf16[4,256,2048]{2,1,0:T(8,128)(2,1)}, bf16[684,2,2048]{2,1,0:T(2,128)(...) custom-call(bf16[1024,2048]{1,0:T(8,128)(2,1)} %convolution_convert_fusion.refs_0_, ...), custom_call_target="tpu_custom_call" | custom-call | tf_op jit(solution)/shard_map/exchange_2/pallas_call | solution.py:522
  350.8 12.6 %bitcast_add_fusion.3 = f32[2,1024,684]{1,2,0:T(8,128)S(1)} fusion(f32[2,684]{1,0:T(2,128)S(1)} %copy-done.78, bf16[684,2,2048]{2,1,0:T(2,128)(2,1)} %bitcast.237, bf16[1024,2048]{1,0:T(8,128)(2,1)} %get-tuple-element.142), kind=kOutput, calls=%fused_computation.16 | convolution fusion | flops 5739208704 | bytes 15406432 | tf_op jit(solution)/shard_map/td,ncd->ctn/dot_general | solution.py:932
  367.2 5.9 fusion.86
  373.2 7.6 bitcast_add_fusion.2
  384.6 6.0 add_convert_fusion.refs_0_
  390.7 113.6 %exchange_3.1 = (bf16[256,2048]{1,0:T(8,128)(2,1)}, f32[256,2048]{1,0:T(8,128)S(1)}, f32[3,8,2048]{2,1,0:T(8,128)S(1)}, bf16[1024,2048]{1,0:T(8,128)(2,1)S(1)}) custom-call(bf16[1024,2048]{1,0:T(8,128)(2,1)S(1)} %add_convert_fusion.refs_0_, f32[256,2048]{1,0:T(8,128)S(1)} %get-tuple-element.146.refs_1_, bf16[256,2048]{1,0:T(8,128)(2,1)S(1)} %bitcast_select_fusion.refs_2_, ...), custom_call_target="tpu_custom_call" | custom-call | tf_op jit(solution)/shard_map/exchange_3/pallas_call | solution.py:522
  509.1 7.3 convolution_convert_fusion.1
  519.6 5.5 convolution_convert_fusion.2
  528.0 9.7 multiply_bitcast_fusion
  537.7 6.3 fusion.12
  544.0 17.2 %copy.81 = bf16[2,684,2048]{2,0,1:T(2,128)(2,1)} copy(bf16[2,684,2048]{2,1,0:T(8,128)(2,1)S(1)} %fusion.12) | data formatting | bytes 11206656 | tf_op jit(solution)/shard_map/td,ctn->ncd/dot_general | solution.py:996
  561.2 5.4 dynamic-slice_bitcast_fusion.2
  567.2 8.4 multiply_bitcast_fusion.1
  575.6 13.6 %fusion.4 = f32[1024,2048,1]{1,0,2:T(8,128)} fusion(bf16[684,2,2048]{2,1,0:T(2,128)(2,1)} %get-tuple-element.143, f32[1,1024,684]{1,2,0:T(8,128)S(1)} %copy-done.66, f32[1,1024,684]{1,2,0:T(8,128)S(1)} %copy-done.64), kind=kOutput, calls=%fused_computation.25 | convolution fusion | flops 5740609536 | bytes 19595264 | tf_op jit(solution)/shard_map/ctn,ncd->td/dot_general | solution.py:902
  589.3 12.2 %fusion.1.refs_0_ = bf16[1024,2048]{1,0:T(8,128)(2,1)} fusion(f32[1024,2048,1]{1,0,2:T(8,128)} %fusion.4, bf16[684,2,2048]{2,1,0:T(2,128)(2,1)S(1)} %bitcast.241, f32[1,1024,684]{1,2,0:T(8,128)S(1)} %get-tuple-element.181, f32[1,1024,684]{1,2,0:T(8,128)S(1)} %get-tuple-element.180), kind=kOutput, calls=%fused_computation.12 | convolution fusion | flops 5744803840 | bytes 23789568 | tf_op jit(solution)/shard_map/ctn,ncd->td/dot_general | solution.py:902
  601.4 6.3 fusion.14
  607.7 13.0 %copy.82 = bf16[2,684,2048]{2,0,1:T(2,128)(2,1)S(1)} copy(bf16[2,684,2048]{2,1,0:T(8,128)(2,1)S(1)} %fusion.14) | data formatting | bytes 11206656 | tf_op jit(solution)/shard_map/td,ctn->ncd/dot_general | solution.py:996
  654.6 9.4 collective-permute-done.16
  666.6 5.6 fusion.2
  681.1 77.9 %exchange_4.1 = (f32[256,2048]{1,0:T(8,128)S(1)}, f32[3,8,2048]{2,1,0:T(8,128)S(1)}, bf16[171,2,2048]{2,1,0:T(2,128)(2,1)S(1)}, bf16[171,2,2048]{2,1,0:T(2,128)(2,1)S(1)}, bf16[1024,2048]{1,0:T(8,128)(2,1)}) custom-call(bf16[1024,2048]{1,0:T(8,128)(2,1)} %fusion.1.refs_0_, f32[256,2048]{1,0:T(8,128)S(1)} %get-tuple-element.146.refs_1_, ...), custom_call_target="tpu_custom_call" | custom-call | tf_op jit(solution)/shard_map/exchange_4/pallas_call | solution.py:522
  770.5 21.7 %attend_back.1 = (bf16[3,1024,256]{2,1,0:T(8,128)(2,1)S(1)}, bf16[3,1024,256]{2,1,0:T(8,128)(2,1)S(1)}) custom-call(s32[5]{0:T(128)S(1)} %copy-done.36, bf16[1024,1536]{1,0:T(8,128)(2,1)S(1)} %copy-done.6, bf16[1024,512]{1,0:T(8,128)(2,1)S(1)} %convolution_convert_fusion.4.grad_context, f32[1024,128]{1,0:T(8,128)S(1)} %copy-done.2, ...), custom_call_target="tpu_custom_call" | custom-call | tf_op jit(solution)/shard_map/attend_back/pallas_call | solution.py:762
  802.7 5.7 fusion.78
  815.8 7.6 fusion.refs_0_
  836.0 13.4 %collective-permute-done.29 = f32[6,2048]{1,0:T(8,128)S(1)} collective-permute-done((f32[6,2048]{1,0:T(8,128)S(1)}, f32[6,2048]{1,0:T(8,128)S(1)}, u32[]{:S(2)}, u32[]{:S(2)}) %collective-permute-start.29) | collective-permute-done | bytes 49184 | tf_op jit(solution)/shard_map/ppermute | solution.py:29
  852.2 26.5 %collective-permute-done.25 = f32[2136]{0:T(1024)S(1)} collective-permute-done((f32[2136]{0:T(1024)S(1)}, f32[2136]{0:T(1024)S(1)}, u32[]{:S(2)}, u32[]{:S(2)}) %collective-permute-start.25) | collective-permute-done | bytes 8576 | tf_op jit(solution)/shard_map/ppermute | solution.py:29
  892.9 87.4 %exchange_5.1 = (bf16[256,2048]{1,0:T(8,128)(2,1)S(1)}, bf16[2,64,2048]{2,1,0:T(8,128)(2,1)S(1)}, bf16[3,512,256]{2,1,0:T(8,128)(2,1)S(1)}, bf16[3,512,256]{2,1,...) custom-call(bf16[1024,2048]{1,0:T(8,128)(2,1)} %fusion.refs_0_, ...), custom_call_target="tpu_custom_call" | custom-call | tf_op jit(solution)/shard_map/exchange_5/pallas_call | solution.py:522
  985.3 51.4 %exchange_6.1 = (bf16[4,256,2048]{2,1,0:T(8,128)(2,1)S(1)}, bf16[64,2048]{1,0:T(8,128)(2,1)S(1)}, bf16[3,512,256]{2,1,0:T(8,128)(2,1)S(1)}, bf16[684,2048]{1,0:T(8,128)(2,1)S(1)}) custom-call(bf16[256,2048]{1,0:T(8,128)(2,1)S(1)} %get-tuple-element.159.refs_0_, bf16[64,2048]{1,0:T(8,128)(2,1)S(1)} %slice_bitcast_fusion.5.refs_1_, ...), custom_call_target="tpu_custom_call" | custom-call | tf_op jit(solution)/shard_map/exchange_6/pallas_call | solution.py:522
  1040.9 33.5 %exchange_7.1 = (bf16[384,2048]{1,0:T(8,128)(2,1)S(1)}, bf16[256,2048]{1,0:T(8,128)(2,1)S(1)}, bf16[3,2048,256]{2,1,0:T(8,128)(2,1)S(1)}) custom-call(bf16[256,2048]{1,0:T(8,128)(2,1)S(1)} %broadcast_select_fusion.4.refs_0_, bf16[256,2048]{1,0:T(8,128)(2,1)S(1)} %broadcast_select_fusion.2.refs_1_, bf16[64,2048]{1,0:T(8,128)(2,1)S(1)} %fusion.68.refs_2_, ...), custom_call_target="tpu_custom_call" | custom-call | tf_op jit(solution)/shard_map/exchange_7/pallas_call | solution.py:522
  1085.3 7.3 convert_bitcast_fusion
  (356 shorter events, 175.3 us)
Async XLA Ops:
  11.5 198.6 %copy-start.28 = (s32[1,1,4,256]{3,1,2,0:T(1,128)}, s32[1,1,4,256]{3,1,2,0:T(1,128)S(1)}, u32[]{:S(2)}) copy-start(s32[1,1,4,256]{3,1,2,0:T(1,128)S(1)} %copy.62) | copy-start | bytes 12292
  113.1 97.0 %copy-start.35 = (s32[5]{0:T(128)}, s32[5]{0:T(128)S(1)}, u32[]{:S(2)}) copy-start(s32[5]{0:T(128)S(1)} %pad_add_fusion.1.place) | copy-start | bytes 64
  117.5 80.9 %copy-start.8 = (bf16[2048,3,256]{2,0,1:T(8,128)(2,1)S(1)}, bf16[2048,3,256]{2,0,1:T(8,128)(2,1)}, u32[]{:S(2)}) copy-start(bf16[2048,3,256]{2,0,1:T(8,128)(2,1)} %param.27) | copy-start | bytes 9437188
  507.6 124.3 %collective-permute-start.18 = (bf16[256,2048]{1,0:T(8,128)(2,1)}, bf16[256,2048]{1,0:T(8,128)(2,1)}, u32[]{:S(2)}, u32[]{:S(2)}) collective-permute-start(bf16[256,2048]{1,0:T(8,128)(2,1)} %get-tuple-element.155), channel_id=1, source_target_pairs={{0,16},{8,24},{16,0},{24,8},{1,17},{9,25},{17,1},{25,9},{2,18},{10... | collective-permute-start | bytes 3145736 | tf_op jit(solution)/shard_map/ppermute | solution.py:29
  509.1 139.4 %collective-permute-start.17 = (bf16[256,2048]{1,0:T(8,128)(2,1)}, bf16[256,2048]{1,0:T(8,128)(2,1)}, u32[]{:S(2)}, u32[]{:S(2)}) collective-permute-start(bf16[256,2048]{1,0:T(8,128)(2,1)} %get-tuple-element.155), channel_id=1, source_target_pairs={{0,8},{8,0},{16,24},{24,16},{1,9},{9,1},{17,25},{25,17},{2,10},{10... | collective-permute-start | bytes 3145736 | tf_op jit(solution)/shard_map/ppermute | solution.py:29
  519.1 125.5 %collective-permute-start.21 = (bf16[684,1024]{1,0:T(8,128)(2,1)}, bf16[684,1024]{1,0:T(8,128)(2,1)}, u32[]{:S(2)}, u32[]{:S(2)}) collective-permute-start(bf16[684,1024]{1,0:T(8,128)(2,1)} %constant_dynamic-slice_fusion.1), channel_id=1, source_target_pairs={{0,8},{8,0},{16,24},{24,16},{1,9},{9,1},{17,25},{25,17},{2,10},{10... | collective-permute-start | bytes 4202504 | tf_op jit(solution)/shard_map/ppermute | solution.py:29
  528.0 105.8 %collective-permute-start.15 = (bf16[684,1024]{1,0:T(8,128)(2,1)}, bf16[684,1024]{1,0:T(8,128)(2,1)}, u32[]{:S(2)}, u32[]{:S(2)}) collective-permute-start(bf16[684,1024]{1,0:T(8,128)(2,1)} %constant_dynamic-slice_fusion.3), channel_id=1, source_target_pairs={{0,8},{8,0},{16,24},{24,16},{1,9},{9,1},{17,25},{25,17},{2,10},{10... | collective-permute-start | bytes 4202504 | tf_op jit(solution)/shard_map/ppermute | solution.py:29
  566.7 99.9 %collective-permute-start.11 = (bf16[342,2,2048]{2,1,0:T(2,128)(2,1)}, bf16[342,2,2048]{2,1,0:T(2,128)(2,1)}, u32[]{:S(2)}, u32[]{:S(2)}) collective-permute-start(bf16[342,2,2048]{2,1,0:T(2,128)(2,1)} %dynamic-slice_bitcast_fusion.2), channel_id=1, source_target_pairs={{0,8},{8,0},{16,24},{24,16},{1,9},{9,1},{17,25},{25,17},{2,10},{10... | collective-permute-start | bytes 8405000 | tf_op jit(solution)/shard_map/ppermute | solution.py:29
  567.2 22.1 %slice-start = ((s8[5603328]{0:T(1024)(128)(4,1)}), s8[4194304]{0:T(1024)(128)(4,1)S(1)}, s32[]{:S(2)}) async-start(s8[5603328]{0:T(1024)(128)(4,1)} %bitcast.239), calls=%async_computation | async-start | bytes 8388608
  575.6 25.8 %copy-start.67 = (f32[1,1024,684]{1,2,0:T(8,128)}, f32[1,1024,684]{1,2,0:T(8,128)S(1)}, u32[]{:S(2)}) copy-start(f32[1,1024,684]{1,2,0:T(8,128)S(1)} %get-tuple-element.180) | copy-start | bytes 8404996
  575.6 25.8 %copy-start.69 = (f32[1,1024,684]{1,2,0:T(8,128)}, f32[1,1024,684]{1,2,0:T(8,128)S(1)}, u32[]{:S(2)}) copy-start(f32[1,1024,684]{1,2,0:T(8,128)S(1)} %get-tuple-element.181) | copy-start | bytes 8404996
  631.9 16.6 %collective-permute-start.19 = (bf16[256,2048]{1,0:T(8,128)(2,1)}, bf16[256,2048]{1,0:T(8,128)(2,1)}, u32[]{:S(2)}, u32[]{:S(2)}) collective-permute-start(bf16[256,2048]{1,0:T(8,128)(2,1)} %collective-permute-done.18), channel_id=1, source_target_pairs={{0,8},{8,0},{16,24},{24,16},{1,9},{9,1},{17,25},{25,17},{2,10},{10... | collective-permute-start | bytes 3145736 | tf_op jit(solution)/shard_map/ppermute | solution.py:29
  633.8 40.0 %collective-permute-start.10 = (bf16[342,2,2048]{2,1,0:T(2,128)(2,1)}, bf16[342,2,2048]{2,1,0:T(2,128)(2,1)}, u32[]{:S(2)}, u32[]{:S(2)}) collective-permute-start(bf16[342,2,2048]{2,1,0:T(2,128)(2,1)} %dynamic-slice_bitcast_fusion.3), channel_id=1, source_target_pairs={{0,8},{8,0},{16,24},{24,16},{1,9},{9,1},{17,25},{25,17},{2,10},{10... | collective-permute-start | bytes 8405000 | tf_op jit(solution)/shard_map/ppermute | solution.py:29
  645.1 19.0 %collective-permute-start.16 = (bf16[684,512]{1,0:T(8,128)(2,1)}, bf16[684,512]{1,0:T(8,128)(2,1)}, u32[]{:S(2)}, u32[]{:S(2)}) collective-permute-start(bf16[684,512]{1,0:T(8,128)(2,1)} %constant_dynamic-slice_fusion.2), channel_id=1, source_target_pairs={{0,16},{8,24},{16,0},{24,8},{1,17},{9,25},{17,1},{25,9},{2,18},{10... | collective-permute-start | bytes 2101256 | tf_op jit(solution)/shard_map/ppermute | solution.py:29
  652.0 330.8 %collective-permute-start.22 = (bf16[684,512]{1,0:T(8,128)(2,1)}, bf16[684,512]{1,0:T(8,128)(2,1)}, u32[]{:S(2)}, u32[]{:S(2)}) collective-permute-start(bf16[684,512]{1,0:T(8,128)(2,1)} %constant_dynamic-slice_fusion), channel_id=1, source_target_pairs={{0,16},{8,24},{16,0},{24,8},{1,17},{9,25},{17,1},{25,9},{2,18},{10... | collective-permute-start | bytes 2101256 | tf_op jit(solution)/shard_map/ppermute | solution.py:29
  678.5 80.6 %copy-start.48 = (bf16[342,2,2048]{2,1,0:T(2,128)(2,1)}, bf16[342,2,2048]{2,1,0:T(2,128)(2,1)S(1)}, u32[]{:S(2)}) copy-start(bf16[342,2,2048]{2,1,0:T(2,128)(2,1)S(1)} %fusion.3) | copy-start | bytes 8404996
  681.1 80.4 %copy-start.76 = (bf16[512,2048]{1,0:T(8,128)(2,1)S(1)}, bf16[512,2048]{1,0:T(8,128)(2,1)}, u32[]{:S(2)}) copy-start(bf16[512,2048]{1,0:T(8,128)(2,1)} %copy-done.75) | copy-start | bytes 6291460
  770.5 22.0 %copy-start.38 = (bf16[1024,2048]{1,0:T(8,128)(2,1)S(1)}, bf16[1024,2048]{1,0:T(8,128)(2,1)}, u32[]{:S(2)}) copy-start(bf16[1024,2048]{1,0:T(8,128)(2,1)} %copy-done.37) | copy-start | bytes 12582916
  808.4 14.9 %collective-permute-start.23 = (f32[2,2136]{1,0:T(2,128)S(1)}, f32[2,2136]{1,0:T(2,128)S(1)}, u32[]{:S(2)}, u32[]{:S(2)}) collective-permute-start(f32[2,2136]{1,0:T(2,128)S(1)} %maximum_maximum_fusion), channel_id=1, source_target_pairs={{0,8},{8,0},{16,24},{24,16},{1,9},{9,1},{17,25},{25,17},{2,10},{10... | collective-permute-start | bytes 51272 | tf_op jit(solution)/shard_map/ppermute | solution.py:29
  808.6 15.3 %collective-permute-start.26 = (f32[6,2048]{1,0:T(8,128)S(1)}, f32[6,2048]{1,0:T(8,128)S(1)}, u32[]{:S(2)}, u32[]{:S(2)}) collective-permute-start(f32[6,2048]{1,0:T(8,128)S(1)} %pad_maximum_fusion.2), channel_id=1, source_target_pairs={{0,8},{8,0},{16,24},{24,16},{1,9},{9,1},{17,25},{25,17},{2,10},{10... | collective-permute-start | bytes 147464 | tf_op jit(solution)/shard_map/ppermute | solution.py:29
  811.7 69.6 %collective-permute-start.12 = (bf16[2,128,2048]{2,1,0:T(8,128)(2,1)}, bf16[2,128,2048]{2,1,0:T(8,128)(2,1)}, u32[]{:S(2)}, u32[]{:S(2)}) collective-permute-start(bf16[2,128,2048]{2,1,0:T(8,128)(2,1)} %constant_dynamic-slice_fusion.7), channel_id=1, source_target_pairs={{0,8},{8,0},{16,24},{24,16},{1,9},{9,1},{17,25},{25,17},{2,10},{10... | collective-permute-start | bytes 3145736 | tf_op jit(solution)/shard_map/ppermute | solution.py:29
  815.6 67.6 %collective-permute-start.20 = (bf16[171,2,2048]{2,1,0:T(2,128)(2,1)}, bf16[171,2,2048]{2,1,0:T(2,128)(2,1)}, u32[]{:S(2)}, u32[]{:S(2)}) collective-permute-start(bf16[171,2,2048]{2,1,0:T(2,128)(2,1)} %add_convert_fusion.6), channel_id=1, source_target_pairs={{0,4},{1,5},{2,6},{3,7},{4,0},{5,1},{6,2},{7,3},{8,12},{9,13},{10,... | collective-permute-start | bytes 4202504 | tf_op jit(solution)/shard_map/ppermute | solution.py:29
  823.3 27.7 %copy-start.59 = (bf16[3,256,2048]{1,2,0:T(8,128)(2,1)S(1)}, bf16[3,256,2048]{1,2,0:T(8,128)(2,1)}, u32[]{:S(2)}) copy-start(bf16[3,256,2048]{1,2,0:T(8,128)(2,1)} %fusion.26) | copy-start | bytes 9437188
  823.4 5.6 collective-permute-start.24
  824.0 4.3 collective-permute-start.27
  828.3 4.3 collective-permute-start.28
  832.7 16.7 %collective-permute-start.29 = (f32[6,2048]{1,0:T(8,128)S(1)}, f32[6,2048]{1,0:T(8,128)S(1)}, u32[]{:S(2)}, u32[]{:S(2)}) collective-permute-start(f32[6,2048]{1,0:T(8,128)S(1)} %add.323), channel_id=1, source_target_pairs={{0,2},{1,3},{2,0},{3,1},{4,6},{5,7},{6,4},{7,5},{8,10},{9,11},{10,... | collective-permute-start | bytes 147464 | tf_op jit(solution)/shard_map/ppermute | solution.py:29
  833.4 45.4 %collective-permute-start.25 = (f32[2136]{0:T(1024)S(1)}, f32[2136]{0:T(1024)S(1)}, u32[]{:S(2)}, u32[]{:S(2)}) collective-permute-start(f32[2136]{0:T(1024)S(1)} %get-tuple-element.174), channel_id=1, source_target_pairs={{0,4},{1,5},{2,6},{3,7},{4,0},{5,1},{6,2},{7,3},{8,12},{9,13},{10,... | collective-permute-start | bytes 25640 | tf_op jit(solution)/shard_map/ppermute | solution.py:29
  849.3 30.7 %collective-permute-start.30 = (f32[6,2048]{1,0:T(8,128)S(1)}, f32[6,2048]{1,0:T(8,128)S(1)}, u32[]{:S(2)}, u32[]{:S(2)}) collective-permute-start(f32[6,2048]{1,0:T(8,128)S(1)} %add.324), channel_id=1, source_target_pairs={{0,4},{1,5},{2,6},{3,7},{4,0},{5,1},{6,2},{7,3},{8,12},{9,13},{10,... | collective-permute-start | bytes 147464 | tf_op jit(solution)/shard_map/ppermute | solution.py:29
  852.2 31.0 %copy-start.24 = (bf16[171,2,2048]{2,1,0:T(2,128)(2,1)S(1)}, bf16[171,2,2048]{2,1,0:T(2,128)(2,1)}, u32[]{:S(2)}) copy-start(bf16[171,2,2048]{2,1,0:T(2,128)(2,1)} %copy-done.23) | copy-start | bytes 4202500
  878.8 9.3 collective-permute-start.13
  880.1 10.2 collective-permute-start.14
  (87 other events, 426.2 us)

commit v3 on v2

--- a/solution.py
+++ b/solution.py
@@ -50,6 +50,7 @@
 
 
 ROW_TILE = 16
+UP1, UP2, UP4, UP5 = 2, 2, 2, 2
 
 
 def row_tiles(count, body):
@@ -96,11 +97,6 @@
         if offset & bit:
             index = partner(index, bit)
     return index
-
-
-def mirrored(index, count):
-    bits = bits_of(count)
-    return sum(((index // bit) % 2) * (count // (2 * bit)) for bit in bits)
 
 
 def dp_copies(n_dp):
@@ -140,18 +136,31 @@
 
 
 class Cargo:
-    def __init__(self, inputs, outputs, count, run):
+    def __init__(self, inputs, outputs, count, run, early=0, from_out=None):
         self.inputs, self.outputs, self.count, self.run = inputs, outputs, count, run
-
-
-def send_share(weight, axis, n_dp):
+        self.early, self.from_out = early, from_out
+
+    def sooner(self, count=1):
+        self.early = count
+        return self
+
+
+def portion_bounds(part, last_axis, portion):
+    if portion is None:
+        return 0, part
+    cut = part // 2 // 128 * 128 if last_axis else part // 2
+    return ((0, cut), (cut, part))[portion]
+
+
+def send_share(weight, axis, n_dp, portion=None):
     part = weight.shape[axis] // n_dp
+    low, high = portion_bounds(part, axis == weight.ndim - 1, portion)
     shape = list(weight.shape)
-    shape[axis] = part
+    shape[axis] = high - low
 
     def run(ship, ins, outs):
         c = ship.far(
-            along(ins[0], axis, ship.d * part, part),
+            along(ins[0], axis, ship.d * part + low, high - low),
             outs[0],
             "tensor",
             partner(ship.t, ship.width),
@@ -164,19 +173,38 @@
     return Cargo([weight], [(tuple(shape), weight.dtype)], 1, run)
 
 
-def join_shares(share, axis, n_dp):
-    part = share.shape[axis]
-    shape = list(share.shape)
-    shape[axis] = part * n_dp
+def join_shares(weight, share, axis, n_dp, portion=None):
+    part = weight.shape[axis] // n_dp
+    cut = share.shape[axis]
 
     def run(ship, ins, outs):
-        view = lambda i: along(outs[0], axis, i * part, part)
-        put = ship.near(ins[0], view(ship.d), ship.slots(1))
+        first = lambda i: along(outs[0], axis, i * part, cut)
+        second = lambda i: along(outs[0], axis, i * part + cut, part - cut)
+        steps = [dp_steps(ship, first, first=ins[0])]
+        put = ship.near(ins[0], first(ship.d), ship.slots(1))
         put.start()
-        yield from dp_steps(ship, view, first=ins[0])
+        if cut < part:
+            c = ship.far(
+                along(ins[1], axis, ship.d * part + cut, part - cut),
+                second(ship.d),
+                "tensor",
+                partner(ship.t, ship.width),
+                ship.slots(1),
+            )
+            c.start()
+        next(steps[0])
+        yield
+        if cut < part:
+            c.wait()
+            steps.append(dp_steps(ship, second))
+        while steps:
+            steps = [g for g in steps if next(g, g) is not g]
+            if steps:
+                yield
         put.wait()
 
-    return Cargo([share], [(tuple(shape), share.dtype)], 1 + dp_copies(n_dp), run)
+    inputs = [share] + ([weight] if cut < part else [])
+    return Cargo(inputs, [(weight.shape, weight.dtype)], 2 + 2 * dp_copies(n_dp), run)
 
 
 def fetch(weight, axis, n_dp):
@@ -199,6 +227,13 @@
     return Cargo([weight], [(weight.shape, weight.dtype)], 1 + dp_copies(n_dp), run)
 
 
+def present(array):
+    def run(ship, ins, outs):
+        yield
+
+    return Cargo([array], [], 0, run)
+
+
 def swap_cargo(array, axis, bit):
     def run(ship, ins, outs):
         index = ship.d if axis == "dp" else ship.t
@@ -216,7 +251,7 @@
     shape[axis] = part * n_dp
 
     def run(ship, ins, outs):
-        view = lambda i: along(outs[0], axis, mirrored(i, n_dp) * part, part)
+        view = lambda i: along(outs[0], axis, i * part, part)
         put = ship.near(ins[0], view(ship.d), ship.slots(1))
         put.start()
         yield from dp_steps(ship, view, first=ins[0])
@@ -225,7 +260,7 @@
     return Cargo([share], [(tuple(shape), share.dtype)], 1 + dp_copies(n_dp), run)
 
 
-def rows_dp(array, n_dp, upper=True):
+def rows_dp(array, n_dp, upper=True, from_out=None):
     def run(ship, ins, outs):
         view = lambda i: outs[0].at[i]
         only = ship.h >= int(upper)
@@ -241,62 +276,81 @@
         def _():
             ship.near(ins[0], view(ship.d), k).wait()
 
-    return Cargo([array], [((n_dp,) + array.shape, array.dtype)], 1 + dp_copies(n_dp), run)
+    outputs = [((n_dp,) + array.shape, array.dtype)]
+    inputs = [array] if from_out is None else []
+    return Cargo(inputs, outputs, 1 + dp_copies(n_dp), run, from_out=from_out)
+
+
+@functools.lru_cache
+def move_plan(size):
+    width = size // 2
+    moves, tables = [], []
+    for slot in range(CAP):
+        owners = range(width if slot else 0, size if slot else width)
+        room = {t: [0, 1] for t in owners}
+        table = [[0, 0] for _ in range(width)]
+        away = []
+
+        def put(j, target):
+            b = slot * size + j
+            place = room[target].pop(0)
+            table[target % width][place] = j
+            moves.append((slot // 2, b // CAP, b % CAP, target, place))
+
+        for j in range(size):
+            at = (slot * size + j) // CAP
+            if room.get(at):
+                put(j, at)
+            else:
+                away.append((j, at))
+        for j, at in away:
+            put(j, min((t for t in owners if room[t]), key=lambda t: (popcount(t ^ at), t)))
+        tables.append(table)
+    return tuple(moves), tables
+
+
+def at_device(t, number, body):
+    pl.when(t == number)(body)
 
 
 def spread_cargo(array, n_dp, n_tensor):
     block = array.shape[0] // CAP
     model = array.shape[1]
+    moves, _ = move_plan(n_tensor)
 
     def run(ship, ins, outs):
-        source = ins[0]
         item, third = outs
         t, d = ship.t, ship.d
         base = ship.slots(4)
 
-        def block_copy(i, start):
-            b = CAP * t + i
-            j = b % n_tensor
-            target = jnp.where(b >= n_tensor, ship.width, 0) + j // 2
-            at = j % 2
-            rows = step(source, i * block, block)
-            for kind in range(2):
-                here = b >= 2 * n_tensor if kind else b < 2 * n_tensor
-                into = step(third.at[d] if kind else item, at * block, block)
-
-                @pl.when(here & (target == t))
-                def _():
-                    c = ship.near(rows, into, base + i)
-                    c.start() if start else c.wait()
-
-                @pl.when(here & (target != t))
-                def _():
-                    c = ship.far(rows, into, "tensor", target, base + i, base + 2 * kind + at)
-                    c.start() if start else c.wait_send()
-
-        def wait_place(kind, at):
-            b = (2 if kind else ship.h) * n_tensor + 2 * ship.q + at
-
-            @pl.when(b // CAP != t)
-            def _():
-                into = step(third.at[d] if kind else item, at * block, block)
-                ship.far(into, into, "tensor", t, base, base + 2 * kind + at).wait_recv()
-
-        for i in reversed(range(CAP)):
-            block_copy(i, True)
+        def into(kind, place):
+            return step(third.at[d] if kind else item, place * block, block)
+
+        def copy(move):
+            kind, source, i, target, place = move
+            rows = step(ins[0], i * block, block)
+            if source == target:
+                return ship.near(rows, into(kind, place), base + i)
+            return ship.far(rows, into(kind, place), "tensor", target, base + i, base + 2 * kind + place)
+
+        def visit(chosen, action):
+            for number in range(n_tensor):
+                mine = [m for m in moves if chosen(m, number)]
+                if mine:
+                    at_device(t, number, lambda mine=mine: [action(copy(m)) for m in mine] and None)
+
+        start, wait = (lambda c: c.start()), (lambda c: c.wait())
+        came, left = (lambda c: c.wait_recv()), (lambda c: c.wait_send())
+        stays = lambda m: m[1] == m[3]
+        visit(lambda m, n: m[1] == n and m[0] == 1, start)
+        visit(lambda m, n: m[1] == n and m[0] == 0, start)
         yield
-        for i in range(CAP):
-            block_copy(i, False)
-        only = ship.h == 1
-
-        @pl.when(only)
-        def _():
-            for at in range(2):
-                wait_place(1, at)
-
-        yield from dp_steps(ship, lambda i: third.at[i], only=only)
-        for at in range(2):
-            wait_place(0, at)
+        visit(lambda m, n: m[3] == n and m[0] == 1 and not stays(m), came)
+        visit(lambda m, n: m[3] == n and m[0] == 1 and stays(m), wait)
+        yield from dp_steps(ship, lambda i: third.at[i], only=ship.h == 1)
+        visit(lambda m, n: m[3] == n and m[0] == 0 and not stays(m), came)
+        visit(lambda m, n: m[3] == n and m[0] == 0 and stays(m), wait)
+        visit(lambda m, n: m[1] == n and not stays(m), left)
 
     outputs = [((2 * block, model), array.dtype), ((n_dp, 2 * block, model), array.dtype)]
     return Cargo([array], outputs, 4 + dp_copies(n_dp), run)
@@ -305,50 +359,58 @@
 def return_cargo(item, third, n_tensor):
     block = item.shape[0] // 2
     model = item.shape[1]
+    moves, _ = move_plan(n_tensor)
 
     def run(ship, ins, outs):
         t = ship.t
         base = ship.slots(4)
 
-        def send(kind, at, start):
-            b = (2 if kind else ship.h) * n_tensor + 2 * ship.q + at
-            target, i = b // CAP, b % CAP
-            rows = step(ins[kind], at * block, block)
-            into = step(outs[0], i * block, block)
-
-            @pl.when(target == t)
-            def _():
-                c = ship.near(rows, into, base + 2 * kind + at)
-                c.start() if start else c.wait()
-
-            @pl.when(target != t)
-            def _():
-                c = ship.far(rows, into, "tensor", target, base + 2 * kind + at, base + i)
-                c.start() if start else c.wait_send()
-
-        def all_sends(start):
-            for at in range(2):
-                send(0, at, start)
-
-            @pl.when(ship.h == 1)
-            def _():
-                for at in range(2):
-                    send(1, at, start)
-
-        all_sends(True)
+        def copy(move):
+            kind, target, i, holder, place = move
+            rows = step(ins[kind], place * block, block)
+            to = step(outs[0], i * block, block)
+            k = base + 2 * kind + place
+            if holder == target:
+                return ship.near(rows, to, k)
+            return ship.far(rows, to, "tensor", target, k, base + i)
+
+        def visit(chosen, action):
+            for number in range(n_tensor):
+                mine = [m for m in moves if chosen(m, number)]
+                if mine:
+                    at_device(t, number, lambda mine=mine: [action(copy(m)) for m in mine] and None)
+
+        stays = lambda m: m[1] == m[3]
+        visit(lambda m, n: m[3] == n, lambda c: c.start())
         yield
-        for i in range(CAP):
-            b = CAP * t + i
-            holder = jnp.where(b >= n_tensor, ship.width, 0) + (b % n_tensor) // 2
-
-            @pl.when(holder != t)
-            def _():
-                into = step(outs[0], i * block, block)
-                ship.far(into, into, "tensor", t, base, base + i).wait_recv()
-
-        all_sends(False)
+        visit(lambda m, n: m[1] == n and not stays(m), lambda c: c.wait_recv())
+        visit(lambda m, n: m[3] == n and stays(m), lambda c: c.wait())
+        visit(lambda m, n: m[3] == n and not stays(m), lambda c: c.wait_send())
 
     return Cargo([item, third], [((CAP * block, model), item.dtype)], 4, run)
+
+
+def gather_tensor(array, n_tensor, cut=False):
+    share = array.shape[1] // n_tensor if cut else array.shape[1]
+
+    def run(ship, ins, outs):
+        base = ship.slots(n_tensor)
+        part = lambda i: along(ins[0], 1, i * share, share) if cut else ins[0]
+        put = ship.near(part(ship.t), outs[0].at[ship.t], base)
+        put.start()
+        others = [(k, (ship.t + k) % n_tensor) for k in range(1, n_tensor)]
+        copies = [
+            ship.far(part(other), outs[0].at[ship.t], "tensor", other, base + k) for k, other in others
+        ]
+        for c in copies:
+            c.start()
+        yield
+        for c in copies:
+            c.wait()
+        put.wait()
+
+    shape = (n_tensor, array.shape[0], share)
+    return Cargo([array], [(shape, array.dtype)], n_tensor, run)
 
 
 def exchange(
@@ -363,10 +425,12 @@
     scatter=False,
     gather=False,
     cargo=(),
+    upper_part=2,
     vmem_mib=40,
 ):
     width = n_tensor // 2
-    half = rows // 2
+    cut = rows // upper_part
+    begins, sizes = (0, cut), (cut, rows - cut)
     pieces = [(o, hs) for o in range(1, width) for hs in range(2)]
     number = {piece: k for k, piece in enumerate(pieces)}
     bits = bits_of(width)
@@ -413,13 +477,23 @@
             )
         pl.semaphore_wait(barrier, len(greeted))
 
-        stages = []
+        stages, waiting, soon = [], [], []
         for c in cargo:
             c_ins, cargo_ins = cargo_ins[: len(c.inputs)], cargo_ins[len(c.inputs) :]
             c_outs, cargo_outs = cargo_outs[: len(c.outputs)], cargo_outs[len(c.outputs) :]
-            stages.append(c.run(ship, c_ins, c_outs))
-        for stage in stages:
-            next(stage)
+            if c.from_out is None:
+                stage = c.run(ship, c_ins, c_outs)
+                next(stage)
+                stages.append(stage)
+                soon.append([stage, c.early])
+            else:
+                waiting.append(c.run(ship, [outs[c.from_out]], c_outs))
+
+        def advance():
+            for entry in soon:
+                if entry[1]:
+                    entry[1] -= 1
+                    next(entry[0])
 
         if scatter:
             part = ins[0]
@@ -427,12 +501,12 @@
             for piece in scatter_order:
                 o, hs = piece
                 came = incoming(piece)
-                base = o * rows + hs * half
+                base, half = o * rows + begins[hs], sizes[hs]
                 for p in came:
                     copies[p].wait_recv()
                 source = step(part, base, half)
                 if came:
-                    source = arrived.at[number[came[0]]]
+                    source = step(arrived.at[number[came[0]]], 0, half)
 
                     def add(r, base=base, came=came):
                         total = part[pl.ds(base + r, ROW_TILE)].astype(f32)
@@ -444,43 +518,51 @@
                 k = number[piece]
                 copies[piece] = pltpu.make_async_remote_copy(
                     src_ref=source,
-                    dst_ref=arrived.at[k],
+                    dst_ref=step(arrived.at[k], 0, half),
                     send_sem=s_send.at[k],
                     recv_sem=s_recv.at[k],
                     device_id={"tensor": partner(t, last_bit(piece))},
                     device_id_type=pl.DeviceIdType.MESH,
                 )
                 copies[piece].start()
+            advance()
             for piece in pieces:
                 if popcount(piece[0]) == 1:
                     copies[piece].wait_recv()
 
         def summed(hs, r):
-            total = ins[0][pl.ds(hs * half + r, ROW_TILE)].astype(f32)
+            total = ins[0][pl.ds(begins[hs] + r, ROW_TILE)].astype(f32)
             for bit in bits:
                 total = total + arrived[number[(bit, hs)], pl.ds(r, ROW_TILE)].astype(f32)
             return total
 
         if middle is not None:
-            middle(half, summed, ins, outs, own)
+            middle((begins, sizes), summed, ins, outs, own)
+        for stage in waiting:
+            next(stage)
+        stages = waiting + stages
 
         if gather:
             keep = pltpu.make_async_copy(own, step(gathered, 0, rows), local_sem)
             keep.start()
             sent = {}
+            forwarding = False
             for piece in gather_order:
                 o, hs = piece
                 bit = last_bit(piece)
                 before = o ^ bit
+                if before and not forwarding:
+                    forwarding = True
+                    advance()
                 if before:
                     sent[(before, hs)].wait_recv()
-                    source = step(gathered, before * rows + hs * half, half)
+                    source = step(gathered, before * rows + begins[hs], sizes[hs])
                 else:
-                    source = step(own, hs * half, half)
+                    source = step(own, begins[hs], sizes[hs])
                 k = number[piece]
                 sent[piece] = pltpu.make_async_remote_copy(
                     src_ref=source,
-                    dst_ref=step(gathered, o * rows + hs * half, half),
+                    dst_ref=step(gathered, o * rows + begins[hs], sizes[hs]),
                     send_sem=g_send.at[k],
                     recv_sem=g_recv.at[k],
                     device_id={"tensor": partner(t, bit)},
@@ -513,7 +595,7 @@
     count = len(pieces)
     if scatter:
         scratch += [
-            pltpu.VMEM((count, half, model), bf16),
+            pltpu.VMEM((count, max(sizes), model), bf16),
             pltpu.SemaphoreType.DMA((count,)),
             pltpu.SemaphoreType.DMA((count,)),
         ]
@@ -552,23 +634,24 @@
     return scale_inv * (centred - normed * jnp.mean(grad_normed * normed, -1, keepdims=True))
 
 
-def each_tile(half, body):
+def each_tile(parts, body):
+    begins, sizes = parts
     for hs in range(2):
-        row_tiles(half, lambda r, hs=hs: body(hs, r, pl.ds(hs * half + r, ROW_TILE)))
+        row_tiles(sizes[hs], lambda r, hs=hs: body(hs, r, pl.ds(begins[hs] + r, ROW_TILE)))
 
 
 def fold(values):
     return jnp.sum(values.reshape(-1, 8, values.shape[-1]), 0)
 
 
-def gather_middle(half, summed, ins, outs, own):
+def gather_middle(parts, summed, ins, outs, own):
     def body(hs, r, at):
         own[at] = ins[0][at]
 
-    each_tile(half, body)
-
-
-def first_middle(half, summed, ins, outs, own):
+    each_tile(parts, body)
+
+
+def first_middle(parts, summed, ins, outs, own):
     _, tokens, b_out, gain, shift = ins
 
     def body(hs, r, at):
@@ -577,10 +660,10 @@
         normed, _ = norm_tile(first)
         own[at] = (normed * gain[...] + shift[...]).astype(bf16)
 
-    each_tile(half, body)
-
-
-def second_middle(half, summed, ins, outs, own):
+    each_tile(parts, body)
+
+
+def second_middle(parts, summed, ins, outs, own):
     _, first_sum, cotangent, b_down, gain_one, shift_one, gain_two, shift_two = ins
     layer_rows, grad_second, sums = outs
     sums[...] = jnp.zeros_like(sums)
@@ -599,10 +682,10 @@
         sums[1] += fold(grad)
         sums[2] += fold(back)
 
-    each_tile(half, body)
-
-
-def third_middle(half, summed, ins, outs, own):
+    each_tile(parts, body)
+
+
+def third_middle(parts, summed, ins, outs, own):
     _, first_sum, grad_second, gain_one = ins
     grad_first, sums = outs
     sums[...] = jnp.zeros_like(sums)
@@ -617,16 +700,16 @@
         sums[1] += fold(grad)
         sums[2] += fold(back)
 
-    each_tile(half, body)
-
-
-def last_middle(half, summed, ins, outs, own):
+    each_tile(parts, body)
+
+
+def last_middle(parts, summed, ins, outs, own):
     _, grad_first = ins
 
     def body(hs, r, at):
         outs[0][at] = (summed(hs, r) + deep_alpha * grad_first[at]).astype(bf16)
 
-    each_tile(half, body)
+    each_tile(parts, body)
 
 
 def pick(index, values):
@@ -648,17 +731,16 @@
     return vectors * cos_table + pltpu.roll(vectors, HD // 2, 1) * sin_table
 
 
-def score_tile(queries, keys, base, key_at, prefix_len):
+def score_tile(queries, keys, query_at, key_at, prefix_len):
     scores = lax.dot_general(
         queries, keys, (((1,), (1,)), ((), ())), preferred_element_type=f32
     ) * HD ** (-0.5)
-    query_at = base + lax.broadcasted_iota(jnp.int32, (queries.shape[0], 1), 0)
     allowed = (key_at < prefix_len) | (key_at <= query_at)
     return jnp.where(allowed, scores, negative)
 
 
 def attend_kernel(
-    heads, rows, place, own, other, bias, cos_table, sin_table, key_at, turned, context
+    heads, rows, place, own, other, bias, cos_table, sin_table, key_at, query_at, turned, context
 ):
     prefix_len = place[0]
     size = heads * HD
@@ -679,7 +761,7 @@
             scores = score_tile(
                 turned[run, at : at + HD],
                 turned[:, size + at : size + at + HD],
-                place[1 + i],
+                query_at[run],
                 key_at[...],
                 prefix_len,
             )
@@ -693,7 +775,7 @@
         lax.fori_loop(0, LEN // rows, one_block, 0)
 
 
-def attend(linear, bias, place, cos_table, sin_table, key_at, rows):
+def attend(linear, bias, place, cos_table, sin_table, key_at, query_at, rows):
     size = 2 * 3 * linear[0].shape[2]
     heads = size // (3 * HD)
     vmem = pl.BlockSpec(memory_space=pltpu.VMEM)
@@ -703,15 +785,27 @@
             jax.ShapeDtypeStruct((LEN, size), bf16),
             jax.ShapeDtypeStruct((LEN, size // 3), bf16),
         ],
-        in_specs=[pl.BlockSpec(memory_space=pltpu.SMEM)] + [vmem] * 6,
+        in_specs=[pl.BlockSpec(memory_space=pltpu.SMEM)] + [vmem] * 7,
         out_specs=[vmem] * 2,
         compiler_params=pltpu.CompilerParams(vmem_limit_bytes=40 << 20),
         name="attend",
-    )(place, *linear, bias, cos_table, sin_table, key_at)
+    )(place, *linear, bias, cos_table, sin_table, key_at, query_at)
 
 
 def attend_back_kernel(
-    heads, rows, place, turned, grad_context, cos_table, sin_table, key_at, own, other, dk, dv
+    heads,
+    rows,
+    place,
+    turned,
+    grad_context,
+    cos_table,
+    sin_table,
+    key_at,
+    query_at,
+    own,
+    other,
+    dk,
+    dv,
 ):
     prefix_len = place[0]
     size = heads * HD
@@ -730,7 +824,7 @@
             run = pl.ds(pl.multiple_of(i * rows, rows), rows)
             queries = turned[run, at : at + HD]
             keys = turned[:, size + at : size + at + HD]
-            scores = score_tile(queries, keys, place[1 + i], key_at[...], prefix_len)
+            scores = score_tile(queries, keys, query_at[run], key_at[...], prefix_len)
             raw = jnp.exp(scores - jnp.max(scores, -1, keepdims=True))
             probs = raw / jnp.sum(raw, -1, keepdims=True)
             grad = grad_context[run, at : at + HD]
@@ -755,19 +849,39 @@
         grad_linear[2, :, came] = dv[...].astype(bf16)
 
 
-def attend_back(turned, grad_context, place, cos_table, sin_table, key_at, rows):
+def attend_back(turned, grad_context, place, cos_table, sin_table, key_at, query_at, rows):
     size = turned.shape[1]
     heads = size // (3 * HD)
     vmem = pl.BlockSpec(memory_space=pltpu.VMEM)
     return pl.pallas_call(
         functools.partial(attend_back_kernel, heads, rows),
         out_shape=[jax.ShapeDtypeStruct((3, LEN, size // 6), bf16)] * 2,
-        in_specs=[pl.BlockSpec(memory_space=pltpu.SMEM)] + [vmem] * 5,
+        in_specs=[pl.BlockSpec(memory_space=pltpu.SMEM)] + [vmem] * 6,
         out_specs=[vmem] * 2,
         scratch_shapes=[pltpu.VMEM((LEN, HD), f32), pltpu.VMEM((LEN, HD), f32)],
         compiler_params=pltpu.CompilerParams(vmem_limit_bytes=40 << 20),
         name="attend_back",
-    )(place, turned, grad_context, cos_table, sin_table, key_at)
+    )(place, turned, grad_context, cos_table, sin_table, key_at, query_at)
+
+
+def interleave_kernel(gate, up, out):
+    out[:, 0, :] = gate[...].astype(f32)
+    out[:, 1, :] = up[...].astype(f32)
+
+
+def interleave(gate, up):
+    count, model = gate.shape
+    size = 64
+    block = pl.BlockSpec((size, model), lambda i: (i, 0))
+    return pl.pallas_call(
+        interleave_kernel,
+        grid=(pl.cdiv(count, size),),
+        in_specs=[block, block],
+        out_specs=pl.BlockSpec((size, 2, model), lambda i: (i, 0, 0)),
+        out_shape=jax.ShapeDtypeStruct((count, 2, model), f32),
+        compiler_params=pltpu.CompilerParams(vmem_limit_bytes=24 << 20),
+        name="interleave",
+    )(gate, up)
 
 
 def on_device(
@@ -798,7 +912,6 @@
     q = t % width
     rows = LEN // width
     model = tokens.shape[1]
-    block = LEN // n_tensor
 
     counts = jnp.sum((cluster[None, :] == jnp.arange(n_dp)[:, None]).astype(jnp.int32), 1)
     spare = jnp.maximum(2 - counts, 0)
@@ -828,8 +941,8 @@
         item = lax.cond(any_empty, with_empty, lambda v: v, item)
         return jnp.where((h == 1) & foreign, third[source_here], item)
 
-    def sorted_out(item, everywhere, absolute):
-        third = everywhere[out_index if absolute else d ^ out_index]
+    def sorted_out(item, everywhere):
+        third = everywhere[out_index]
 
         def with_empty(third):
             other = across(permute(item, "tensor", n_tensor, width), n_dp)
@@ -859,33 +972,46 @@
     swap = functools.partial(exchange, n_dp=n_dp, n_tensor=n_tensor, rows=rows, model=model)
     facts = jnp.stack([prefix, span_offset])
 
-    _, (spread_tokens, (wq_other,), (facts_all,), (bq_other,), (bg_other,)) = swap(
+    _, (spread_tokens, (wq_share,), (facts_all,), (bq_other,), (bg_other,)) = swap(
         0,
         cargo=[
             spread_cargo(tokens, n_dp, n_tensor),
-            fetch(wq, 1, n_dp),
+            send_share(wq, 1, n_dp, 0),
             rows_dp(tile_of(facts), n_dp, upper=False),
             swap_cargo(tile_of(b_qkv), "tensor", width),
             swap_cargo(tile_of(b_gu), "tensor", width),
         ],
     )
-    wq = [wq, wq_other]
     bq = jnp.stack([b_qkv, bq_other[:3, :width_qkv]])
     bg = [b_gu, bg_other[:2, :width_ffn]]
     facts_all = facts_all[:, :2, :CAP]
     own_tokens = chosen(*spread_tokens)
-    (tokens_all,), ((wo_other,), (wg_share,)) = swap(
+    (tokens_all,), ((wq_other,), (wo_other,)) = swap(
         1,
+        upper_part=UP1,
         inputs=[own_tokens],
         middle=gather_middle,
         gather=True,
-        cargo=[fetch(w_out, 0, n_dp), send_share(wg, cut_ffn, n_dp)],
-    )
+        cargo=[
+            join_shares(wq, wq_share, 1, n_dp, 1).sooner(1),
+            fetch(w_out, 0, n_dp),
+        ],
+    )
+    wq = [wq, wq_other]
+    wd_part = model // n_dp
+    wd_share = lax.dynamic_slice_in_dim(w_down, d * wd_part, wd_part, 1)
+    wg_part = wg.shape[cut_ffn] // n_dp
+    wg_low, wg_high = portion_bounds(wg_part, cut_ffn == 2, 0)
+    wg_share = lax.dynamic_slice_in_dim(wg, d * wg_part + wg_low, wg_high - wg_low, cut_ffn)
+    wg_share, wd_share, tokens_all = lax.optimization_barrier((wg_share, wd_share, tokens_all))
+    wg_share, wd_share = flipped(wg_share), flipped(wd_share)
     fact = jnp.where(foreign, facts_all[source_here][:, 2], jnp.where(h == 0, facts[:, 0], facts[:, 1]))
     prefix_len, span_start = fact[0], fact[1]
 
-    starts = (q ^ jnp.arange(width)) * rows
-    position = (starts[:, None] + jnp.arange(rows)[None, :]).reshape(LEN)
+    block = LEN // n_tensor
+    tables = jnp.asarray(move_plan(n_tensor)[1], jnp.int32)
+    starts = tables[jnp.where(foreign, CAP - 1, h)][q ^ jnp.arange(width)].reshape(n_tensor) * block
+    position = (starts[:, None] + jnp.arange(block)[None, :]).reshape(LEN)
     placed = jnp.where(position < prefix_len, position, span_start + position - prefix_len).astype(f32)
     frequency = theta_base ** (-(jnp.arange(HD // 2).astype(f32) * 2.0 / HD))
     angles = placed[:, None] * frequency[None, :]
@@ -893,7 +1019,8 @@
     cos_table = jnp.concatenate([cos_half, cos_half], 1)
     sin_table = jnp.concatenate([-sin_half, sin_half], 1)
     key_at = position[None, :].astype(jnp.int32)
-    place = jnp.concatenate([prefix_len[None], starts]).astype(jnp.int32)
+    query_at = position[:, None].astype(jnp.int32)
+    place = prefix_len[None].astype(jnp.int32)
 
     def dot(a, b):
         return jnp.dot(a, b, preferred_element_type=f32)
@@ -904,20 +1031,21 @@
 
     wo = jnp.concatenate([w_out, wo_other], 0)
     linear = [jnp.einsum("td,cdn->ctn", tokens_all, wq[p], preferred_element_type=f32) for p in pairs]
-    turned, context = attend(linear, bq, place, cos_table, sin_table, key_at, rows)
+    turned, context = attend(linear, bq, place, cos_table, sin_table, key_at, query_at, rows)
     partial_out = dot(context, wo).astype(bf16)
     full = ((rows, model), f32)
-    (first_sum, hidden_all), (spread_cotangent, (wg_other,), (wd_other,)) = swap(
+    (first_sum, hidden_all), ((wg_other,), (wd_other,), spread_cotangent) = swap(
         2,
+        upper_part=UP2,
         inputs=[partial_out, own_tokens, row(b_out), row(gain_one), row(shift_one)],
         outputs=[full],
         middle=first_middle,
         scatter=True,
         gather=True,
         cargo=[
-            spread_cargo(cotangent, n_dp, n_tensor),
-            join_shares(wg_share, cut_ffn, n_dp),
-            fetch(w_down, 1, n_dp),
+            join_shares(wg, wg_share, cut_ffn, n_dp, 1).sooner(2),
+            join_shares(w_down, wd_share, 1, n_dp).sooner(1),
+            spread_cargo(cotangent, n_dp, n_tensor).sooner(2),
         ],
     )
     wg = [wg, wg_other]
@@ -937,7 +1065,8 @@
         pull.append(pull_act)
     partial_fed = sum_of("tn,nd->td", inner, wd)
     sums_shape = ((3, 8, model), f32)
-    (layer_rows, grad_second, sums_two, grad_fed_all), _ = swap(
+    layer_shape = jax.ShapeDtypeStruct((rows, model), bf16)
+    (layer_rows, grad_second, sums_two, grad_fed_all), ((layer_everywhere,),) = swap(
         3,
         inputs=[
             partial_fed,
@@ -953,29 +1082,31 @@
         middle=second_middle,
         scatter=True,
         gather=True,
-    )
-
-    def halve(value, axis, bit):
-        part = value.shape[axis] // 2
-        upper = ((d & bit) != 0).astype(jnp.int32)
-        return (
-            lax.dynamic_slice_in_dim(value, upper * part, part, axis),
-            lax.dynamic_slice_in_dim(value, (1 - upper) * part, part, axis),
-        )
+        cargo=[rows_dp(layer_shape, n_dp, from_out=0)],
+    )
 
     def add(a, b):
         return (a.astype(f32) + b.astype(f32)).astype(bf16)
 
     dp_bits = bits_of(n_dp)
 
-    def dot_rows(a, b):
-        return lax.dot_general(a, b, (((0,), (0,)), ((), ())), preferred_element_type=f32)
-
-    def halve_first(value, axis):
-        for bit in dp_bits[:-1]:
-            keep, send = halve(value, axis, bit)
-            value = add(keep, permute(send, "dp", n_dp, bit))
-        return halve(value, axis, dp_bits[-1])
+    share = model // n_dp
+
+    def columns_of(array):
+        return [lax.dynamic_slice_in_dim(array, (d ^ o) * share, share, 1) for o in range(n_dp)]
+
+    def halve(columns, make, axis):
+        odd = range(1, n_dp, 2)
+        sent = make(jnp.concatenate([columns[o] for o in odd], 1)).astype(bf16)
+        came = permute(sent, "dp", n_dp, 1)
+        pieces = {}
+        for k, o in enumerate(odd):
+            piece = lax.slice_in_dim(came, k * share, (k + 1) * share, axis=axis)
+            pieces[o - 1] = (make(columns[o - 1]) + piece.astype(f32)).astype(bf16)
+        for bit in dp_bits[1:-1]:
+            for o in [o for o in pieces if o & bit]:
+                pieces[o ^ bit] = add(pieces[o ^ bit], permute(pieces.pop(o), "dp", n_dp, bit))
+        return pieces[0], pieces[dp_bits[-1]]
 
     def across_dp(value):
         return swap_cargo(value, "dp", dp_bits[-1])
@@ -988,106 +1119,129 @@
         for p in pairs
     ]
 
-    def halve_pair(values, axis):
-        halves = [halve_first(v.astype(bf16), axis) for v in values]
-        return [x[0] for x in halves], [x[1] for x in halves]
-
-    grad_w_gu = [
-        jnp.einsum("td,ctn->ncd", hidden_all, grad_gate_up[p], preferred_element_type=f32)
-        for p in pairs
-    ]
-    gu_keep, gu_send = halve_pair(grad_w_gu, cut_ffn)
-    grad_w_down = [
-        jnp.einsum("tn,td->nd", inner[p], grad_fed_all, preferred_element_type=f32) for p in pairs
-    ]
-    down_keep, down_send = halve_pair(grad_w_down, 1)
+    hidden_columns = columns_of(hidden_all)
+    fed_columns = columns_of(grad_fed_all)
+
+    def ein(spec, a):
+        return lambda b: jnp.einsum(spec, a, b, preferred_element_type=f32)
+
+    down_keep, down_send = zip(*[halve(fed_columns, ein("tn,td->nd", inner[p]), 1) for p in pairs])
+    gu_keep, gu_send = zip(
+        *[
+            halve(hidden_columns, ein("tn,td->nd", grad_gate_up[p][c]), 1)
+            for p in pairs
+            for c in range(2)
+        ]
+    )
+    down = [add(down_keep[p], permute(down_send[p], "dp", n_dp, dp_bits[-1])) for p in pairs]
     grad_b_gu = jnp.stack([jnp.sum(grad_gate_up[p].astype(f32), 1) for p in pairs])
     partial_hidden = sum_of("ctn,ncd->td", grad_gate_up, wg)
-    (grad_first, sums_one, grad_att_all), ((gu_came0,), (gu_came1,)) = swap(
+    (
+        (grad_first, sums_one, grad_att_all),
+        (*gu_came, _),
+    ) = swap(
         4,
+        upper_part=UP4,
         inputs=[partial_hidden, first_sum, grad_second, row(gain_one)],
         outputs=[full, sums_shape],
         middle=third_middle,
         scatter=True,
         gather=True,
-        cargo=[across_dp(gu_send[0]), across_dp(gu_send[1])],
-    )
-    gu = add(gu_keep[0], gu_came0)
-    gu_other = add(gu_keep[1], gu_came1)
-    gu = add(gu, flipped(gu_other))
-    down = [add(down_keep[p], permute(down_send[p], "dp", n_dp, dp_bits[-1])) for p in pairs]
-    layer_everywhere = jnp.stack(across(layer_rows, n_dp))
+        cargo=[
+            *[across_dp(v) for v in gu_send],
+            present(down[1]),
+        ],
+    )
+    down_sent, grad_att_all = lax.optimization_barrier((down[1], grad_att_all))
+    down = add(down[0], flipped(down_sent))
+    gu = [add(gu_keep[k], gu_came[k][0]) for k in range(4)]
+    gate_came = flipped(gu[2])
     grad_context = lax.dot_general(
         grad_att_all, wo, (((1,), (1,)), ((), ())), preferred_element_type=f32
     ).astype(bf16)
-    grad_linear = attend_back(turned, grad_context, place, cos_table, -sin_table, key_at, rows)
-    grad_w_out = dot_rows(context, grad_att_all).astype(bf16).reshape(2, width_qkv, model)
-    grad_w_qkv = [
-        jnp.einsum("td,ctn->cdn", tokens_all, grad_linear[p], preferred_element_type=f32)
-        for p in pairs
-    ]
+    grad_linear = attend_back(
+        turned, grad_context, place, cos_table, -sin_table, key_at, query_at, rows
+    )
+    out_keep, out_send = halve(columns_of(grad_att_all), ein("tn,td->nd", context), 1)
+    token_columns = columns_of(tokens_all)
+    qkv_keep, qkv_send = zip(
+        *[halve(token_columns, ein("ctn,td->cdn", grad_linear[p]), 1) for p in pairs]
+    )
     grad_b_qkv = jnp.stack([jnp.sum(grad_linear[p].astype(f32), 1) for p in pairs])
-    out_keep, out_send = halve_first(grad_w_out, 1)
-    qkv_keep, qkv_send = halve_pair(grad_w_qkv, 1)
     partial_in = sum_of("ctn,cdn->td", grad_linear, wq)
+    bias = jnp.concatenate(
+        [grad_b_qkv.reshape(2, 3 * width_qkv), grad_b_gu.reshape(2, 2 * width_ffn)], 1
+    )
+    bias = jnp.pad(bias, ((0, 0), (0, -bias.shape[1] % model))).reshape(-1, model)
+    bias_rows = bias.shape[0] // 2
+    upto = lambda array: jnp.pad(array, ((0, -array.shape[0] % 8), (0, 0)))
+    norm_grads = jnp.concatenate([jnp.sum(sums_one, 1), jnp.sum(sums_two, 1)])
+    small = jnp.concatenate([upto(norm_grads), upto(bias[:bias_rows]), upto(bias[bias_rows:])])
+    bias_at = small.shape[0] - 2 * upto(bias[:bias_rows]).shape[0]
     (
         (input_rows,),
-        ((out_came,), (qkv_came0,), (qkv_came1,), (down_came,), (layer_out,), (gu,)),
+        (
+            (input_everywhere,),
+            (out_came,),
+            (qkv_came0,),
+            (qkv_came1,),
+            _,
+            _,
+            (up_came,),
+            (small,),
+        ),
     ) = swap(
         5,
+        upper_part=UP5,
         inputs=[partial_in, grad_first],
         outputs=[((rows, model), bf16)],
         middle=last_middle,
         scatter=True,
         cargo=[
+            rows_dp(layer_shape, n_dp, from_out=0),
             across_dp(out_send),
             across_dp(qkv_send[0]),
             across_dp(qkv_send[1]),
-            across_pair(down[1]),
-            return_cargo(*sorted_out(layer_rows, layer_everywhere, False), n_tensor),
-            gather_dp(gu, cut_ffn, n_dp),
+            present(gate_came),
+            present(down),
+            across_pair(gu[3]),
+            rows_dp(small, n_dp, upper=False),
         ],
     )
-    down = add(down[0], down_came)
-    out = add(out_keep, out_came)
+    gate, up = add(gu[0], gate_came), add(gu[1], up_came)
+    out = add(out_keep, out_came).reshape(2, width_qkv, share)
     qkv = [add(qkv_keep[0], qkv_came0), add(qkv_keep[1], qkv_came1)]
-    _, ((input_everywhere,), (out_came,), (qkv_came,), (down,)) = swap(
+    small = jnp.sum(small, 0)
+    bias_own, bias_other = jnp.split(small[bias_at:], 2)
+    _, ((input_grad,), (out_came,), (qkv_came,), (gate,), (up,), (down,), (norms,), (bias_came,)) = swap(
         6,
         cargo=[
-            rows_dp(input_rows, n_dp),
+            return_cargo(*sorted_out(input_rows, input_everywhere), n_tensor),
             across_pair(out[1]),
             across_pair(qkv[1]),
+            gather_dp(gate, 1, n_dp),
+            gather_dp(up, 1, n_dp),
             gather_dp(down, 1, n_dp),
+            gather_tensor(small[:bias_at], n_tensor, cut=True),
+            swap_cargo(bias_other, "tensor", width),
         ],
     )
+    bias = (bias_own + bias_came)[:bias_rows].reshape(-1)
     out = add(out[0], out_came)
     qkv = add(qkv[0], qkv_came)
-    _, ((input_grad,), (out,), (qkv,)) = swap(
+    _, ((out,), (qkv,), (norms,), (layer_out,)) = swap(
         7,
         cargo=[
-            return_cargo(*sorted_out(input_rows, input_everywhere, True), n_tensor),
-            gather_dp(out, 0, n_dp),
+            gather_dp(out, 1, n_dp),
             gather_dp(qkv, 1, n_dp),
+            gather_tensor(jnp.sum(norms, 0), n_tensor),
+            return_cargo(*sorted_out(layer_rows, layer_everywhere), n_tensor),
         ],
     )
 
-    def reduce_small(everywhere, pair):
-        for bit in dp_bits:
-            everywhere, pair = jax.tree.map(
-                lambda v: v + permute(v, "dp", n_dp, bit), (everywhere, pair)
-            )
-        own = pair[0] + flipped(pair[1])
-        for bit in bits_of(n_tensor):
-            everywhere = everywhere + permute(everywhere, "tensor", n_tensor, bit)
-        return everywhere, own
-
-    norm_grads = jnp.concatenate([jnp.sum(sums_one, 1), jnp.sum(sums_two, 1)])
-    bias = jnp.concatenate(
-        [grad_b_qkv.reshape(2, 3 * width_qkv), grad_b_gu.reshape(2, 2 * width_ffn)], 1
-    )
-    norm_grads, bias = reduce_small(norm_grads, bias)
+    norm_grads = norms.transpose(1, 0, 2).reshape(-1, model)
     grad_b_qkv = bias[: 3 * width_qkv].reshape(3, width_qkv)
-    grad_b_gu = bias[3 * width_qkv :].reshape(2, width_ffn)
+    grad_b_gu = bias[3 * width_qkv : 3 * width_qkv + 2 * width_ffn].reshape(2, width_ffn)
     return (
         layer_out.astype(f32),
         input_grad.astype(f32),
@@ -1097,7 +1251,7 @@
         norm_grads[2],
         norm_grads[0],
         norm_grads[1],
-        gu.astype(f32).transpose(2, 1, 0),
+        interleave(gate, up).transpose(2, 1, 0),
         grad_b_gu,
         down.astype(f32),
         norm_grads[5],

time: 1110 us -> 1000 us (0.901)
  Pallas kernels: 692 us -> 651 us
  other arithmetic: 79.9 us -> 52.8 us
  local copies, waits for them, and re-layouts: 94 us -> 67.1 us
  waiting for transfers between devices: 54.5 us -> 40.3 us
  matrix products: 144 us -> 156 us
    pallas_call x8, Pallas kernels: 655 us -> 606 us  [exchange(): pl.pallas_call(kernel, out_shape=shapes, in_specs=[vmem] * n_in + [anywhe...]
    dot_general x2 -> x0, local copies, waits for them, and re-layouts: 30.3 us -> none  [on_device(): jnp.einsum('td,ctn->ncd', hidden_all, grad_gate_up[p], preferred_element_...]
    convert_element_type x15 -> x10, other arithmetic: 33.6 us -> 13.3 us  [add(): return (a.astype(f32) + b.astype(f32)).astype(bf16)]
    dynamic_slice x14 -> x6, local copies, waits for them, and re-layouts: 21.9 us -> 7.36 us  [the longest x4 3.83 us: columns_of(): lax.dynamic_slice_in_dim(array, (d ^ o) * share, share, 1)]
    ppermute x21 -> x15, waiting for transfers between devices: 54.5 us -> 40.3 us  [permute(): return lax.ppermute(value, axis, [(i, i ^ bit) for i in range(size)])]
    dot_general x7 -> x27, matrix products: 39.1 us -> 51.3 us  [ein(): return lambda b: jnp.einsum(spec, a, b, preferred_element_type=f32)]
    unnamed x201 -> x258, local copies, waits for them, and re-layouts: 33.7 us -> 45.4 us
  transfers between devices with their start and end apart: 21 -> 15, of which waited for: 5 -> 3; matrix products, arithmetic and copies ran while one was open for 18% -> 11% of each run, Pallas kernels for 17% -> 12%
where the time goes in v3:
time: 1000 us; the launch traced here: 990 us
  Pallas kernels  651 us (65%)
  matrix products  156 us (16%)
  local copies, waits for them, and re-layouts  67.1 us (7%)
  other arithmetic  52.8 us (5%)
  waiting for transfers between devices  40.3 us (4%)
  between operations  12.8 us (1%)
  starting transfers between devices  10.2 us (1%)
    pallas_call x8, Pallas kernels, exchange(): pl.pallas_call(kernel, out_shape=shapes, in_specs=[vmem] * n_in + [anywhe...  606 us
    dot_general x27, matrix products, ein(): return lambda b: jnp.einsum(spec, a, b, preferred_element_type=f32)  51.3 us
    dot_general x6, matrix products, sum_of(): jnp.einsum(spec, a[p], b[p], preferred_element_type=f32)  49.7 us
    unnamed x258, local copies, waits for them, and re-layouts  45.4 us
    ppermute x15, waiting for transfers between devices, permute(): return lax.ppermute(value, axis, [(i, i ^ bit) for i in range(size)])  40.3 us
    pallas_call x1, Pallas kernels, attend_back(): pl.pallas_call(functools.partial(attend_back_kernel, heads, rows), out_sh...  22.6 us
  transfers between devices with their start and end apart: 15, of which 3 were waited for; matrix products, arithmetic and copies ran while one was open for 11% of the time, Pallas kernels for 12%

profile of v3, /device:TPU:10, one launch (start us, length us, event | category | flops | bytes accessed | tf_op | source)
XLA Modules:
  0.0 990.4 jit_solution(6802844796655548843)
XLA Ops:
  17.8 55.4 %exchange_0.1 = (bf16[256,2048]{1,0:T(8,128)(2,1)}, bf16[4,256,2048]{2,1,0:T(8,128)(2,1)}, bf16[3,256,256]{2,1,0:T(8,128)(2,1)S(1)}, s32[4,8,128]{2,1,0:T(8,128)...) custom-call(bf16[384,2048]{1,0:T(8,128)(2,1)S(1)} %copy-done.37, bf16[3,2048,256]{2,1,0:T(8,128)(2,1)S(1)} %bitcast.273, ...), custom_call_target="tpu_custom_call" | custom-call | tf_op jit(solution)/shard_map/exchange_0/pallas_call | solution.py:604
  77.0 57.8 %exchange_1.1 = (bf16[3,2048,256]{2,1,0:T(8,128)(2,1)S(1)}, bf16[256,2048]{1,0:T(8,128)(2,1)S(1)}, bf16[1024,2048]{1,0:T(8,128)(2,1)S(1)}) custom-call(bf16[256,2048]{1,0:T(8,128)(2,1)S(1)} %bitcast_select_fusion.1.refs_0_.refs_1_, bf16[3,256,256]{2,1,0:T(8,128)(2,1)S(1)} %get-tuple-element.148.refs_1_, bf16[3,2048,256]{2,1,0:T(8,128)(2,1)S(1)} %bitcast.274, ...), custom_call_target="tpu_custom_call" | custom-call | tf_op jit(solution)/shard_map/exchange_1/pallas_call | solution.py:604
  148.8 8.4 fusion.44.own
  157.2 5.1 fusion.47.other
  179.3 15.6 %attend.1 = (bf16[1024,1536]{1,0:T(8,128)(2,1)S(1)}, bf16[1024,512]{1,0:T(8,128)(2,1)S(1)}) custom-call(s32[1]{0:T(128)} %bitcast.12.place, f32[3,1024,256]{2,1,0:T(8,128)S(1)} %copy-done.16, f32[3,1024,256]{2,1,0:T(8,128)S(1)} %copy-done.17, f32[2,3,256]{2,1,0:T(4,128)S(1)} %pad_maximum_fusion.6.bias, f32[1024,128]{1,0:T(8,128)S(1)} %copy-done.10, ...), custom_call_target="tpu_custom_call" | custom-call | tf_op jit(solution)/shard_map/attend/pallas_call | solution.py:782
  198.1 4.4 convolution_convert_fusion.refs_0_
  202.6 105.8 %exchange_2.1 = (f32[256,2048]{1,0:T(8,128)S(1)}, bf16[684,2,2048]{2,1,0:T(2,128)(2,1)}, bf16[684,2048]{1,0:T(8,128)(2,1)S(1)}, bf16[256,2048]{1,0:T(8,128)(2,1)...) custom-call(bf16[1024,2048]{1,0:T(8,128)(2,1)} %convolution_convert_fusion.refs_0_, ...), custom_call_target="tpu_custom_call" | custom-call | tf_op jit(solution)/shard_map/exchange_2/pallas_call | solution.py:604
  310.3 8.8 bitcast_add_fusion.2
  320.8 4.0 select_convert_fusion
  324.9 5.8 fusion.158
  330.6 7.6 bitcast_add_fusion.3
  342.1 7.4 add_convert_fusion.refs_0_
  349.6 91.2 %exchange_3.1 = (bf16[256,2048]{1,0:T(8,128)(2,1)}, f32[256,2048]{1,0:T(8,128)S(1)}, f32[3,8,2048]{2,1,0:T(8,128)S(1)}, bf16[4,256,2048]{2,1,0:T(8,128)(2,1)S(1)}, bf16[1024,2048]{1,0:T(8,128)(2,1)S(1)}) custom-call(bf16[1024,2048]{1,0:T(8,128)(2,1)} %add_convert_fusion.refs_0_, f32[256,2048]{1,0:T(8,128)S(1)} %copy-done.8, ...), custom_call_target="tpu_custom_call" | custom-call | tf_op jit(solution)/shard_map/exchange_3/pallas_call | solution.py:604
  440.8 9.1 multiply_bitcast_fusion
  449.9 6.9 multiply_bitcast_fusion.1
  476.5 10.0 %fusion.2 = f32[1024,2048,1]{1,0,2:T(8,128)} fusion(bf16[2,1024,684]{1,2,0:T(8,128)(2,1)S(1)} %get-tuple-element.205, bf16[684,2,2048]{2,1,0:T(2,128)(2,1)S(1)} %bitcast.295), kind=kOutput, calls=%fused_computation.19 | convolution fusion | flops 5737807872 | bytes 16793600 | tf_op jit(solution)/shard_map/ctn,ncd->td/dot_general | solution.py:1029
  493.8 13.4 %fusion.1.refs_0_ = bf16[1024,2048]{1,0:T(8,128)(2,1)} fusion(f32[1024,2048,1]{1,0,2:T(8,128)} %fusion.2, bf16[2,1024,684]{1,2,0:T(8,128)(2,1)} %copy-done.84, bf16[684,2,2048]{2,1,0:T(2,128)(2,1)} %get-tuple-element.157), kind=kOutput, calls=%fused_computation.10 | convolution fusion | flops 5742002176 | bytes 20987904 | tf_op jit(solution)/shard_map/ctn,ncd->td/dot_general | solution.py:1029
  528.5 78.4 %exchange_4.1 = (f32[256,2048]{1,0:T(8,128)S(1)}, f32[3,8,2048]{2,1,0:T(8,128)S(1)}, bf16[684,512]{1,0:T(8,128)(2,1)S(1)}, bf16[684,512]{1,0:T(8,128)(2,1)S(1)},...) custom-call(bf16[1024,2048]{1,0:T(8,128)(2,1)} %fusion.1.refs_0_, ...), custom_call_target="tpu_custom_call" | custom-call | tf_op jit(solution)/shard_map/exchange_4/pallas_call | solution.py:604
  609.1 4.8 convolution_convert_fusion.9.grad_context
  614.0 22.6 %attend_back.1 = (bf16[3,1024,256]{2,1,0:T(8,128)(2,1)S(1)}, bf16[3,1024,256]{2,1,0:T(8,128)(2,1)S(1)}) custom-call(s32[1]{0:T(128)} %bitcast.12.place, bf16[1024,1536]{1,0:T(8,128)(2,1)S(1)} %copy-done.19, bf16[1024,512]{1,0:T(8,128)(2,1)S(1)} %convolution_convert_fusion.9.grad_context, f32[1024,128]{1,0:T(8,128)S(1)} %copy-done.11, ...), custom_call_target="tpu_custom_call" | custom-call | tf_op jit(solution)/shard_map/attend_back/pallas_call | solution.py:856
  644.0 5.9 fusion.150
  654.0 3.1 fusion.55
  659.8 7.2 fusion.refs_0_
  667.1 3.0 fusion.54
  671.6 25.0 %collective-permute-done.24 = bf16[684,512]{1,0:T(8,128)(2,1)} collective-permute-done((bf16[684,512]{1,0:T(8,128)(2,1)}, bf16[684,512]{1,0:T(8,128)(2,1)}, u32[]{:S(2)}, u32[]{:S(2)}) %collective-permute-start.24) | collective-permute-done | bytes 700448 | tf_op jit(solution)/shard_map/ppermute | solution.py:29
  698.2 13.0 %collective-permute-done.21.refs_5_ = bf16[684,512]{1,0:T(8,128)(2,1)S(1)} collective-permute-done((bf16[684,512]{1,0:T(8,128)(2,1)}, bf16[684,512]{1,0:T(8,128)(2,1)S(1)}, u32[]{:S(2)}, u32[]{:S(2)}) %collective-permute-start.21) | collective-permute-done | bytes 700448 | tf_op jit(solution)/shard_map/ppermute | solution.py:29
  722.4 59.5 %exchange_5.1 = (bf16[256,2048]{1,0:T(8,128)(2,1)}, bf16[4,256,2048]{2,1,0:T(8,128)(2,1)S(1)}, bf16[512,512]{1,0:T(8,128)(2,1)S(1)}, bf16[3,512,256]{2,1,0:T(8,1...) custom-call(bf16[1024,2048]{1,0:T(8,128)(2,1)} %fusion.refs_0_, ...), custom_call_target="tpu_custom_call" | custom-call | tf_op jit(solution)/shard_map/exchange_5/pallas_call | solution.py:604
  798.4 112.1 %exchange_6.1 = (bf16[384,2048]{1,0:T(8,128)(2,1)S(1)}, bf16[256,512]{1,0:T(8,128)(2,1)S(1)}, bf16[3,512,256]{2,1,0:T(8,128)(2,1)S(1)}, bf16[684,2048]{1,0:T(8,1...) custom-call(bf16[256,2048]{1,0:T(8,128)(2,1)S(1)} %copy-done.14, ...), custom_call_target="tpu_custom_call" | custom-call | tf_op jit(solution)/shard_map/exchange_6/pallas_call | solution.py:604
  921.7 46.0 %exchange_7.1 = (bf16[256,2048]{1,0:T(8,128)(2,1)S(1)}, bf16[3,2048,256]{2,1,0:T(8,128)(2,1)S(1)}, f32[8,8,256]{2,1,0:T(8,128)S(1)}, bf16[384,2048]{1,0:T(8,128)(2,1)S(1)}) custom-call(bf16[256,512]{1,0:T(8,128)(2,1)S(1)} %add_convert_fusion.22.refs_0_, bf16[3,512,256]{2,1,0:T(8,128)(2,1)S(1)} %add_convert_fusion.3.refs_1_, ...), custom_call_target="tpu_custom_call" | custom-call | tf_op jit(solution)/shard_map/exchange_7/pallas_call | solution.py:604
  974.9 3.2 convert_element_type.490
  978.1 3.7 convert_bitcast_fusion
  983.0 7.0 interleave.1
  (410 shorter events, 166.5 us)
Async XLA Ops:
  75.0 59.7 %copy-start.5 = (bf16[256,2048]{1,0:T(8,128)(2,1)}, bf16[256,2048]{1,0:T(8,128)(2,1)S(1)}, u32[]{:S(2)}) copy-start(bf16[256,2048]{1,0:T(8,128)(2,1)S(1)} %bitcast_select_fusion.1.refs_0_.refs_1_) | copy-start | bytes 3145732
  139.4 63.1 %collective-permute-start.10 = (bf16[85,2,2048]{2,1,0:T(2,128)(2,1)}, bf16[85,2,2048]{2,1,0:T(2,128)(2,1)}, u32[]{:S(2)}, u32[]{:S(2)}) collective-permute-start(bf16[85,2,2048]{2,1,0:T(2,128)(2,1)} %dynamic-slice_bitcast_fusion.4), channel_id=1, source_target_pairs={{0,4},{1,5},{2,6},{3,7},{4,0},{5,1},{6,2},{7,3},{8,12},{9,13},{10,... | collective-permute-start | bytes 2088968 | tf_op jit(solution)/shard_map/ppermute | solution.py:29
  140.2 62.3 %collective-permute-start.11 = (bf16[684,512]{1,0:T(8,128)(2,1)}, bf16[684,512]{1,0:T(8,128)(2,1)}, u32[]{:S(2)}, u32[]{:S(2)}) collective-permute-start(bf16[684,512]{1,0:T(8,128)(2,1)} %constant_dynamic-slice_fusion.9), channel_id=1, source_target_pairs={{0,4},{1,5},{2,6},{3,7},{4,0},{5,1},{6,2},{7,3},{8,12},{9,13},{10,... | collective-permute-start | bytes 2101256 | tf_op jit(solution)/shard_map/ppermute | solution.py:29
  144.6 193.6 %copy-start.116 = (pred[684]{0:T(1024)(128)(4,1)}, pred[684]{0:T(1024)(128)(4,1)S(1)}, u32[]{:S(2)}) copy-start(pred[684]{0:T(1024)(128)(4,1)S(1)} %add_compare_fusion.1) | copy-start | bytes 2056
  148.2 25.3 %copy-start.67 = (s32[8,128]{1,0:T(8,128)}, s32[8,128]{1,0:T(8,128)S(1)}, u32[]{:S(2)}) copy-start(s32[8,128]{1,0:T(8,128)S(1)} %iota_add_fusion) | copy-start | bytes 12292
  167.6 153.2 %copy-start.118 = (pred[684]{0:T(1024)(128)(4,1)}, pred[684]{0:T(1024)(128)(4,1)S(1)}, u32[]{:S(2)}) copy-start(pred[684]{0:T(1024)(128)(4,1)S(1)} %add_compare_fusion) | copy-start | bytes 2056
  198.1 112.1 %slice-start = ((s8[5603328]{0:T(1024)(128)(4,1)}), s8[1409024]{0:T(1024)(128)(4,1)S(1)}, s32[]{:S(2)}) async-start(s8[5603328]{0:T(1024)(128)(4,1)} %bitcast.290), calls=%async_computation | async-start | bytes 2818048
  202.6 107.7 %slice-start.1 = ((s8[5603328]{0:T(1024)(128)(4,1)}), s8[4194304]{0:T(1024)(128)(4,1)S(1)}, s32[]{:S(2)}) async-start(s8[5603328]{0:T(1024)(128)(4,1)} %bitcast.290), calls=%async_computation.1 | async-start | bytes 8388608
  324.8 146.1 %copy-start.92 = (bf16[1024,684]{0,1:T(8,128)(2,1)}, bf16[1024,684]{0,1:T(8,128)(2,1)S(1)}, u32[]{:S(2)}) copy-start(bf16[1024,684]{0,1:T(8,128)(2,1)S(1)} %select_convert_fusion) | copy-start | bytes 4202500
  349.6 91.3 %copy-start.117 = (pred[684]{0:T(1024)(128)(4,1)S(1)}, pred[684]{0:T(1024)(128)(4,1)}, u32[]{:S(2)}) copy-start(pred[684]{0:T(1024)(128)(4,1)} %copy-done.116) | copy-start | bytes 2056
  440.8 29.9 %copy-start.49 = (bf16[1024,2048]{1,0:T(8,128)(2,1)}, bf16[1024,2048]{1,0:T(8,128)(2,1)S(1)}, u32[]{:S(2)}) copy-start(bf16[1024,2048]{1,0:T(8,128)(2,1)S(1)} %get-tuple-element.164) | copy-start | bytes 12582916
  491.6 19.0 %collective-permute-start.15 = (bf16[684,1024]{1,0:T(8,128)(2,1)}, bf16[684,1024]{1,0:T(8,128)(2,1)S(1)}, u32[]{:S(2)}, u32[]{:S(2)}) collective-permute-start(bf16[684,1024]{1,0:T(8,128)(2,1)} %convolution_convert_fusion.6), channel_id=1, source_target_pairs={{0,8},{8,0},{16,24},{24,16},{1,9},{9,1},{17,25},{25,17},{2,10},{10... | collective-permute-start | bytes 4202504 | tf_op jit(solution)/shard_map/ppermute | solution.py:29
  491.6 23.6 %collective-permute-start.14 = (bf16[684,1024]{1,0:T(8,128)(2,1)}, bf16[684,1024]{1,0:T(8,128)(2,1)S(1)}, u32[]{:S(2)}, u32[]{:S(2)}) collective-permute-start(bf16[684,1024]{1,0:T(8,128)(2,1)} %convolution_convert_fusion.7), channel_id=1, source_target_pairs={{0,8},{8,0},{16,24},{24,16},{1,9},{9,1},{17,25},{25,17},{2,10},{10... | collective-permute-start | bytes 4202504 | tf_op jit(solution)/shard_map/ppermute | solution.py:29
  492.1 26.7 %collective-permute-start.17 = (bf16[684,1024]{1,0:T(8,128)(2,1)}, bf16[684,1024]{1,0:T(8,128)(2,1)S(1)}, u32[]{:S(2)}, u32[]{:S(2)}) collective-permute-start(bf16[684,1024]{1,0:T(8,128)(2,1)} %convolution_convert_fusion.4), channel_id=1, source_target_pairs={{0,8},{8,0},{16,24},{24,16},{1,9},{9,1},{17,25},{25,17},{2,10},{10... | collective-permute-start | bytes 4202504 | tf_op jit(solution)/shard_map/ppermute | solution.py:29
  492.1 15.1 %collective-permute-start.12 = (bf16[684,1024]{1,0:T(8,128)(2,1)}, bf16[684,1024]{1,0:T(8,128)(2,1)S(1)}, u32[]{:S(2)}, u32[]{:S(2)}) collective-permute-start(bf16[684,1024]{1,0:T(8,128)(2,1)} %convolution_convert_fusion.8), channel_id=1, source_target_pairs={{0,8},{8,0},{16,24},{24,16},{1,9},{9,1},{17,25},{25,17},{2,10},{10... | collective-permute-start | bytes 4202504 | tf_op jit(solution)/shard_map/ppermute | solution.py:29
  492.6 16.1 %collective-permute-start.22 = (bf16[684,1024]{1,0:T(8,128)(2,1)}, bf16[684,1024]{1,0:T(8,128)(2,1)S(1)}, u32[]{:S(2)}, u32[]{:S(2)}) collective-permute-start(bf16[684,1024]{1,0:T(8,128)(2,1)} %convolution_convert_fusion.3), channel_id=1, source_target_pairs={{0,8},{8,0},{16,24},{24,16},{1,9},{9,1},{17,25},{25,17},{2,10},{10... | collective-permute-start | bytes 4202504 | tf_op jit(solution)/shard_map/ppermute | solution.py:29
  507.2 16.1 %collective-permute-start.16 = (bf16[684,1024]{1,0:T(8,128)(2,1)S(1)}, bf16[684,1024]{1,0:T(8,128)(2,1)S(1)}, u32[]{:S(2)}, u32[]{:S(2)}) collective-permute-start(bf16[684,1024]{1,0:T(8,128)(2,1)S(1)} %copy-done.120), channel_id=1, source_target_pairs={{0,8},{8,0},{16,24},{24,16},{1,9},{9,1},{17,25},{25,17},{2,10},{10... | collective-permute-start | bytes 4202504 | tf_op jit(solution)/shard_map/ppermute | solution.py:29
  508.7 18.7 %collective-permute-start.13 = (bf16[684,512]{1,0:T(8,128)(2,1)S(1)}, bf16[684,512]{1,0:T(8,128)(2,1)S(1)}, u32[]{:S(2)}, u32[]{:S(2)}) collective-permute-start(bf16[684,512]{1,0:T(8,128)(2,1)S(1)} %add_convert_fusion.17), channel_id=1, source_target_pairs={{0,16},{8,24},{16,0},{24,8},{1,17},{9,25},{17,1},{25,9},{2,18},{10... | collective-permute-start | bytes 2101256 | tf_op jit(solution)/shard_map/ppermute | solution.py:29
  510.6 160.8 %collective-permute-start.23 = (bf16[684,512]{1,0:T(8,128)(2,1)}, bf16[684,512]{1,0:T(8,128)(2,1)}, u32[]{:S(2)}, u32[]{:S(2)}) collective-permute-start(bf16[684,512]{1,0:T(8,128)(2,1)} %add_convert_fusion.13), channel_id=1, source_target_pairs={{0,16},{8,24},{16,0},{24,8},{1,17},{9,25},{17,1},{25,9},{2,18},{10... | collective-permute-start | bytes 2101256 | tf_op jit(solution)/shard_map/ppermute | solution.py:29
  528.5 80.6 %copy-start.109 = (bf16[512,2048]{1,0:T(8,128)(2,1)S(1)}, bf16[512,2048]{1,0:T(8,128)(2,1)}, u32[]{:S(2)}) copy-start(bf16[512,2048]{1,0:T(8,128)(2,1)} %copy-done.107) | copy-start | bytes 6291460
  636.6 23.2 %copy-start.35 = (bf16[3,1024,256]{2,1,0:T(8,128)(2,1)}, bf16[3,1024,256]{2,1,0:T(8,128)(2,1)S(1)}, u32[]{:S(2)}) copy-start(bf16[3,1024,256]{2,1,0:T(8,128)(2,1)S(1)} %get-tuple-element.170) | copy-start | bytes 4718596
  636.6 30.5 %copy-start.33 = (bf16[3,1024,256]{2,1,0:T(8,128)(2,1)}, bf16[3,1024,256]{2,1,0:T(8,128)(2,1)S(1)}, u32[]{:S(2)}) copy-start(bf16[3,1024,256]{2,1,0:T(8,128)(2,1)S(1)} %get-tuple-element.169) | copy-start | bytes 4718596
  649.8 46.7 %collective-permute-start.24 = (bf16[684,512]{1,0:T(8,128)(2,1)}, bf16[684,512]{1,0:T(8,128)(2,1)}, u32[]{:S(2)}, u32[]{:S(2)}) collective-permute-start(bf16[684,512]{1,0:T(8,128)(2,1)} %add_convert_fusion.16.refs_8_), channel_id=1, source_target_pairs={{0,4},{1,5},{2,6},{3,7},{4,0},{5,1},{6,2},{7,3},{8,12},{9,13},{10,... | collective-permute-start | bytes 2101256 | tf_op jit(solution)/shard_map/ppermute | solution.py:29
  653.7 57.5 %collective-permute-start.21 = (bf16[684,512]{1,0:T(8,128)(2,1)}, bf16[684,512]{1,0:T(8,128)(2,1)S(1)}, u32[]{:S(2)}, u32[]{:S(2)}) collective-permute-start(bf16[684,512]{1,0:T(8,128)(2,1)} %add_convert_fusion.15), channel_id=1, source_target_pairs={{0,4},{1,5},{2,6},{3,7},{4,0},{5,1},{6,2},{7,3},{8,12},{9,13},{10,... | collective-permute-start | bytes 2101256 | tf_op jit(solution)/shard_map/ppermute | solution.py:29
  657.0 60.4 %collective-permute-start.20 = (bf16[3,1024,256]{2,1,0:T(8,128)(2,1)}, bf16[3,1024,256]{2,1,0:T(8,128)(2,1)}, u32[]{:S(2)}, u32[]{:S(2)}) collective-permute-start(bf16[3,1024,256]{2,1,0:T(8,128)(2,1)} %fusion.55), channel_id=1, source_target_pairs={{0,8},{8,0},{16,24},{24,16},{1,9},{9,1},{17,25},{25,17},{2,10},{10... | collective-permute-start | bytes 4718600 | tf_op jit(solution)/shard_map/ppermute | solution.py:29
  659.3 53.5 %collective-permute-start.18 = (bf16[512,1024]{1,0:T(8,128)(2,1)}, bf16[512,1024]{1,0:T(8,128)(2,1)}, u32[]{:S(2)}, u32[]{:S(2)}) collective-permute-start(bf16[512,1024]{1,0:T(8,128)(2,1)} %fusion.56), channel_id=1, source_target_pairs={{0,8},{8,0},{16,24},{24,16},{1,9},{9,1},{17,25},{25,17},{2,10},{10... | collective-permute-start | bytes 3145736 | tf_op jit(solution)/shard_map/ppermute | solution.py:29
  670.1 26.4 %copy-start.105 = (bf16[684,512]{1,0:T(8,128)(2,1)S(1)}, bf16[684,512]{1,0:T(8,128)(2,1)}, u32[]{:S(2)}) copy-start(bf16[684,512]{1,0:T(8,128)(2,1)} %add_convert_fusion.14) | copy-start | bytes 2101252
  670.1 41.0 %copy-start.61 = (bf16[684,512]{1,0:T(8,128)(2,1)S(1)}, bf16[684,512]{1,0:T(8,128)(2,1)}, u32[]{:S(2)}) copy-start(bf16[684,512]{1,0:T(8,128)(2,1)} %copy-done.60) | copy-start | bytes 2101252
  671.4 48.4 %collective-permute-start.19 = (bf16[3,1024,256]{2,1,0:T(8,128)(2,1)}, bf16[3,1024,256]{2,1,0:T(8,128)(2,1)S(1)}, u32[]{:S(2)}, u32[]{:S(2)}) collective-permute-start(bf16[3,1024,256]{2,1,0:T(8,128)(2,1)} %fusion.54), channel_id=1, source_target_pairs={{0,8},{8,0},{16,24},{24,16},{1,9},{9,1},{17,25},{25,17},{2,10},{10... | collective-permute-start | bytes 4718600 | tf_op jit(solution)/shard_map/ppermute | solution.py:29
  671.5 41.3 %copy-start.81 = (bf16[1024,512]{1,0:T(8,128)(2,1)S(1)}, bf16[1024,512]{1,0:T(8,128)(2,1)}, u32[]{:S(2)}) copy-start(bf16[1024,512]{1,0:T(8,128)(2,1)} %copy-done.79) | copy-start | bytes 3145732
  671.5 41.3 %copy-start.102 = (bf16[1024,2048]{1,0:T(8,128)(2,1)S(1)}, bf16[1024,2048]{1,0:T(8,128)(2,1)}, u32[]{:S(2)}) copy-start(bf16[1024,2048]{1,0:T(8,128)(2,1)} %get-tuple-element.167) | copy-start | bytes 12582916
  798.4 117.3 %copy-start.90 = (bf16[512,512]{1,0:T(8,128)(2,1)S(1)}, bf16[512,512]{1,0:T(8,128)(2,1)}, u32[]{:S(2)}) copy-start(bf16[512,512]{1,0:T(8,128)(2,1)} %copy-done.89) | copy-start | bytes 1572868
  (110 other events, 529.1 us)

commit v4 on v3

--- a/solution.py
+++ b/solution.py
@@ -138,10 +138,14 @@
 class Cargo:
     def __init__(self, inputs, outputs, count, run, early=0, from_out=None):
         self.inputs, self.outputs, self.count, self.run = inputs, outputs, count, run
-        self.early, self.from_out = early, from_out
+        self.early, self.from_out, self.late = early, from_out, from_out is not None
 
     def sooner(self, count=1):
         self.early = count
+        return self
+
+    def later(self):
+        self.late = True
         return self
 
 
@@ -481,13 +485,14 @@
         for c in cargo:
             c_ins, cargo_ins = cargo_ins[: len(c.inputs)], cargo_ins[len(c.inputs) :]
             c_outs, cargo_outs = cargo_outs[: len(c.outputs)], cargo_outs[len(c.outputs) :]
-            if c.from_out is None:
+            if not c.late:
                 stage = c.run(ship, c_ins, c_outs)
                 next(stage)
                 stages.append(stage)
                 soon.append([stage, c.early])
             else:
-                waiting.append(c.run(ship, [outs[c.from_out]], c_outs))
+                source = c_ins if c.from_out is None else [outs[c.from_out]]
+                waiting.append(c.run(ship, source, c_outs))
 
         def advance():
             for entry in soon:
@@ -1153,16 +1158,19 @@
         ],
     )
     down_sent, grad_att_all = lax.optimization_barrier((down[1], grad_att_all))
-    down = add(down[0], flipped(down_sent))
+    down_came = flipped(down_sent)
     gu = [add(gu_keep[k], gu_came[k][0]) for k in range(4)]
     gate_came = flipped(gu[2])
     grad_context = lax.dot_general(
         grad_att_all, wo, (((1,), (1,)), ((), ())), preferred_element_type=f32
     ).astype(bf16)
+    out_keep, out_send = halve(columns_of(grad_att_all), ein("tn,td->nd", context), 1)
+    out = add(out_keep, permute(out_send, "dp", n_dp, dp_bits[-1])).reshape(2, width_qkv, share)
     grad_linear = attend_back(
         turned, grad_context, place, cos_table, -sin_table, key_at, query_at, rows
     )
-    out_keep, out_send = halve(columns_of(grad_att_all), ein("tn,td->nd", context), 1)
+    down_came, *grad_linear = lax.optimization_barrier((down_came, *grad_linear))
+    down = add(down[0], down_came)
     token_columns = columns_of(tokens_all)
     qkv_keep, qkv_send = zip(
         *[halve(token_columns, ein("ctn,td->cdn", grad_linear[p]), 1) for p in pairs]
@@ -1199,7 +1207,7 @@
         scatter=True,
         cargo=[
             rows_dp(layer_shape, n_dp, from_out=0),
-            across_dp(out_send),
+            across_pair(out[1]).later(),
             across_dp(qkv_send[0]),
             across_dp(qkv_send[1]),
             present(gate_came),
@@ -1209,15 +1217,13 @@
         ],
     )
     gate, up = add(gu[0], gate_came), add(gu[1], up_came)
-    out = add(out_keep, out_came).reshape(2, width_qkv, share)
     qkv = [add(qkv_keep[0], qkv_came0), add(qkv_keep[1], qkv_came1)]
     small = jnp.sum(small, 0)
     bias_own, bias_other = jnp.split(small[bias_at:], 2)
-    _, ((input_grad,), (out_came,), (qkv_came,), (gate,), (up,), (down,), (norms,), (bias_came,)) = swap(
+    _, ((input_grad,), (qkv_came,), (gate,), (up,), (down,), (norms,), (bias_came,)) = swap(
         6,
         cargo=[
             return_cargo(*sorted_out(input_rows, input_everywhere), n_tensor),
-            across_pair(out[1]),
             across_pair(qkv[1]),
             gather_dp(gate, 1, n_dp),
             gather_dp(up, 1, n_dp),

time: 1000 us -> 990 us (0.990)
  matrix products: 156 us -> 179 us
  waiting for transfers between devices: 40.3 us -> 23.6 us
    ppermute x15 -> x16, waiting for transfers between devices: 40.3 us -> 23.6 us  [permute(): return lax.ppermute(value, axis, [(i, i ^ bit) for i in range(size)])]
    dot_general x27, matrix products: 51.3 us -> 67.2 us  [ein(): return lambda b: jnp.einsum(spec, a, b, preferred_element_type=f32)]
    unnamed x258 -> x268, local copies, waits for them, and re-layouts: 45.4 us -> 42 us
  transfers between devices with their start and end apart: 15 -> 16, of which waited for: 3 -> 2; matrix products, arithmetic and copies ran while one was open for 11% -> 13% of each run, Pallas kernels for 12% -> 12%
where the time goes in v4:
time: 990 us; the launch traced here: 979 us
  Pallas kernels  644 us (65%)
  matrix products  179 us (18%)
  local copies, waits for them, and re-layouts  61.6 us (6%)
  other arithmetic  45.8 us (5%)
  waiting for transfers between devices  23.6 us (2%)
  between operations  13.2 us (1%)
  starting transfers between devices  11.3 us (1%)
    pallas_call x8, Pallas kernels, exchange(): pl.pallas_call(kernel, out_shape=shapes, in_specs=[vmem] * n_in + [anywhe...  599 us
    dot_general x27, matrix products, ein(): return lambda b: jnp.einsum(spec, a, b, preferred_element_type=f32)  67.2 us
    dot_general x6, matrix products, sum_of(): jnp.einsum(spec, a[p], b[p], preferred_element_type=f32)  52.9 us
    unnamed x268, local copies, waits for them, and re-layouts  42 us
    ppermute x16, waiting for transfers between devices, permute(): return lax.ppermute(value, axis, [(i, i ^ bit) for i in range(size)])  23.6 us
    pallas_call x1, Pallas kernels, attend_back(): pl.pallas_call(functools.partial(attend_back_kernel, heads, rows), out_sh...  22.3 us
  transfers between devices with their start and end apart: 16, of which 2 were waited for; matrix products, arithmetic and copies ran while one was open for 13% of the time, Pallas kernels for 12%

profile of v4, /device:TPU:10, one launch (start us, length us, event | category | flops | bytes accessed | tf_op | source)
XLA Modules:
  0.0 978.7 jit_solution(4637555950431120083)
XLA Ops:
  17.8 55.4 %exchange_0.1 = (bf16[256,2048]{1,0:T(8,128)(2,1)}, bf16[4,256,2048]{2,1,0:T(8,128)(2,1)}, bf16[3,256,256]{2,1,0:T(8,128)(2,1)S(1)}, s32[4,8,128]{2,1,0:T(8,128)...) custom-call(bf16[384,2048]{1,0:T(8,128)(2,1)S(1)} %copy-done.38, bf16[3,2048,256]{2,1,0:T(8,128)(2,1)S(1)} %bitcast.265, ...), custom_call_target="tpu_custom_call" | custom-call | tf_op jit(solution)/shard_map/exchange_0/pallas_call | solution.py:609
  76.9 57.4 %exchange_1.1 = (bf16[3,2048,256]{2,1,0:T(8,128)(2,1)S(1)}, bf16[256,2048]{1,0:T(8,128)(2,1)S(1)}, bf16[1024,2048]{1,0:T(8,128)(2,1)S(1)}) custom-call(bf16[256,2048]{1,0:T(8,128)(2,1)S(1)} %bitcast_select_fusion.1.refs_0_.refs_1_, bf16[3,256,256]{2,1,0:T(8,128)(2,1)S(1)} %get-tuple-element.150.refs_1_, bf16[3,2048,256]{2,1,0:T(8,128)(2,1)S(1)} %bitcast.266, ...), custom_call_target="tpu_custom_call" | custom-call | tf_op jit(solution)/shard_map/exchange_1/pallas_call | solution.py:609
  148.5 8.4 fusion.44.own
  156.9 5.1 fusion.47.other
  178.9 15.5 %attend.1 = (bf16[1024,1536]{1,0:T(8,128)(2,1)S(1)}, bf16[1024,512]{1,0:T(8,128)(2,1)S(1)}) custom-call(s32[1]{0:T(128)} %bitcast.12.place, f32[3,1024,256]{2,1,0:T(8,128)S(1)} %copy-done.16, f32[3,1024,256]{2,1,0:T(8,128)S(1)} %copy-done.17, f32[2,3,256]{2,1,0:T(4,128)S(1)} %pad_maximum_fusion.6.bias, f32[1024,128]{1,0:T(8,128)S(1)} %copy-done.10, ...), custom_call_target="tpu_custom_call" | custom-call | tf_op jit(solution)/shard_map/attend/pallas_call | solution.py:787
  197.6 4.4 convolution_convert_fusion.refs_0_
  202.1 105.1 %exchange_2.1 = (f32[256,2048]{1,0:T(8,128)S(1)}, bf16[684,2,2048]{2,1,0:T(2,128)(2,1)}, bf16[684,2048]{1,0:T(8,128)(2,1)S(1)}, bf16[256,2048]{1,0:T(8,128)(2,1)...) custom-call(bf16[1024,2048]{1,0:T(8,128)(2,1)} %convolution_convert_fusion.refs_0_, ...), custom_call_target="tpu_custom_call" | custom-call | tf_op jit(solution)/shard_map/exchange_2/pallas_call | solution.py:609
  309.0 8.8 bitcast_add_fusion.2
  319.6 3.9 select_convert_fusion
  323.5 5.7 fusion.150
  329.3 7.6 bitcast_add_fusion.3
  340.8 7.4 add_convert_fusion.refs_0_
  348.2 93.7 %exchange_3.1 = (bf16[256,2048]{1,0:T(8,128)(2,1)}, f32[256,2048]{1,0:T(8,128)S(1)}, f32[3,8,2048]{2,1,0:T(8,128)S(1)}, bf16[4,256,2048]{2,1,0:T(8,128)(2,1)S(1)}, bf16[1024,2048]{1,0:T(8,128)(2,1)S(1)}) custom-call(bf16[1024,2048]{1,0:T(8,128)(2,1)} %add_convert_fusion.refs_0_, f32[256,2048]{1,0:T(8,128)S(1)} %copy-done.8, ...), custom_call_target="tpu_custom_call" | custom-call | tf_op jit(solution)/shard_map/exchange_3/pallas_call | solution.py:609
  441.9 10.6 %multiply_bitcast_fusion = (f32[1,1024,684]{1,2,0:T(8,128)}, f32[1,1024,684]{1,2,0:T(8,128)}) fusion(pred[684]{0:T(1024)(128)(4,1)S(1)} %copy-done.122, f32[2,1024,684]{1,2,0:T(8,128)} %copy-done.87, bf16[1024,2048]{1,0:T(8,128)(2,1)S(1)} %get-tuple-element.166, bf16[684,2048]{1,0:T(8,128)(2,1)S(1)} %copy-done.83), kind=kOutput, calls=%fused_computation.58 | convolution fusion | flops 2885013504 | bytes 18203308 | tf_op jit(solution)/shard_map/td,nd->tn/dot_general | solution.py:1123
  452.6 6.9 multiply_bitcast_fusion.1
  472.7 10.2 %fusion.2 = f32[1024,2048,1]{1,0,2:T(8,128)} fusion(bf16[2,1024,684]{1,2,0:T(8,128)(2,1)S(1)} %get-tuple-element.209, bf16[684,2,2048]{2,1,0:T(2,128)(2,1)S(1)} %bitcast.287), kind=kOutput, calls=%fused_computation.19 | convolution fusion | flops 5737807872 | bytes 16793600 | tf_op jit(solution)/shard_map/ctn,ncd->td/dot_general | solution.py:1034
  489.3 16.5 %fusion.1.refs_0_ = bf16[1024,2048]{1,0:T(8,128)(2,1)} fusion(f32[1024,2048,1]{1,0,2:T(8,128)} %fusion.2, bf16[2,1024,684]{1,2,0:T(8,128)(2,1)S(1)} %get-tuple-element.211, bf16[684,2,2048]{2,1,0:T(2,128)(2,1)} %get-tuple-element.159), kind=kOutput, calls=%fused_computation.10 | convolution fusion | flops 5742002176 | bytes 20987904 | tf_op jit(solution)/shard_map/ctn,ncd->td/dot_general | solution.py:1034
  544.3 80.1 %exchange_4.1 = (f32[256,2048]{1,0:T(8,128)S(1)}, f32[3,8,2048]{2,1,0:T(8,128)S(1)}, bf16[684,512]{1,0:T(8,128)(2,1)S(1)}, bf16[684,512]{1,0:T(8,128)(2,1)S(1)},...) custom-call(bf16[1024,2048]{1,0:T(8,128)(2,1)} %fusion.1.refs_0_, ...), custom_call_target="tpu_custom_call" | custom-call | tf_op jit(solution)/shard_map/exchange_4/pallas_call | solution.py:609
  624.4 7.3 convolution_convert_fusion.9.grad_context
  637.8 3.1 fusion.56
  641.1 22.3 %attend_back.1 = (bf16[3,1024,256]{2,1,0:T(8,128)(2,1)S(1)}, bf16[3,1024,256]{2,1,0:T(8,128)(2,1)S(1)}) custom-call(s32[1]{0:T(128)} %bitcast.12.place, bf16[1024,1536]{1,0:T(8,128)(2,1)S(1)} %copy-done.19, bf16[1024,512]{1,0:T(8,128)(2,1)S(1)} %copy-done.53, f32[1024,128]{1,0:T(8,128)S(1)} %copy-done.11, f32[1024,128]{1,0:T(8,128)S(1)} %copy-done.33, ...), custom_call_target="tpu_custom_call" | custom-call | tf_op jit(solution)/shard_map/attend_back/pallas_call | solution.py:861
  664.7 13.6 %collective-permute-done.20 = bf16[684,512]{1,0:T(8,128)(2,1)S(1)} collective-permute-done((bf16[684,512]{1,0:T(8,128)(2,1)}, bf16[684,512]{1,0:T(8,128)(2,1)S(1)}, u32[]{:S(2)}, u32[]{:S(2)}) %collective-permute-start.20) | collective-permute-done | bytes 700448 | tf_op jit(solution)/shard_map/ppermute | solution.py:29
  678.4 5.9 fusion.142
  690.8 7.2 fusion.refs_0_
  707.3 9.9 %collective-permute-done.19 = bf16[512,512]{1,0:T(8,128)(2,1)S(1)} collective-permute-done((bf16[512,512]{1,0:T(8,128)(2,1)S(1)}, bf16[512,512]{1,0:T(8,128)(2,1)S(1)}, u32[]{:S(2)}, u32[]{:S(2)}) %collective-permute-start.19) | collective-permute-done | bytes 524320 | tf_op jit(solution)/shard_map/ppermute | solution.py:29
  722.1 69.8 %exchange_5.1 = (bf16[256,2048]{1,0:T(8,128)(2,1)}, bf16[4,256,2048]{2,1,0:T(8,128)(2,1)S(1)}, bf16[256,512]{1,0:T(8,128)(2,1)S(1)}, bf16[3,512,256]{2,1,0:T(8,1...) custom-call(bf16[1024,2048]{1,0:T(8,128)(2,1)} %fusion.refs_0_, ...), custom_call_target="tpu_custom_call" | custom-call | tf_op jit(solution)/shard_map/exchange_5/pallas_call | solution.py:609
  802.6 3.1 fusion.50
  807.2 91.8 %exchange_6.1 = (bf16[384,2048]{1,0:T(8,128)(2,1)S(1)}, bf16[3,512,256]{2,1,0:T(8,128)(2,1)S(1)}, bf16[684,2048]{1,0:T(8,128)(2,1)S(1)}, bf16[684,2048]{1,0:T(8,...) custom-call(bf16[256,2048]{1,0:T(8,128)(2,1)S(1)} %copy-done.14, ...), custom_call_target="tpu_custom_call" | custom-call | tf_op jit(solution)/shard_map/exchange_6/pallas_call | solution.py:609
  910.1 45.9 %exchange_7.1 = (bf16[256,2048]{1,0:T(8,128)(2,1)S(1)}, bf16[3,2048,256]{2,1,0:T(8,128)(2,1)S(1)}, f32[8,8,256]{2,1,0:T(8,128)S(1)}, bf16[384,2048]{1,0:T(8,128)(2,1)S(1)}) custom-call(bf16[256,512]{1,0:T(8,128)(2,1)S(1)} %add_convert_fusion.22.refs_0_, bf16[3,512,256]{2,1,0:T(8,128)(2,1)S(1)} %add_convert_fusion.3.refs_1_, ...), custom_call_target="tpu_custom_call" | custom-call | tf_op jit(solution)/shard_map/exchange_7/pallas_call | solution.py:609
  963.1 3.2 convert_element_type.490
  966.4 3.7 convert_bitcast_fusion
  971.3 7.0 interleave.1
  (422 shorter events, 169.0 us)
Async XLA Ops:
  75.0 59.4 %copy-start.5 = (bf16[256,2048]{1,0:T(8,128)(2,1)}, bf16[256,2048]{1,0:T(8,128)(2,1)S(1)}, u32[]{:S(2)}) copy-start(bf16[256,2048]{1,0:T(8,128)(2,1)S(1)} %bitcast_select_fusion.1.refs_0_.refs_1_) | copy-start | bytes 3145732
  139.0 63.0 %collective-permute-start.10 = (bf16[85,2,2048]{2,1,0:T(2,128)(2,1)}, bf16[85,2,2048]{2,1,0:T(2,128)(2,1)}, u32[]{:S(2)}, u32[]{:S(2)}) collective-permute-start(bf16[85,2,2048]{2,1,0:T(2,128)(2,1)} %dynamic-slice_bitcast_fusion.4), channel_id=1, source_target_pairs={{0,4},{1,5},{2,6},{3,7},{4,0},{5,1},{6,2},{7,3},{8,12},{9,13},{10,... | collective-permute-start | bytes 2088968 | tf_op jit(solution)/shard_map/ppermute | solution.py:29
  139.8 62.2 %collective-permute-start.11 = (bf16[684,512]{1,0:T(8,128)(2,1)}, bf16[684,512]{1,0:T(8,128)(2,1)}, u32[]{:S(2)}, u32[]{:S(2)}) collective-permute-start(bf16[684,512]{1,0:T(8,128)(2,1)} %constant_dynamic-slice_fusion.9), channel_id=1, source_target_pairs={{0,4},{1,5},{2,6},{3,7},{4,0},{5,1},{6,2},{7,3},{8,12},{9,13},{10,... | collective-permute-start | bytes 2101256 | tf_op jit(solution)/shard_map/ppermute | solution.py:29
  144.3 192.6 %copy-start.121 = (pred[684]{0:T(1024)(128)(4,1)}, pred[684]{0:T(1024)(128)(4,1)S(1)}, u32[]{:S(2)}) copy-start(pred[684]{0:T(1024)(128)(4,1)S(1)} %add_compare_fusion.1) | copy-start | bytes 2056
  147.8 25.2 %copy-start.72 = (s32[8,128]{1,0:T(8,128)}, s32[8,128]{1,0:T(8,128)S(1)}, u32[]{:S(2)}) copy-start(s32[8,128]{1,0:T(8,128)S(1)} %iota_add_fusion) | copy-start | bytes 12292
  167.2 152.3 %copy-start.123 = (pred[684]{0:T(1024)(128)(4,1)}, pred[684]{0:T(1024)(128)(4,1)S(1)}, u32[]{:S(2)}) copy-start(pred[684]{0:T(1024)(128)(4,1)S(1)} %add_compare_fusion) | copy-start | bytes 2056
  197.6 111.4 %slice-start = ((s8[5603328]{0:T(1024)(128)(4,1)}), s8[1409024]{0:T(1024)(128)(4,1)S(1)}, s32[]{:S(2)}) async-start(s8[5603328]{0:T(1024)(128)(4,1)} %bitcast.282), calls=%async_computation | async-start | bytes 2818048
  202.0 107.0 %slice-start.1 = ((s8[5603328]{0:T(1024)(128)(4,1)}), s8[4194304]{0:T(1024)(128)(4,1)S(1)}, s32[]{:S(2)}) async-start(s8[5603328]{0:T(1024)(128)(4,1)} %bitcast.282), calls=%async_computation.1 | async-start | bytes 8388608
  323.5 143.7 %copy-start.93 = (bf16[1024,684]{0,1:T(8,128)(2,1)}, bf16[1024,684]{0,1:T(8,128)(2,1)S(1)}, u32[]{:S(2)}) copy-start(bf16[1024,684]{0,1:T(8,128)(2,1)S(1)} %select_convert_fusion) | copy-start | bytes 4202500
  348.2 93.7 %copy-start.122 = (pred[684]{0:T(1024)(128)(4,1)S(1)}, pred[684]{0:T(1024)(128)(4,1)}, u32[]{:S(2)}) copy-start(pred[684]{0:T(1024)(128)(4,1)} %copy-done.121) | copy-start | bytes 2056
  441.9 25.1 %copy-start.49 = (bf16[1024,2048]{1,0:T(8,128)(2,1)}, bf16[1024,2048]{1,0:T(8,128)(2,1)S(1)}, u32[]{:S(2)}) copy-start(bf16[1024,2048]{1,0:T(8,128)(2,1)S(1)} %get-tuple-element.166) | copy-start | bytes 12582916
  485.2 34.9 %collective-permute-start.15 = (bf16[684,1024]{1,0:T(8,128)(2,1)}, bf16[684,1024]{1,0:T(8,128)(2,1)}, u32[]{:S(2)}, u32[]{:S(2)}) collective-permute-start(bf16[684,1024]{1,0:T(8,128)(2,1)} %convolution_convert_fusion.6), channel_id=1, source_target_pairs={{0,8},{8,0},{16,24},{24,16},{1,9},{9,1},{17,25},{25,17},{2,10},{10... | collective-permute-start | bytes 4202504 | tf_op jit(solution)/shard_map/ppermute | solution.py:29
  485.2 41.6 %collective-permute-start.14 = (bf16[684,1024]{1,0:T(8,128)(2,1)}, bf16[684,1024]{1,0:T(8,128)(2,1)}, u32[]{:S(2)}, u32[]{:S(2)}) collective-permute-start(bf16[684,1024]{1,0:T(8,128)(2,1)} %convolution_convert_fusion.7), channel_id=1, source_target_pairs={{0,8},{8,0},{16,24},{24,16},{1,9},{9,1},{17,25},{25,17},{2,10},{10... | collective-permute-start | bytes 4202504 | tf_op jit(solution)/shard_map/ppermute | solution.py:29
  485.7 28.1 %collective-permute-start.12 = (bf16[684,1024]{1,0:T(8,128)(2,1)}, bf16[684,1024]{1,0:T(8,128)(2,1)}, u32[]{:S(2)}, u32[]{:S(2)}) collective-permute-start(bf16[684,1024]{1,0:T(8,128)(2,1)} %convolution_convert_fusion.8), channel_id=1, source_target_pairs={{0,8},{8,0},{16,24},{24,16},{1,9},{9,1},{17,25},{25,17},{2,10},{10... | collective-permute-start | bytes 4202504 | tf_op jit(solution)/shard_map/ppermute | solution.py:29
  485.7 31.2 %collective-permute-start.24 = (bf16[684,1024]{1,0:T(8,128)(2,1)}, bf16[684,1024]{1,0:T(8,128)(2,1)}, u32[]{:S(2)}, u32[]{:S(2)}) collective-permute-start(bf16[684,1024]{1,0:T(8,128)(2,1)} %convolution_convert_fusion.3), channel_id=1, source_target_pairs={{0,8},{8,0},{16,24},{24,16},{1,9},{9,1},{17,25},{25,17},{2,10},{10... | collective-permute-start | bytes 4202504 | tf_op jit(solution)/shard_map/ppermute | solution.py:29
  513.7 20.3 %collective-permute-start.17 = (bf16[684,1024]{1,0:T(8,128)(2,1)}, bf16[684,1024]{1,0:T(8,128)(2,1)S(1)}, u32[]{:S(2)}, u32[]{:S(2)}) collective-permute-start(bf16[684,1024]{1,0:T(8,128)(2,1)} %convolution_convert_fusion.4), channel_id=1, source_target_pairs={{0,8},{8,0},{16,24},{24,16},{1,9},{9,1},{17,25},{25,17},{2,10},{10... | collective-permute-start | bytes 4202504 | tf_op jit(solution)/shard_map/ppermute | solution.py:29
  513.7 25.8 %collective-permute-start.16 = (bf16[684,1024]{1,0:T(8,128)(2,1)}, bf16[684,1024]{1,0:T(8,128)(2,1)S(1)}, u32[]{:S(2)}, u32[]{:S(2)}) collective-permute-start(bf16[684,1024]{1,0:T(8,128)(2,1)} %convolution_convert_fusion.5), channel_id=1, source_target_pairs={{0,8},{8,0},{16,24},{24,16},{1,9},{9,1},{17,25},{25,17},{2,10},{10... | collective-permute-start | bytes 4202504 | tf_op jit(solution)/shard_map/ppermute | solution.py:29
  516.9 25.4 %collective-permute-start.13 = (bf16[684,512]{1,0:T(8,128)(2,1)S(1)}, bf16[684,512]{1,0:T(8,128)(2,1)S(1)}, u32[]{:S(2)}, u32[]{:S(2)}) collective-permute-start(bf16[684,512]{1,0:T(8,128)(2,1)S(1)} %add_convert_fusion.17), channel_id=1, source_target_pairs={{0,16},{8,24},{16,0},{24,8},{1,17},{9,25},{17,1},{25,9},{2,18},{10... | collective-permute-start | bytes 2101256 | tf_op jit(solution)/shard_map/ppermute | solution.py:29
  520.1 178.7 %collective-permute-start.25 = (bf16[684,512]{1,0:T(8,128)(2,1)}, bf16[684,512]{1,0:T(8,128)(2,1)}, u32[]{:S(2)}, u32[]{:S(2)}) collective-permute-start(bf16[684,512]{1,0:T(8,128)(2,1)} %add_convert_fusion.13), channel_id=1, source_target_pairs={{0,16},{8,24},{16,0},{24,8},{1,17},{9,25},{17,1},{25,9},{2,18},{10... | collective-permute-start | bytes 2101256 | tf_op jit(solution)/shard_map/ppermute | solution.py:29
  542.5 89.2 %copy-start.21 = (bf16[684,512]{1,0:T(8,128)(2,1)}, bf16[684,512]{1,0:T(8,128)(2,1)S(1)}, u32[]{:S(2)}) copy-start(bf16[684,512]{1,0:T(8,128)(2,1)S(1)} %add_convert_fusion.16.refs_8_) | copy-start | bytes 2101252
  544.3 80.1 %copy-start.116 = (bf16[512,2048]{1,0:T(8,128)(2,1)S(1)}, bf16[512,2048]{1,0:T(8,128)(2,1)}, u32[]{:S(2)}) copy-start(bf16[512,2048]{1,0:T(8,128)(2,1)} %copy-done.114) | copy-start | bytes 6291460
  633.4 45.0 %collective-permute-start.20 = (bf16[684,512]{1,0:T(8,128)(2,1)}, bf16[684,512]{1,0:T(8,128)(2,1)S(1)}, u32[]{:S(2)}, u32[]{:S(2)}) collective-permute-start(bf16[684,512]{1,0:T(8,128)(2,1)} %copy-done.21), channel_id=1, source_target_pairs={{0,4},{1,5},{2,6},{3,7},{4,0},{5,1},{6,2},{7,3},{8,12},{9,13},{10,... | collective-permute-start | bytes 2101256 | tf_op jit(solution)/shard_map/ppermute | solution.py:29
  635.8 64.7 %collective-permute-start.23 = (bf16[684,512]{1,0:T(8,128)(2,1)S(1)}, bf16[684,512]{1,0:T(8,128)(2,1)S(1)}, u32[]{:S(2)}, u32[]{:S(2)}) collective-permute-start(bf16[684,512]{1,0:T(8,128)(2,1)S(1)} %add_convert_fusion.15), channel_id=1, source_target_pairs={{0,4},{1,5},{2,6},{3,7},{4,0},{5,1},{6,2},{7,3},{8,12},{9,13},{10,... | collective-permute-start | bytes 2101256 | tf_op jit(solution)/shard_map/ppermute | solution.py:29
  640.9 59.9 %collective-permute-start.18 = (bf16[512,1024]{1,0:T(8,128)(2,1)S(1)}, bf16[512,1024]{1,0:T(8,128)(2,1)S(1)}, u32[]{:S(2)}, u32[]{:S(2)}) collective-permute-start(bf16[512,1024]{1,0:T(8,128)(2,1)S(1)} %fusion.56), channel_id=1, source_target_pairs={{0,8},{8,0},{16,24},{24,16},{1,9},{9,1},{17,25},{25,17},{2,10},{10... | collective-permute-start | bytes 3145736 | tf_op jit(solution)/shard_map/ppermute | solution.py:29
  641.1 22.4 %copy-start.62 = (bf16[684,512]{1,0:T(8,128)(2,1)S(1)}, bf16[684,512]{1,0:T(8,128)(2,1)}, u32[]{:S(2)}) copy-start(bf16[684,512]{1,0:T(8,128)(2,1)} %copy-done.61) | copy-start | bytes 2101252
  641.1 22.4 %copy-start.108 = (bf16[684,512]{1,0:T(8,128)(2,1)S(1)}, bf16[684,512]{1,0:T(8,128)(2,1)}, u32[]{:S(2)}) copy-start(bf16[684,512]{1,0:T(8,128)(2,1)} %fusion.64) | copy-start | bytes 2101252
  641.1 37.3 %copy-start.4 = (bf16[2048,3,256]{2,0,1:T(8,128)(2,1)S(1)}, bf16[2048,3,256]{2,0,1:T(8,128)(2,1)}, u32[]{:S(2)}) copy-start(bf16[2048,3,256]{2,0,1:T(8,128)(2,1)} %param.28) | copy-start | bytes 9437188
  663.4 34.6 %copy-start.34 = (bf16[3,1024,256]{2,1,0:T(8,128)(2,1)}, bf16[3,1024,256]{2,1,0:T(8,128)(2,1)S(1)}, u32[]{:S(2)}) copy-start(bf16[3,1024,256]{2,1,0:T(8,128)(2,1)S(1)} %get-tuple-element.174) | copy-start | bytes 4718596
  663.4 34.9 %copy-start.36 = (bf16[3,1024,256]{2,1,0:T(8,128)(2,1)}, bf16[3,1024,256]{2,1,0:T(8,128)(2,1)S(1)}, u32[]{:S(2)}) copy-start(bf16[3,1024,256]{2,1,0:T(8,128)(2,1)S(1)} %get-tuple-element.175) | copy-start | bytes 4718596
  690.3 27.0 %collective-permute-start.22 = (bf16[3,1024,256]{2,1,0:T(8,128)(2,1)}, bf16[3,1024,256]{2,1,0:T(8,128)(2,1)}, u32[]{:S(2)}, u32[]{:S(2)}) collective-permute-start(bf16[3,1024,256]{2,1,0:T(8,128)(2,1)} %fusion.55), channel_id=1, source_target_pairs={{0,8},{8,0},{16,24},{24,16},{1,9},{9,1},{17,25},{25,17},{2,10},{10... | collective-permute-start | bytes 4718600 | tf_op jit(solution)/shard_map/ppermute | solution.py:29
  690.3 29.4 %collective-permute-start.21 = (bf16[3,1024,256]{2,1,0:T(8,128)(2,1)}, bf16[3,1024,256]{2,1,0:T(8,128)(2,1)}, u32[]{:S(2)}, u32[]{:S(2)}) collective-permute-start(bf16[3,1024,256]{2,1,0:T(8,128)(2,1)} %fusion.54), channel_id=1, source_target_pairs={{0,8},{8,0},{16,24},{24,16},{1,9},{9,1},{17,25},{25,17},{2,10},{10... | collective-permute-start | bytes 4718600 | tf_op jit(solution)/shard_map/ppermute | solution.py:29
  703.3 13.9 %collective-permute-start.19 = (bf16[512,512]{1,0:T(8,128)(2,1)S(1)}, bf16[512,512]{1,0:T(8,128)(2,1)S(1)}, u32[]{:S(2)}, u32[]{:S(2)}) collective-permute-start(bf16[512,512]{1,0:T(8,128)(2,1)S(1)} %add_convert_fusion.20), channel_id=1, source_target_pairs={{0,16},{8,24},{16,0},{24,8},{1,17},{9,25},{17,1},{25,9},{2,18},{10... | collective-permute-start | bytes 1572872 | tf_op jit(solution)/shard_map/ppermute | solution.py:29
  (116 other events, 583.2 us)

commit v5 on v4

--- a/solution.py
+++ b/solution.py
@@ -1165,11 +1165,11 @@
         grad_att_all, wo, (((1,), (1,)), ((), ())), preferred_element_type=f32
     ).astype(bf16)
     out_keep, out_send = halve(columns_of(grad_att_all), ein("tn,td->nd", context), 1)
-    out = add(out_keep, permute(out_send, "dp", n_dp, dp_bits[-1])).reshape(2, width_qkv, share)
     grad_linear = attend_back(
         turned, grad_context, place, cos_table, -sin_table, key_at, query_at, rows
     )
-    down_came, *grad_linear = lax.optimization_barrier((down_came, *grad_linear))
+    down_came, out_send, *grad_linear = lax.optimization_barrier((down_came, out_send, *grad_linear))
+    out = add(out_keep, permute(out_send, "dp", n_dp, dp_bits[-1])).reshape(2, width_qkv, share)
     down = add(down[0], down_came)
     token_columns = columns_of(tokens_all)
     qkv_keep, qkv_send = zip(

time: 990 us -> 978 us (0.988)
  matrix products: 179 us -> 167 us
    unnamed x268 -> x266, local copies, waits for them, and re-layouts: 42 us -> 45.9 us
  transfers between devices with their start and end apart: 16 -> 16, of which waited for: 2 -> 3; matrix products, arithmetic and copies ran while one was open for 13% -> 12% of each run, Pallas kernels for 12% -> 12%
where the time goes in v5:
time: 978 us; the launch traced here: 968 us
  Pallas kernels  644 us (66%)
  matrix products  167 us (17%)
  local copies, waits for them, and re-layouts  66.2 us (7%)
  other arithmetic  47.6 us (5%)
  waiting for transfers between devices  18.1 us (2%)
  between operations  13 us (1%)
  starting transfers between devices  12.1 us (1%)
    pallas_call x8, Pallas kernels, exchange(): pl.pallas_call(kernel, out_shape=shapes, in_specs=[vmem] * n_in + [anywhe...  599 us
    dot_general x27, matrix products, ein(): return lambda b: jnp.einsum(spec, a, b, preferred_element_type=f32)  67.7 us
    unnamed x266, local copies, waits for them, and re-layouts  45.9 us
    dot_general x6, matrix products, sum_of(): jnp.einsum(spec, a[p], b[p], preferred_element_type=f32)  43.9 us
    pallas_call x1, Pallas kernels, attend_back(): pl.pallas_call(functools.partial(attend_back_kernel, heads, rows), out_sh...  22.5 us
  transfers between devices with their start and end apart: 16, of which 3 were waited for; matrix products, arithmetic and copies ran while one was open for 12% of the time, Pallas kernels for 12%

profile of v5, /device:TPU:10, one launch (start us, length us, event | category | flops | bytes accessed | tf_op | source)
XLA Modules:
  0.0 968.0 jit_solution(13916626560398739121)
XLA Ops:
  17.8 55.4 %exchange_0.1 = (bf16[256,2048]{1,0:T(8,128)(2,1)}, bf16[4,256,2048]{2,1,0:T(8,128)(2,1)}, bf16[3,256,256]{2,1,0:T(8,128)(2,1)S(1)}, s32[4,8,128]{2,1,0:T(8,128)...) custom-call(bf16[384,2048]{1,0:T(8,128)(2,1)S(1)} %copy-done.35, bf16[3,2048,256]{2,1,0:T(8,128)(2,1)S(1)} %bitcast.265, ...), custom_call_target="tpu_custom_call" | custom-call | tf_op jit(solution)/shard_map/exchange_0/pallas_call | solution.py:609
  77.0 57.8 %exchange_1.1 = (bf16[3,2048,256]{2,1,0:T(8,128)(2,1)S(1)}, bf16[256,2048]{1,0:T(8,128)(2,1)S(1)}, bf16[1024,2048]{1,0:T(8,128)(2,1)S(1)}) custom-call(bf16[256,2048]{1,0:T(8,128)(2,1)S(1)} %bitcast_select_fusion.1.refs_0_.refs_1_, bf16[3,256,256]{2,1,0:T(8,128)(2,1)S(1)} %get-tuple-element.151.refs_1_, bf16[3,2048,256]{2,1,0:T(8,128)(2,1)S(1)} %bitcast.266, ...), custom_call_target="tpu_custom_call" | custom-call | tf_op jit(solution)/shard_map/exchange_1/pallas_call | solution.py:609
  148.8 8.4 fusion.44.own
  157.2 5.1 fusion.47.other
  179.3 15.5 %attend.1 = (bf16[1024,1536]{1,0:T(8,128)(2,1)S(1)}, bf16[1024,512]{1,0:T(8,128)(2,1)S(1)}) custom-call(s32[1]{0:T(128)} %bitcast.12.place, f32[3,1024,256]{2,1,0:T(8,128)S(1)} %copy-done.16, f32[3,1024,256]{2,1,0:T(8,128)S(1)} %copy-done.17, f32[2,3,256]{2,1,0:T(4,128)S(1)} %pad_maximum_fusion.6.bias, f32[1024,128]{1,0:T(8,128)S(1)} %copy-done.10, ...), custom_call_target="tpu_custom_call" | custom-call | tf_op jit(solution)/shard_map/attend/pallas_call | solution.py:787
  198.0 4.4 convolution_convert_fusion.refs_0_
  202.4 105.7 %exchange_2.1 = (f32[256,2048]{1,0:T(8,128)S(1)}, bf16[684,2,2048]{2,1,0:T(2,128)(2,1)}, bf16[684,2048]{1,0:T(8,128)(2,1)S(1)}, bf16[256,2048]{1,0:T(8,128)(2,1)...) custom-call(bf16[1024,2048]{1,0:T(8,128)(2,1)} %convolution_convert_fusion.refs_0_, ...), custom_call_target="tpu_custom_call" | custom-call | tf_op jit(solution)/shard_map/exchange_2/pallas_call | solution.py:609
  310.0 8.8 bitcast_add_fusion.2
  320.5 3.9 select_convert_fusion
  324.5 5.7 fusion.150
  330.2 7.6 bitcast_add_fusion.3
  341.7 7.4 add_convert_fusion.refs_0_
  349.2 92.4 %exchange_3.1 = (bf16[256,2048]{1,0:T(8,128)(2,1)}, f32[256,2048]{1,0:T(8,128)S(1)}, f32[3,8,2048]{2,1,0:T(8,128)S(1)}, bf16[4,256,2048]{2,1,0:T(8,128)(2,1)S(1)}, bf16[1024,2048]{1,0:T(8,128)(2,1)S(1)}) custom-call(bf16[1024,2048]{1,0:T(8,128)(2,1)} %add_convert_fusion.refs_0_, f32[256,2048]{1,0:T(8,128)S(1)} %copy-done.8, ...), custom_call_target="tpu_custom_call" | custom-call | tf_op jit(solution)/shard_map/exchange_3/pallas_call | solution.py:609
  441.7 10.6 %multiply_bitcast_fusion = (f32[1,1024,684]{1,2,0:T(8,128)}, f32[1,1024,684]{1,2,0:T(8,128)}) fusion(pred[684]{0:T(1024)(128)(4,1)S(1)} %copy-done.120, f32[2,1024,684]{1,2,0:T(8,128)} %copy-done.85, bf16[1024,2048]{1,0:T(8,128)(2,1)S(1)} %get-tuple-element.167, bf16[684,2048]{1,0:T(8,128)(2,1)S(1)} %copy-done.79), kind=kOutput, calls=%fused_computation.58 | convolution fusion | flops 2885013504 | bytes 18203308 | tf_op jit(solution)/shard_map/td,nd->tn/dot_general | solution.py:1123
  452.3 6.9 multiply_bitcast_fusion.1
  472.4 10.2 %fusion.2 = f32[1024,2048,1]{1,0,2:T(8,128)} fusion(bf16[2,1024,684]{1,2,0:T(8,128)(2,1)S(1)} %get-tuple-element.211, bf16[684,2,2048]{2,1,0:T(2,128)(2,1)S(1)} %bitcast.287), kind=kOutput, calls=%fused_computation.19 | convolution fusion | flops 5737807872 | bytes 16793600 | tf_op jit(solution)/shard_map/ctn,ncd->td/dot_general | solution.py:1034
  484.9 3.2 convert_reduce_fusion
  491.9 11.9 %fusion.1.refs_0_ = bf16[1024,2048]{1,0:T(8,128)(2,1)} fusion(f32[1024,2048,1]{1,0,2:T(8,128)} %fusion.2, bf16[2,1024,684]{1,2,0:T(8,128)(2,1)S(1)} %get-tuple-element.213, bf16[684,2,2048]{2,1,0:T(2,128)(2,1)S(1)} %bitcast.306), kind=kOutput, calls=%fused_computation.10 | convolution fusion | flops 5742002176 | bytes 20987904 | tf_op jit(solution)/shard_map/ctn,ncd->td/dot_general | solution.py:1034
  540.7 80.2 %exchange_4.1 = (f32[256,2048]{1,0:T(8,128)S(1)}, f32[3,8,2048]{2,1,0:T(8,128)S(1)}, bf16[684,512]{1,0:T(8,128)(2,1)S(1)}, bf16[684,512]{1,0:T(8,128)(2,1)S(1)},...) custom-call(bf16[1024,2048]{1,0:T(8,128)(2,1)} %fusion.1.refs_0_, ...), custom_call_target="tpu_custom_call" | custom-call | tf_op jit(solution)/shard_map/exchange_4/pallas_call | solution.py:609
  627.0 3.3 convolution_convert_fusion.9.grad_context
  637.8 22.5 %attend_back.1 = (bf16[3,1024,256]{2,1,0:T(8,128)(2,1)S(1)}, bf16[3,1024,256]{2,1,0:T(8,128)(2,1)S(1)}) custom-call(s32[1]{0:T(128)} %bitcast.12.place, bf16[1024,1536]{1,0:T(8,128)(2,1)S(1)} %copy-done.19, bf16[1024,512]{1,0:T(8,128)(2,1)S(1)} %copy-done.50, f32[1024,128]{1,0:T(8,128)S(1)} %copy-done.11, f32[1024,128]{1,0:T(8,128)S(1)} %copy-done.30, ...), custom_call_target="tpu_custom_call" | custom-call | tf_op jit(solution)/shard_map/attend_back/pallas_call | solution.py:861
  661.4 4.9 collective-permute-done.23.refs_5_
  670.6 10.7 %collective-permute-done.19 = bf16[684,512]{1,0:T(8,128)(2,1)S(1)} collective-permute-done((bf16[684,512]{1,0:T(8,128)(2,1)}, bf16[684,512]{1,0:T(8,128)(2,1)S(1)}, u32[]{:S(2)}, u32[]{:S(2)}) %collective-permute-start.19) | collective-permute-done | bytes 700448 | tf_op jit(solution)/shard_map/ppermute | solution.py:29
  687.8 3.5 fusion.142
  694.4 5.2 fusion.refs_0_
  711.1 69.8 %exchange_5.1 = (bf16[256,2048]{1,0:T(8,128)(2,1)}, bf16[4,256,2048]{2,1,0:T(8,128)(2,1)S(1)}, bf16[256,512]{1,0:T(8,128)(2,1)S(1)}, bf16[3,512,256]{2,1,0:T(8,1...) custom-call(bf16[1024,2048]{1,0:T(8,128)(2,1)} %fusion.refs_0_, ...), custom_call_target="tpu_custom_call" | custom-call | tf_op jit(solution)/shard_map/exchange_5/pallas_call | solution.py:609
  791.4 3.1 fusion.50
  796.0 92.2 %exchange_6.1 = (bf16[384,2048]{1,0:T(8,128)(2,1)S(1)}, bf16[3,512,256]{2,1,0:T(8,128)(2,1)S(1)}, bf16[684,2048]{1,0:T(8,128)(2,1)S(1)}, bf16[684,2048]{1,0:T(8,...) custom-call(bf16[256,2048]{1,0:T(8,128)(2,1)S(1)} %copy-done.14, ...), custom_call_target="tpu_custom_call" | custom-call | tf_op jit(solution)/shard_map/exchange_6/pallas_call | solution.py:609
  899.3 45.9 %exchange_7.1 = (bf16[256,2048]{1,0:T(8,128)(2,1)S(1)}, bf16[3,2048,256]{2,1,0:T(8,128)(2,1)S(1)}, f32[8,8,256]{2,1,0:T(8,128)S(1)}, bf16[384,2048]{1,0:T(8,128)(2,1)S(1)}) custom-call(bf16[256,512]{1,0:T(8,128)(2,1)S(1)} %add_convert_fusion.22.refs_0_, bf16[3,512,256]{2,1,0:T(8,128)(2,1)S(1)} %add_convert_fusion.3.refs_1_, ...), custom_call_target="tpu_custom_call" | custom-call | tf_op jit(solution)/shard_map/exchange_7/pallas_call | solution.py:609
  952.4 3.2 convert_element_type.490
  955.7 3.7 convert_bitcast_fusion
  960.6 7.0 interleave.1
  (421 shorter events, 178.9 us)
Async XLA Ops:
  75.1 59.7 %copy-start.5 = (bf16[256,2048]{1,0:T(8,128)(2,1)}, bf16[256,2048]{1,0:T(8,128)(2,1)S(1)}, u32[]{:S(2)}) copy-start(bf16[256,2048]{1,0:T(8,128)(2,1)S(1)} %bitcast_select_fusion.1.refs_0_.refs_1_) | copy-start | bytes 3145732
  139.4 63.0 %collective-permute-start.10 = (bf16[85,2,2048]{2,1,0:T(2,128)(2,1)}, bf16[85,2,2048]{2,1,0:T(2,128)(2,1)}, u32[]{:S(2)}, u32[]{:S(2)}) collective-permute-start(bf16[85,2,2048]{2,1,0:T(2,128)(2,1)} %dynamic-slice_bitcast_fusion.4), channel_id=1, source_target_pairs={{0,4},{1,5},{2,6},{3,7},{4,0},{5,1},{6,2},{7,3},{8,12},{9,13},{10,... | collective-permute-start | bytes 2088968 | tf_op jit(solution)/shard_map/ppermute | solution.py:29
  140.2 62.2 %collective-permute-start.11 = (bf16[684,512]{1,0:T(8,128)(2,1)}, bf16[684,512]{1,0:T(8,128)(2,1)}, u32[]{:S(2)}, u32[]{:S(2)}) collective-permute-start(bf16[684,512]{1,0:T(8,128)(2,1)} %constant_dynamic-slice_fusion.9), channel_id=1, source_target_pairs={{0,4},{1,5},{2,6},{3,7},{4,0},{5,1},{6,2},{7,3},{8,12},{9,13},{10,... | collective-permute-start | bytes 2101256 | tf_op jit(solution)/shard_map/ppermute | solution.py:29
  144.6 193.2 %copy-start.119 = (pred[684]{0:T(1024)(128)(4,1)}, pred[684]{0:T(1024)(128)(4,1)S(1)}, u32[]{:S(2)}) copy-start(pred[684]{0:T(1024)(128)(4,1)S(1)} %add_compare_fusion.1) | copy-start | bytes 2056
  148.2 25.3 %copy-start.68 = (s32[8,128]{1,0:T(8,128)}, s32[8,128]{1,0:T(8,128)S(1)}, u32[]{:S(2)}) copy-start(s32[8,128]{1,0:T(8,128)S(1)} %iota_add_fusion) | copy-start | bytes 12292
  167.5 153.0 %copy-start.121 = (pred[684]{0:T(1024)(128)(4,1)}, pred[684]{0:T(1024)(128)(4,1)S(1)}, u32[]{:S(2)}) copy-start(pred[684]{0:T(1024)(128)(4,1)S(1)} %add_compare_fusion) | copy-start | bytes 2056
  198.0 112.0 %slice-start = ((s8[5603328]{0:T(1024)(128)(4,1)}), s8[1409024]{0:T(1024)(128)(4,1)S(1)}, s32[]{:S(2)}) async-start(s8[5603328]{0:T(1024)(128)(4,1)} %bitcast.282), calls=%async_computation | async-start | bytes 2818048
  202.4 107.5 %slice-start.1 = ((s8[5603328]{0:T(1024)(128)(4,1)}), s8[4194304]{0:T(1024)(128)(4,1)S(1)}, s32[]{:S(2)}) async-start(s8[5603328]{0:T(1024)(128)(4,1)} %bitcast.282), calls=%async_computation.1 | async-start | bytes 8388608
  324.5 142.5 %copy-start.91 = (bf16[1024,684]{0,1:T(8,128)(2,1)}, bf16[1024,684]{0,1:T(8,128)(2,1)S(1)}, u32[]{:S(2)}) copy-start(bf16[1024,684]{0,1:T(8,128)(2,1)S(1)} %select_convert_fusion) | copy-start | bytes 4202500
  349.2 92.5 %copy-start.120 = (pred[684]{0:T(1024)(128)(4,1)S(1)}, pred[684]{0:T(1024)(128)(4,1)}, u32[]{:S(2)}) copy-start(pred[684]{0:T(1024)(128)(4,1)} %copy-done.119) | copy-start | bytes 2056
  441.6 25.1 %copy-start.46 = (bf16[1024,2048]{1,0:T(8,128)(2,1)}, bf16[1024,2048]{1,0:T(8,128)(2,1)S(1)}, u32[]{:S(2)}) copy-start(bf16[1024,2048]{1,0:T(8,128)(2,1)S(1)} %get-tuple-element.167) | copy-start | bytes 12582916
  490.9 24.4 %collective-permute-start.15 = (bf16[684,1024]{1,0:T(8,128)(2,1)}, bf16[684,1024]{1,0:T(8,128)(2,1)}, u32[]{:S(2)}, u32[]{:S(2)}) collective-permute-start(bf16[684,1024]{1,0:T(8,128)(2,1)} %convolution_convert_fusion.6), channel_id=1, source_target_pairs={{0,8},{8,0},{16,24},{24,16},{1,9},{9,1},{17,25},{25,17},{2,10},{10... | collective-permute-start | bytes 4202504 | tf_op jit(solution)/shard_map/ppermute | solution.py:29
  490.9 31.1 %collective-permute-start.14 = (bf16[684,1024]{1,0:T(8,128)(2,1)}, bf16[684,1024]{1,0:T(8,128)(2,1)}, u32[]{:S(2)}, u32[]{:S(2)}) collective-permute-start(bf16[684,1024]{1,0:T(8,128)(2,1)} %convolution_convert_fusion.7), channel_id=1, source_target_pairs={{0,8},{8,0},{16,24},{24,16},{1,9},{9,1},{17,25},{25,17},{2,10},{10... | collective-permute-start | bytes 4202504 | tf_op jit(solution)/shard_map/ppermute | solution.py:29
  491.4 37.7 %collective-permute-start.17 = (bf16[684,1024]{1,0:T(8,128)(2,1)}, bf16[684,1024]{1,0:T(8,128)(2,1)}, u32[]{:S(2)}, u32[]{:S(2)}) collective-permute-start(bf16[684,1024]{1,0:T(8,128)(2,1)} %convolution_convert_fusion.4), channel_id=1, source_target_pairs={{0,8},{8,0},{16,24},{24,16},{1,9},{9,1},{17,25},{25,17},{2,10},{10... | collective-permute-start | bytes 4202504 | tf_op jit(solution)/shard_map/ppermute | solution.py:29
  491.4 17.6 %collective-permute-start.12 = (bf16[684,1024]{1,0:T(8,128)(2,1)}, bf16[684,1024]{1,0:T(8,128)(2,1)}, u32[]{:S(2)}, u32[]{:S(2)}) collective-permute-start(bf16[684,1024]{1,0:T(8,128)(2,1)} %convolution_convert_fusion.8), channel_id=1, source_target_pairs={{0,8},{8,0},{16,24},{24,16},{1,9},{9,1},{17,25},{25,17},{2,10},{10... | collective-permute-start | bytes 4202504 | tf_op jit(solution)/shard_map/ppermute | solution.py:29
  491.9 20.2 %collective-permute-start.24 = (bf16[684,1024]{1,0:T(8,128)(2,1)}, bf16[684,1024]{1,0:T(8,128)(2,1)}, u32[]{:S(2)}, u32[]{:S(2)}) collective-permute-start(bf16[684,1024]{1,0:T(8,128)(2,1)} %convolution_convert_fusion.3), channel_id=1, source_target_pairs={{0,8},{8,0},{16,24},{24,16},{1,9},{9,1},{17,25},{25,17},{2,10},{10... | collective-permute-start | bytes 4202504 | tf_op jit(solution)/shard_map/ppermute | solution.py:29
  509.0 27.9 %collective-permute-start.16 = (bf16[684,1024]{1,0:T(8,128)(2,1)}, bf16[684,1024]{1,0:T(8,128)(2,1)S(1)}, u32[]{:S(2)}, u32[]{:S(2)}) collective-permute-start(bf16[684,1024]{1,0:T(8,128)(2,1)} %convolution_convert_fusion.5), channel_id=1, source_target_pairs={{0,8},{8,0},{16,24},{24,16},{1,9},{9,1},{17,25},{25,17},{2,10},{10... | collective-permute-start | bytes 4202504 | tf_op jit(solution)/shard_map/ppermute | solution.py:29
  512.1 26.6 %collective-permute-start.13 = (bf16[684,512]{1,0:T(8,128)(2,1)S(1)}, bf16[684,512]{1,0:T(8,128)(2,1)S(1)}, u32[]{:S(2)}, u32[]{:S(2)}) collective-permute-start(bf16[684,512]{1,0:T(8,128)(2,1)S(1)} %add_convert_fusion.17), channel_id=1, source_target_pairs={{0,16},{8,24},{16,0},{24,8},{1,17},{9,25},{17,1},{25,9},{2,18},{10... | collective-permute-start | bytes 2101256 | tf_op jit(solution)/shard_map/ppermute | solution.py:29
  515.2 186.9 %collective-permute-start.25 = (bf16[684,512]{1,0:T(8,128)(2,1)}, bf16[684,512]{1,0:T(8,128)(2,1)}, u32[]{:S(2)}, u32[]{:S(2)}) collective-permute-start(bf16[684,512]{1,0:T(8,128)(2,1)} %add_convert_fusion.13), channel_id=1, source_target_pairs={{0,16},{8,24},{16,0},{24,8},{1,17},{9,25},{17,1},{25,9},{2,18},{10... | collective-permute-start | bytes 2101256 | tf_op jit(solution)/shard_map/ppermute | solution.py:29
  622.0 44.3 %collective-permute-start.23 = (bf16[684,512]{1,0:T(8,128)(2,1)}, bf16[684,512]{1,0:T(8,128)(2,1)}, u32[]{:S(2)}, u32[]{:S(2)}) collective-permute-start(bf16[684,512]{1,0:T(8,128)(2,1)} %add_convert_fusion.15), channel_id=1, source_target_pairs={{0,4},{1,5},{2,6},{3,7},{4,0},{5,1},{6,2},{7,3},{8,12},{9,13},{10,... | collective-permute-start | bytes 2101256 | tf_op jit(solution)/shard_map/ppermute | solution.py:29
  627.0 40.7 %collective-permute-start.18 = (bf16[512,1024]{1,0:T(8,128)(2,1)}, bf16[512,1024]{1,0:T(8,128)(2,1)}, u32[]{:S(2)}, u32[]{:S(2)}) collective-permute-start(bf16[512,1024]{1,0:T(8,128)(2,1)} %fusion.56), channel_id=1, source_target_pairs={{0,8},{8,0},{16,24},{24,16},{1,9},{9,1},{17,25},{25,17},{2,10},{10... | collective-permute-start | bytes 3145736 | tf_op jit(solution)/shard_map/ppermute | solution.py:29
  630.4 50.8 %collective-permute-start.19 = (bf16[684,512]{1,0:T(8,128)(2,1)}, bf16[684,512]{1,0:T(8,128)(2,1)S(1)}, u32[]{:S(2)}, u32[]{:S(2)}) collective-permute-start(bf16[684,512]{1,0:T(8,128)(2,1)} %add_convert_fusion.16.refs_8_), channel_id=1, source_target_pairs={{0,4},{1,5},{2,6},{3,7},{4,0},{5,1},{6,2},{7,3},{8,12},{9,13},{10,... | collective-permute-start | bytes 2101256 | tf_op jit(solution)/shard_map/ppermute | solution.py:29
  637.8 22.5 %copy-start.59 = (bf16[684,512]{1,0:T(8,128)(2,1)S(1)}, bf16[684,512]{1,0:T(8,128)(2,1)}, u32[]{:S(2)}) copy-start(bf16[684,512]{1,0:T(8,128)(2,1)} %copy-done.58) | copy-start | bytes 2101252
  637.8 22.6 %copy-start.105 = (bf16[684,512]{1,0:T(8,128)(2,1)S(1)}, bf16[684,512]{1,0:T(8,128)(2,1)}, u32[]{:S(2)}) copy-start(bf16[684,512]{1,0:T(8,128)(2,1)} %fusion.64) | copy-start | bytes 2101252
  637.8 23.6 %copy-start.115 = (f32[3,2048]{1,0:T(4,128)S(1)}, f32[3,2048]{1,0:T(4,128)}, u32[]{:S(2)}) copy-start(f32[3,2048]{1,0:T(4,128)} %reduce_sum.112) | copy-start | bytes 73732
  637.8 28.5 %copy-start.65 = (bf16[684,512]{1,0:T(8,128)(2,1)S(1)}, bf16[684,512]{1,0:T(8,128)(2,1)}, u32[]{:S(2)}) copy-start(bf16[684,512]{1,0:T(8,128)(2,1)} %copy-done.64) | copy-start | bytes 2101252
  637.8 28.5 %copy-start.108 = (bf16[684,512]{1,0:T(8,128)(2,1)S(1)}, bf16[684,512]{1,0:T(8,128)(2,1)}, u32[]{:S(2)}) copy-start(bf16[684,512]{1,0:T(8,128)(2,1)} %fusion.65) | copy-start | bytes 2101252
  660.3 27.6 %copy-start.31 = (bf16[3,1024,256]{2,1,0:T(8,128)(2,1)}, bf16[3,1024,256]{2,1,0:T(8,128)(2,1)S(1)}, u32[]{:S(2)}) copy-start(bf16[3,1024,256]{2,1,0:T(8,128)(2,1)S(1)} %get-tuple-element.176) | copy-start | bytes 4718596
  660.3 34.1 %copy-start.33 = (bf16[3,1024,256]{2,1,0:T(8,128)(2,1)}, bf16[3,1024,256]{2,1,0:T(8,128)(2,1)S(1)}, u32[]{:S(2)}) copy-start(bf16[3,1024,256]{2,1,0:T(8,128)(2,1)S(1)} %get-tuple-element.177) | copy-start | bytes 4718596
  691.3 14.8 %collective-permute-start.20 = (bf16[512,512]{1,0:T(8,128)(2,1)}, bf16[512,512]{1,0:T(8,128)(2,1)S(1)}, u32[]{:S(2)}, u32[]{:S(2)}) collective-permute-start(bf16[512,512]{1,0:T(8,128)(2,1)} %add_convert_fusion.20), channel_id=1, source_target_pairs={{0,16},{8,24},{16,0},{24,8},{1,17},{9,25},{17,1},{25,9},{2,18},{10... | collective-permute-start | bytes 1572872 | tf_op jit(solution)/shard_map/ppermute | solution.py:29
  693.9 12.5 %collective-permute-start.22 = (bf16[3,1024,256]{2,1,0:T(8,128)(2,1)}, bf16[3,1024,256]{2,1,0:T(8,128)(2,1)}, u32[]{:S(2)}, u32[]{:S(2)}) collective-permute-start(bf16[3,1024,256]{2,1,0:T(8,128)(2,1)} %fusion.55), channel_id=1, source_target_pairs={{0,8},{8,0},{16,24},{24,16},{1,9},{9,1},{17,25},{25,17},{2,10},{10... | collective-permute-start | bytes 4718600 | tf_op jit(solution)/shard_map/ppermute | solution.py:29
  693.9 14.9 %collective-permute-start.21 = (bf16[3,1024,256]{2,1,0:T(8,128)(2,1)}, bf16[3,1024,256]{2,1,0:T(8,128)(2,1)}, u32[]{:S(2)}, u32[]{:S(2)}) collective-permute-start(bf16[3,1024,256]{2,1,0:T(8,128)(2,1)} %fusion.54), channel_id=1, source_target_pairs={{0,8},{8,0},{16,24},{24,16},{1,9},{9,1},{17,25},{25,17},{2,10},{10... | collective-permute-start | bytes 4718600 | tf_op jit(solution)/shard_map/ppermute | solution.py:29
  (115 other events, 518.0 us)
